TPU v7x, 128 devices: a whole 4x4x4 slice. The times are simulated.
128 devices in a mesh: pool: 8 (over z, y_hi), tp: 16 (over x, y_lo, core).
Axes of the slice: x: 4, y: 4 (y_hi: 2, y_lo: 2; y = y_hi * 2 + y_lo), z: 4, core: 2. Of those that a mesh axis runs over, the one named last changes fastest.
Arguments:
- pre_q: bfloat16 [20480, 8192], P(('pool', 'tp')), may hold values from -250 to 250
- pre_kv: bfloat16 [2, 20480, 1024], P(None, ('pool', 'tp')), may hold values from -6 to 6
- arrival_q: bfloat16 [8, 8192], replicated, may hold values from -250 to 250
- owner: int32 [8], replicated, may hold values from 0 to 7, as said below
- cache_kv: bfloat16 [2, 32, 8192, 1024], P(None, 'pool', 'tp'), may hold values from -6 to 6
- lengths: int32 [32], P('pool'), may hold values from 2 to 8192, as said below
- dec_q: bfloat16 [4, 32, 8192], P(None, 'pool'), may hold values from -250 to 250
- new_kv: bfloat16 [2, 4, 32, 1024], P(None, None, 'pool'), may hold values from -6 to 6
Outputs:
- prefill_out: bfloat16 [20480, 8192], P(('pool', 'tp'))
- received: bfloat16 [2, 16, 2560, 1024], P(None, 'pool', 'tp')
- decode_out: bfloat16 [4, 32, 8192], P(None, 'pool', 'tp')
- arrival_out: bfloat16 [16, 8192], P('pool', 'tp')
Inputs may be any that keep to these rules, and one draw needn't show every extreme that they name: `owner`: at most two prompts share one decode group, and some decode group takes exactly two. `lengths`: some request has exactly 8192 resident positions.
All inputs are finite; a program needn't handle non-finite values.
Results may differ from a plain program's by a relative error of at most 0.018.
Values may be sent and summed in bfloat16 or wider, within the bound.
No kernel may reach another device: no remote copies, remote signals or barrier semaphores. Data moves between devices by JAX's collectives and lax.ppermute only.
A program may use at most 192 MiB of HBM per device.

v0:
```python
import math

import jax
import jax.numpy as jnp
from jax import lax
from jax.sharding import PartitionSpec as P

H = 64
KVH = 8
HD = 128
STEPS = 4
MOST = 2


NEGATIVE = -1e30


def combined_all(part, axis, combine):
    gathered = jax.tree.map(lambda a: lax.all_gather(a, axis), part)

    def take(source):
        return jax.tree.map(lambda a: lax.dynamic_index_in_dim(a, source, 0, False), gathered)

    return lax.fori_loop(
        1, lax.axis_size(axis), lambda source, state: combine(state, take(source)), take(0)
    )


def block_update(softmax_state, queries, key_rows, value_rows, visible):
    peaks, totals, summed = softmax_state
    score_scale = 1.0 / math.sqrt(HD)
    scores = (
        jnp.einsum("qgre,kge->grqk", queries, key_rows, preferred_element_type=jnp.float32)
        * score_scale
    )
    shown = visible[None, None]
    raised = jnp.maximum(peaks, jnp.max(jnp.where(shown, scores, NEGATIVE), axis=-1))
    weights = jnp.where(shown, jnp.exp(scores - raised[..., None]), 0.0)
    shrink = jnp.exp(peaks - raised)
    totals = totals * shrink + jnp.sum(weights, axis=-1)
    summed = summed * shrink[..., None] + jnp.einsum(
        "grqk,kge->grqe",
        weights.astype(jnp.bfloat16),
        value_rows,
        preferred_element_type=jnp.float32,
    )
    return (raised, totals, summed)


def decode_partial(dec_rows, cache_rows, tail_rows, cache_live, tail_live):
    score_scale = 1.0 / math.sqrt(HD)
    cache_scores = (
        jnp.einsum("srgae,rpge->rgasp", dec_rows, cache_rows[0], preferred_element_type=jnp.float32)
        * score_scale
    )
    tail_scores = (
        jnp.einsum("srgae,trge->rgast", dec_rows, tail_rows[0], preferred_element_type=jnp.float32)
        * score_scale
    )
    cache_mask = cache_live[:, None, None, None, :]
    tail_mask = tail_live[None, None, None]
    peaks = jnp.maximum(
        jnp.max(jnp.where(cache_mask, cache_scores, NEGATIVE), axis=-1),
        jnp.max(jnp.where(tail_mask, tail_scores, NEGATIVE), axis=-1),
    )
    cache_weights = jnp.where(cache_mask, jnp.exp(cache_scores - peaks[..., None]), 0.0)
    tail_weights = jnp.where(tail_mask, jnp.exp(tail_scores - peaks[..., None]), 0.0)
    totals = jnp.sum(cache_weights, axis=-1) + jnp.sum(tail_weights, axis=-1)
    summed = jnp.einsum(
        "rgasp,rpge->rgase",
        cache_weights.astype(jnp.bfloat16),
        cache_rows[1],
        preferred_element_type=jnp.float32,
    )
    summed = summed + jnp.einsum(
        "rgast,trge->rgase",
        tail_weights.astype(jnp.bfloat16),
        tail_rows[1],
        preferred_element_type=jnp.float32,
    )
    return (peaks, totals, summed)


def arrival_partial(arrival_rows, slot_pairs):
    score_scale = 1.0 / math.sqrt(HD)
    scores = (
        jnp.einsum(
            "mgae,mcge->mgac", arrival_rows, slot_pairs[0], preferred_element_type=jnp.float32
        )
        * score_scale
    )
    peaks = jnp.max(scores, axis=-1)
    weights = jnp.exp(scores - peaks[..., None])
    totals = jnp.sum(weights, axis=-1)
    summed = jnp.einsum(
        "mgac,mcge->mgae",
        weights.astype(jnp.bfloat16),
        slot_pairs[1],
        preferred_element_type=jnp.float32,
    )
    return (peaks, totals, summed)


def combine_partials(first, second):
    peaks_one, totals_one, summed_one = first
    peaks_two, totals_two, summed_two = second
    peaks = jnp.maximum(peaks_one, peaks_two)
    weight_one = jnp.exp(peaks_one - peaks)
    weight_two = jnp.exp(peaks_two - peaks)
    row_count, head_count = peaks.shape
    merged = (
        summed_one.reshape(row_count, head_count, -1) * weight_one[..., None]
        + summed_two.reshape(row_count, head_count, -1) * weight_two[..., None]
    )
    return (peaks, totals_one * weight_one + totals_two * weight_two, merged.reshape(row_count, -1))


def body(pre_q, pre_kv, arrival_q, owner, cache_kv, lengths, dec_q, new_kv):
    tokens = pre_q.shape[0]
    repeat = H // KVH
    cycle_index = lax.axis_index("tp")
    queries = pre_q.reshape(tokens, KVH, repeat, HD)
    own_places = cycle_index * tokens + jnp.arange(tokens)
    start_state = (
        jnp.full((KVH, repeat, tokens), NEGATIVE, jnp.float32),
        jnp.zeros((KVH, repeat, tokens), jnp.float32),
        jnp.zeros((KVH, repeat, tokens, HD), jnp.float32),
    )
    shard_piece = lax.all_gather(pre_kv, "tp", axis=1, tiled=True)
    piece_len = shard_piece.shape[1]
    block_len = math.gcd(piece_len, 512)
    block_count = piece_len // block_len
    blocked = jnp.moveaxis(shard_piece.reshape(2, block_count, block_len, KVH, HD), 1, 0)

    def advance(carry, operands):
        pair_block, block_id = operands
        key_places = block_id * block_len + jnp.arange(block_len)
        visible = jnp.logical_and(
            key_places[None, :] <= own_places[:, None], key_places[None, :] >= 0
        )
        return (block_update(carry, queries, pair_block[0], pair_block[1], visible), None)

    result, unused = lax.scan(advance, start_state, (blocked, jnp.arange(block_count)))
    peaks, totals, summed = result
    attention = summed / totals[..., None]
    prefill_out = (
        jnp.transpose(attention, (2, 0, 1, 3)).reshape(tokens, H * HD).astype(jnp.bfloat16)
    )
    pool_count = owner.shape[0]
    pool_index = lax.axis_index("pool")
    prompts = jnp.arange(pool_count)
    shared_owner = owner[:, None] == owner[None, :]
    earlier = prompts[None, :] < prompts[:, None]
    owner_rank = jnp.sum(jnp.logical_and(shared_owner, earlier).astype(jnp.int32), axis=1)
    slot_pick = jnp.logical_and(
        owner[None, :] == pool_index, owner_rank[None, :] == jnp.arange(MOST)[:, None]
    ).astype(jnp.bfloat16)
    gathered = lax.all_gather(pre_kv[None], "pool", axis=0, tiled=True)
    received = jnp.einsum(
        "mp,pctw->cmtw", slot_pick, gathered, preferred_element_type=jnp.float32
    ).astype(jnp.bfloat16)
    arrival_rows = jnp.einsum(
        "mp,pd->md", slot_pick, arrival_q, preferred_element_type=jnp.float32
    ).astype(jnp.bfloat16)
    requests = lengths.shape[0]
    positions = cache_kv.shape[2]
    dec_rows = dec_q.reshape(STEPS, requests, KVH, repeat, HD)
    cache_rows = cache_kv.reshape(2, requests, positions, KVH, HD)
    tail_rows = new_kv.reshape(2, STEPS, requests, KVH, HD)
    cache_places = cycle_index * positions + jnp.arange(positions)
    cache_live = cache_places[None, :] < lengths[:, None]
    step_ids = jnp.arange(STEPS)
    tail_live = jnp.logical_and(step_ids[None, :] <= step_ids[:, None], cycle_index == 0)
    dec_peaks, dec_totals, dec_summed = decode_partial(
        dec_rows, cache_rows, tail_rows, cache_live, tail_live
    )
    dec_count = STEPS * requests
    dec_peaks = jnp.transpose(dec_peaks, (3, 0, 1, 2)).reshape(dec_count, H)
    dec_totals = jnp.transpose(dec_totals, (3, 0, 1, 2)).reshape(dec_count, H)
    dec_summed = jnp.transpose(dec_summed, (3, 0, 1, 2, 4)).reshape(dec_count, H * HD)
    slot_pairs = received.reshape(2, MOST, tokens, KVH, HD)
    arr_peaks, arr_totals, arr_summed = arrival_partial(
        arrival_rows.reshape(MOST, KVH, repeat, HD), slot_pairs
    )
    all_peaks = jnp.concatenate([dec_peaks, arr_peaks.reshape(MOST, H)], axis=0)
    all_totals = jnp.concatenate([dec_totals, arr_totals.reshape(MOST, H)], axis=0)
    all_summed = jnp.concatenate([dec_summed, arr_summed.reshape(MOST, H * HD)], axis=0)
    row_count = dec_count + MOST
    own_heads = H // lax.axis_size("tp")
    merged_peaks, merged_totals, merged_summed = combined_all(
        (all_peaks, all_totals, all_summed), "tp", combine_partials
    )
    finished = (merged_summed.reshape(row_count, H, HD) / merged_totals[..., None]).reshape(
        row_count, H * HD
    )
    finished = lax.dynamic_slice_in_dim(finished, cycle_index * own_heads * HD, own_heads * HD, 1)
    decode_out = finished[:dec_count].reshape(STEPS, requests, own_heads * HD).astype(jnp.bfloat16)
    arrival_out = finished[dec_count:].astype(jnp.bfloat16)
    return (prefill_out, received, decode_out, arrival_out)


def solution(mesh):
    in_specs = (
        P(("pool", "tp"), None),
        P(None, ("pool", "tp"), None),
        P(),
        P(),
        P(None, "pool", "tp", None),
        P("pool"),
        P(None, "pool", None),
        P(None, None, "pool", None),
    )
    out_specs = (
        P(("pool", "tp"), None),
        P(None, "pool", "tp", None),
        P(None, "pool", "tp"),
        P("pool", "tp"),
    )
    return jax.shard_map(body, mesh=mesh, in_specs=in_specs, out_specs=out_specs, check_vma=False)
```

profile of v0, /device:TPU:1, one launch (start us, length us, event | category | flops | bytes accessed | tf_op | source)
XLA Modules:
  0.0 426.5 jit_solution(14411033822516706589)
XLA Ops:
  8.7 2.5 copy.112
  11.2 1.7 copy.72
  12.9 6.1 %fusion.77 = (bf16[1,4,512,1024]{3,2,1,0:T(8,128)(2,1)}, bf16[1,4,512,1024]{3,2,1,0:T(8,128)(2,1)}) fusion(bf16[2,4,512,1024]{3,2,1,0:T(8,128)(2,1)} %param.16), kind=kLoop, calls=%fused_computation.112 | loop fusion | bytes 16777216 | tf_op jit(solution)/shard_map/slice | solution.py:72
  19.0 6.4 %copy.105 = bf16[1,4,512,1024]{2,3,1,0:T(8,128)(2,1)} copy(bf16[1,4,512,1024]{3,2,1,0:T(8,128)(2,1)} %get-tuple-element.351) | data formatting | bytes 8388608
  27.2 4.3 %fusion.26 = (f32[4,8,8,4]{2,3,1,0:T(4,128)S(1)}, f32[4,8,512,4,8]{2,4,3,1,0:T(8,128)}) fusion(pred[4,512]{1,0:T(4,128)(4,1)S(1)} %broadcast_compare_fusion.1, bf16[4,512,8,128,1]{1,3,4,2,0:T(8,128)(2,1)} %bitcast.190, bf16[4,4,8,8,128]{4,3,2,1,0:T(8,128)(2,1)S(1)} %reshape.204), kind=kOutput, calls=%fused_computation.46 | convolution fusion | flops 135789568 | bytes 6559744 | tf_op jit(solution)/shard_map/srgae,rpge->rgasp/dot_general | solution.py:53
  31.9 2.2 fusion.30
  34.2 6.3 %copy.106 = bf16[1,4,512,1024]{2,3,1,0:T(8,128)(2,1)} copy(bf16[1,4,512,1024]{3,2,1,0:T(8,128)(2,1)} %get-tuple-element.350) | data formatting | bytes 8388608
  40.5 4.3 %fusion.40 = f32[4,8,8,4,128]{4,2,3,1,0:T(8,128)S(1)} fusion(bf16[4,512,8,128,1]{1,3,4,2,0:T(8,128)(2,1)} %bitcast.185, f32[4,8,512,4,8]{2,4,3,1,0:T(8,128)} %get-tuple-element.359, f32[4,8,8,4]{2,3,1,0:T(4,128)S(1)} %max.24, pred[4,512]{1,0:T(4,128)(4,1)S(1)} %broadcast_compare_fusion.1), kind=kOutput, calls=%fused_computation.60 | convolution fusion | flops 136314880 | bytes 6821888 | tf_op jit(solution)/shard_map/rgasp,rpge->rgase/dot_general | solution.py:69
  46.5 47.0 %all-gather.13.cloned.1.call-done = bf16[16,160,1024]{2,1,0:T(8,128)(2,1)} async-done(((bf16[2,160,1024]{2,1,0:T(8,128)(2,1)}), bf16[16,160,1024]{2,1,0:T(8,128)(2,1)}) %all-gather.13.cloned.1.call-update) | async-done | bytes 5242896 | tf_op jit(solution)/shard_map/all_gather | solution.py:158
  93.5 5.9 %fusion.34 = bf16[2,2,160,1024]{3,1,2,0:T(2,128)(2,1)S(1)} fusion(bf16[8,2,160,1024]{3,2,1,0:T(8,128)(2,1)} %bitcast.189, pred[8]{0:T(512)(128)(4,1)S(1)} %broadcast_compare_fusion.2, s32[8]{0:T(128)S(1)} %convert_reduce_fusion), kind=kOutput, calls=%fused_computation.52 | convolution fusion | flops 11141152 | bytes 6553640 | tf_op jit(solution)/shard_map/mp,pctw->cmtw/dot_general | solution.py:159
  100.9 1.7 fusion.78
  102.6 2.9 squeeze.64
  105.5 1.6 fusion.80
  110.3 20.6 %all-gather.4 = f32[16,18,64]{2,1,0:T(8,128)S(1)} all-gather(f32[1,18,64]{2,1,0:T(8,128)S(1)} %maximum_bitcast_fusion.1), channel_id=3, replica_groups=mesh['pool'=8,'tp'=16] {'tp'}, dimensions={0}, use_global_device_ids=true | all-gather | bytes 78336 | tf_op jit(solution)/shard_map/all_gather | solution.py:19
  130.8 17.1 %all-gather.5 = f32[16,18,64]{2,1,0:T(8,128)S(1)} all-gather(f32[1,18,64]{2,1,0:T(8,128)S(1)} %maximum_bitcast_fusion.2), channel_id=4, replica_groups=mesh['pool'=8,'tp'=16] {'tp'}, dimensions={0}, use_global_device_ids=true | all-gather | bytes 78336 | tf_op jit(solution)/shard_map/all_gather | solution.py:19
  149.2 2.0 maximum_bitcast_fusion
  151.3 8.1 %all-gather.11.cloned.1.call-done = bf16[2,2560,1024]{2,1,0:T(8,128)(2,1)} async-done(((bf16[2,160,1024]{2,1,0:T(8,128)(2,1)}), bf16[2,2560,1024]{2,1,0:T(8,128)(2,1)}) %all-gather.11.cloned.1.call-update) | async-done | bytes 10485776 | tf_op jit(solution)/shard_map/all_gather | solution.py:129
  159.4 10.7 %copy.111 = bf16[640,8,8,128]{3,2,1,0:T(8,128)(2,1)} copy(bf16[640,8,8,128]{3,1,2,0:T(8,128)(2,1)} %bitcast.186) | data formatting | bytes 20971520
  170.1 180.6 %while.35 = (s32[]{:T(128)}, f32[8,8,160]{2,1,0:T(8,128)S(1)}, f32[8,8,160]{2,1,0:T(8,128)S(1)}, f32[8,8,160,128]{3,2,1,0:T(8,128)}, s32[5]{0:T(128)S(1)}, /*ind...) while((s32[]{:T(128)}, f32[8,8,160]{2,1,0:T(8,128)S(1)}, ...), condition=%wide.region_3.4_spmd.clone, body=%wide.region_0.3_spmd.clone.sunk | while | flops 2746174976 | bytes 167188960 | solution.py:143
  171.5 2.7 constant_dynamic-slice_fusion.3
  174.2 9.8 %fusion.97 = (f32[8,8,160]{2,1,0:T(8,128)S(1)}, f32[8,512,160,8]{1,2,3,0:T(8,128)}) fusion(pred[160,512]{1,0:T(8,128)(4,1)S(1)} %compare_and_fusion.5, bf16[160,8,8,128]{3,0,2,1:T(8,128)(2,1)S(1)} %get-tuple-element.504, bf16[1,1,512,8,128]{4,3,2,0,1:T(8,128)(2,1)S(1)} %get-tuple-element.468), kind=kOutput, calls=%fused_computation.11.clone.1 | convolution fusion | flops 1357895680 | bytes 24764416 | tf_op jit(solution)/shard_map/while/body/eval_jaxpr/qgre,kge->grqk/dot_general | solution.py:33
  184.0 12.0 %fusion.98 = f32[8,8,160]{2,1,0:T(8,128)S(1)} fusion(f32[8,512,160,8]{1,2,3,0:T(8,128)} %get-tuple-element.470, f32[8,8,160]{2,1,0:T(8,128)S(1)} %select_maximum_fusion.2, pred[160,512]{1,0:T(8,128)(4,1)S(1)} %compare_and_fusion.5), kind=kLoop, calls=%fused_computation.15.clone.1 | loop fusion | flops 20961280 | bytes 21135360 | tf_op jit(solution)/shard_map/while/body/eval_jaxpr/reduce_sum | solution.py:40
  196.1 1.8 copy-done.2
  197.9 8.5 %fusion.100 = f32[8,8,160,128]{3,2,1,0:T(8,128)} fusion(f32[8,8,160,128]{3,2,1,0:T(8,128)} %get-tuple-element.489, f32[8,8,160]{2,1,0:T(8,128)S(1)} %get-tuple-element.472, pred[]{:T(512)S(6)} %compare.3, f32[8,512,160,8]{1,2,3,0:T(8,128)S(1)} %copy-done.2, f32[8,8,160]{2,1,0:T(8,128)S(1)} %select_maximum_fusion.2, ...), kind=kOutput, calls=%fused_computation.22.clone.1 | convolution fusion | flops 1367080960 | bytes 32669696 | tf_op jit(solution)/shard_map/while/body/eval_jaxpr/grqk,kge->grqe/dot_general | solution.py:41
  207.7 2.7 constant_dynamic-slice_fusion.3
  210.4 9.9 %fusion.97 = (f32[8,8,160]{2,1,0:T(8,128)S(1)}, f32[8,512,160,8]{1,2,3,0:T(8,128)}) fusion(pred[160,512]{1,0:T(8,128)(4,1)S(1)} %compare_and_fusion.5, bf16[160,8,8,128]{3,0,2,1:T(8,128)(2,1)S(1)} %get-tuple-element.504, bf16[1,1,512,8,128]{4,3,2,0,1:T(8,128)(2,1)S(1)} %get-tuple-element.468), kind=kOutput, calls=%fused_computation.11.clone.1 | convolution fusion | flops 1357895680 | bytes 24764416 | tf_op jit(solution)/shard_map/while/body/eval_jaxpr/qgre,kge->grqk/dot_general | solution.py:33
  220.3 11.8 %fusion.98 = f32[8,8,160]{2,1,0:T(8,128)S(1)} fusion(f32[8,512,160,8]{1,2,3,0:T(8,128)} %get-tuple-element.470, f32[8,8,160]{2,1,0:T(8,128)S(1)} %select_maximum_fusion.2, pred[160,512]{1,0:T(8,128)(4,1)S(1)} %compare_and_fusion.5), kind=kLoop, calls=%fused_computation.15.clone.1 | loop fusion | flops 20961280 | bytes 21135360 | tf_op jit(solution)/shard_map/while/body/eval_jaxpr/reduce_sum | solution.py:40
  232.2 1.7 copy-done.2
  233.9 9.1 %fusion.100 = f32[8,8,160,128]{3,2,1,0:T(8,128)} fusion(f32[8,8,160,128]{3,2,1,0:T(8,128)} %get-tuple-element.489, f32[8,8,160]{2,1,0:T(8,128)S(1)} %get-tuple-element.472, pred[]{:T(512)S(6)} %compare.3, f32[8,512,160,8]{1,2,3,0:T(8,128)S(1)} %copy-done.2, f32[8,8,160]{2,1,0:T(8,128)S(1)} %select_maximum_fusion.2, ...), kind=kOutput, calls=%fused_computation.22.clone.1 | convolution fusion | flops 1367080960 | bytes 32669696 | tf_op jit(solution)/shard_map/while/body/eval_jaxpr/grqk,kge->grqe/dot_general | solution.py:41
  244.4 2.7 constant_dynamic-slice_fusion.3
  247.1 9.7 %fusion.97 = (f32[8,8,160]{2,1,0:T(8,128)S(1)}, f32[8,512,160,8]{1,2,3,0:T(8,128)}) fusion(pred[160,512]{1,0:T(8,128)(4,1)S(1)} %compare_and_fusion.5, bf16[160,8,8,128]{3,0,2,1:T(8,128)(2,1)S(1)} %get-tuple-element.504, bf16[1,1,512,8,128]{4,3,2,0,1:T(8,128)(2,1)S(1)} %get-tuple-element.468), kind=kOutput, calls=%fused_computation.11.clone.1 | convolution fusion | flops 1357895680 | bytes 24764416 | tf_op jit(solution)/shard_map/while/body/eval_jaxpr/qgre,kge->grqk/dot_general | solution.py:33
  256.8 11.7 %fusion.98 = f32[8,8,160]{2,1,0:T(8,128)S(1)} fusion(f32[8,512,160,8]{1,2,3,0:T(8,128)} %get-tuple-element.470, f32[8,8,160]{2,1,0:T(8,128)S(1)} %select_maximum_fusion.2, pred[160,512]{1,0:T(8,128)(4,1)S(1)} %compare_and_fusion.5), kind=kLoop, calls=%fused_computation.15.clone.1 | loop fusion | flops 20961280 | bytes 21135360 | tf_op jit(solution)/shard_map/while/body/eval_jaxpr/reduce_sum | solution.py:40
  269.8 9.1 %fusion.100 = f32[8,8,160,128]{3,2,1,0:T(8,128)} fusion(f32[8,8,160,128]{3,2,1,0:T(8,128)} %get-tuple-element.489, f32[8,8,160]{2,1,0:T(8,128)S(1)} %get-tuple-element.472, pred[]{:T(512)S(6)} %compare.3, f32[8,512,160,8]{1,2,3,0:T(8,128)S(1)} %copy-done.2, f32[8,8,160]{2,1,0:T(8,128)S(1)} %select_maximum_fusion.2, ...), kind=kOutput, calls=%fused_computation.22.clone.1 | convolution fusion | flops 1367080960 | bytes 32669696 | tf_op jit(solution)/shard_map/while/body/eval_jaxpr/grqk,kge->grqe/dot_general | solution.py:41
  280.3 2.7 constant_dynamic-slice_fusion.3
  283.0 9.7 %fusion.97 = (f32[8,8,160]{2,1,0:T(8,128)S(1)}, f32[8,512,160,8]{1,2,3,0:T(8,128)}) fusion(pred[160,512]{1,0:T(8,128)(4,1)S(1)} %compare_and_fusion.5, bf16[160,8,8,128]{3,0,2,1:T(8,128)(2,1)S(1)} %get-tuple-element.504, bf16[1,1,512,8,128]{4,3,2,0,1:T(8,128)(2,1)S(1)} %get-tuple-element.468), kind=kOutput, calls=%fused_computation.11.clone.1 | convolution fusion | flops 1357895680 | bytes 24764416 | tf_op jit(solution)/shard_map/while/body/eval_jaxpr/qgre,kge->grqk/dot_general | solution.py:33
  292.7 11.7 %fusion.98 = f32[8,8,160]{2,1,0:T(8,128)S(1)} fusion(f32[8,512,160,8]{1,2,3,0:T(8,128)} %get-tuple-element.470, f32[8,8,160]{2,1,0:T(8,128)S(1)} %select_maximum_fusion.2, pred[160,512]{1,0:T(8,128)(4,1)S(1)} %compare_and_fusion.5), kind=kLoop, calls=%fused_computation.15.clone.1 | loop fusion | flops 20961280 | bytes 21135360 | tf_op jit(solution)/shard_map/while/body/eval_jaxpr/reduce_sum | solution.py:40
  305.7 9.1 %fusion.100 = f32[8,8,160,128]{3,2,1,0:T(8,128)} fusion(f32[8,8,160,128]{3,2,1,0:T(8,128)} %get-tuple-element.489, f32[8,8,160]{2,1,0:T(8,128)S(1)} %get-tuple-element.472, pred[]{:T(512)S(6)} %compare.3, f32[8,512,160,8]{1,2,3,0:T(8,128)S(1)} %copy-done.2, f32[8,8,160]{2,1,0:T(8,128)S(1)} %select_maximum_fusion.2, ...), kind=kOutput, calls=%fused_computation.22.clone.1 | convolution fusion | flops 1367080960 | bytes 32669696 | tf_op jit(solution)/shard_map/while/body/eval_jaxpr/grqk,kge->grqe/dot_general | solution.py:41
  316.2 2.7 constant_dynamic-slice_fusion.3
  318.9 9.7 %fusion.97 = (f32[8,8,160]{2,1,0:T(8,128)S(1)}, f32[8,512,160,8]{1,2,3,0:T(8,128)}) fusion(pred[160,512]{1,0:T(8,128)(4,1)S(1)} %compare_and_fusion.5, bf16[160,8,8,128]{3,0,2,1:T(8,128)(2,1)S(1)} %get-tuple-element.504, bf16[1,1,512,8,128]{4,3,2,0,1:T(8,128)(2,1)S(1)} %get-tuple-element.468), kind=kOutput, calls=%fused_computation.11.clone.1 | convolution fusion | flops 1357895680 | bytes 24764416 | tf_op jit(solution)/shard_map/while/body/eval_jaxpr/qgre,kge->grqk/dot_general | solution.py:33
  328.6 11.7 %fusion.98 = f32[8,8,160]{2,1,0:T(8,128)S(1)} fusion(f32[8,512,160,8]{1,2,3,0:T(8,128)} %get-tuple-element.470, f32[8,8,160]{2,1,0:T(8,128)S(1)} %select_maximum_fusion.2, pred[160,512]{1,0:T(8,128)(4,1)S(1)} %compare_and_fusion.5), kind=kLoop, calls=%fused_computation.15.clone.1 | loop fusion | flops 20961280 | bytes 21135360 | tf_op jit(solution)/shard_map/while/body/eval_jaxpr/reduce_sum | solution.py:40
  341.6 9.1 %fusion.100 = f32[8,8,160,128]{3,2,1,0:T(8,128)} fusion(f32[8,8,160,128]{3,2,1,0:T(8,128)} %get-tuple-element.489, f32[8,8,160]{2,1,0:T(8,128)S(1)} %get-tuple-element.472, pred[]{:T(512)S(6)} %compare.3, f32[8,512,160,8]{1,2,3,0:T(8,128)S(1)} %copy-done.2, f32[8,8,160]{2,1,0:T(8,128)S(1)} %select_maximum_fusion.2, ...), kind=kOutput, calls=%fused_computation.22.clone.1 | convolution fusion | flops 1367080960 | bytes 32669696 | tf_op jit(solution)/shard_map/while/body/eval_jaxpr/grqk,kge->grqe/dot_general | solution.py:41
  350.7 4.0 fusion.25
  355.8 3.8 copy.157
  360.9 57.1 %while.34 = (s32[]{:T(128)}, f32[18,64]{1,0:T(8,128)S(1)}, f32[18,64]{1,0:T(8,128)S(1)}, f32[18,8192]{1,0:T(8,128)S(1)}, f32[16,18,64]{2,1,0:T(8,128)}, /*index=...) while((s32[]{:T(128)}, f32[18,64]{1,0:T(8,128)S(1)}, ...), condition=%wide.region_12.13_spmd, body=%wide.region_11.12_spmd.sunk | while | flops 449285 | bytes 10073255 | solution.py:24
  363.4 1.5 fusion.94
  367.2 1.5 fusion.94
  371.0 1.5 fusion.94
  374.8 1.5 fusion.94
  (238 shorter events, 73.0 us)
Async XLA Ops:
  7.2 39.1 %copy-start = (bf16[8,8192]{1,0:T(8,128)(2,1)S(1)}, bf16[8,8192]{1,0:T(8,128)(2,1)}, u32[]{:S(2)}) copy-start(bf16[8,8192]{1,0:T(8,128)(2,1)} %param.14) | copy-start | bytes 393220
  7.2 86.3 %all-gather.13.cloned.1.call-start = ((), (), s32[]{:S(2)}) async-start(), calls=%async_computation.1 | async-start | bytes 5898240 | tf_op jit(solution)/shard_map/all_gather | solution.py:158
  7.9 151.5 %all-gather.11.cloned.1.call-start = ((), (), s32[]{:S(2)}) async-start(), calls=%async_computation | async-start | bytes 11141120 | tf_op jit(solution)/shard_map/all_gather | solution.py:129
  8.7 351.0 %all-gather.15.cloned.1.call-start = ((), (), s32[]{:S(2)}) async-start(), calls=%async_computation.2 | async-start | bytes 13369344 | tf_op jit(solution)/shard_map/all_gather | solution.py:19
  19.0 6.4 %copy-start.8 = (bf16[4,4,8192]{2,1,0:T(4,128)(2,1)S(1)}, bf16[4,4,8192]{2,1,0:T(4,128)(2,1)}, u32[]{:S(2)}) copy-start(bf16[4,4,8192]{2,1,0:T(4,128)(2,1)} %param.18) | copy-start | bytes 786436
  19.0 6.7 %copy-start.9 = (bf16[2,4,4,1024]{3,2,1,0:T(4,128)(2,1)S(1)}, bf16[2,4,4,1024]{3,2,1,0:T(4,128)(2,1)}, u32[]{:S(2)}) copy-start(bf16[2,4,4,1024]{3,2,1,0:T(4,128)(2,1)} %param.19) | copy-start | bytes 196612
  19.0 6.8 %copy-start.10 = (s32[4]{0:T(128)S(1)}, s32[4]{0:T(128)}, u32[]{:S(2)}) copy-start(s32[4]{0:T(128)} %param.17) | copy-start | bytes 52
  40.5 5.6 %copy-start.11 = (s32[8]{0:T(128)S(1)}, s32[8]{0:T(128)}, u32[]{:S(2)}) copy-start(s32[8]{0:T(128)} %param.15) | copy-start | bytes 100
  130.8 17.1 %copy-start.6 = (f32[16,18,64]{2,1,0:T(8,128)}, f32[16,18,64]{2,1,0:T(8,128)S(1)}, u32[]{:S(2)}) copy-start(f32[16,18,64]{2,1,0:T(8,128)S(1)} %all-gather.4) | copy-start | bytes 221188
  148.0 0.7 copy-start.7
  159.4 10.7 %copy-start.3 = (f32[8,8,160]{2,1,0:T(8,128)S(1)}, f32[8,8,160]{2,1,0:T(8,128)}, u32[]{:S(2)}) copy-start(f32[8,8,160]{2,1,0:T(8,128)} %custom-call.1) | copy-start | bytes 122884
  184.0 13.9 %copy-start.2 = (f32[8,512,160,8]{1,2,3,0:T(8,128)S(1)}, f32[8,512,160,8]{1,2,3,0:T(8,128)}, u32[]{:S(2)}) copy-start(f32[8,512,160,8]{1,2,3,0:T(8,128)} %get-tuple-element.470) | copy-start | bytes 62914564 | tf_op jit(solution)/shard_map/while
  220.3 13.6 %copy-start.2 = (f32[8,512,160,8]{1,2,3,0:T(8,128)S(1)}, f32[8,512,160,8]{1,2,3,0:T(8,128)}, u32[]{:S(2)}) copy-start(f32[8,512,160,8]{1,2,3,0:T(8,128)} %get-tuple-element.470) | copy-start | bytes 62914564 | tf_op jit(solution)/shard_map/while
  256.8 13.1 %copy-start.2 = (f32[8,512,160,8]{1,2,3,0:T(8,128)S(1)}, f32[8,512,160,8]{1,2,3,0:T(8,128)}, u32[]{:S(2)}) copy-start(f32[8,512,160,8]{1,2,3,0:T(8,128)} %get-tuple-element.470) | copy-start | bytes 62914564 | tf_op jit(solution)/shard_map/while
  292.6 13.1 %copy-start.2 = (f32[8,512,160,8]{1,2,3,0:T(8,128)S(1)}, f32[8,512,160,8]{1,2,3,0:T(8,128)}, u32[]{:S(2)}) copy-start(f32[8,512,160,8]{1,2,3,0:T(8,128)} %get-tuple-element.470) | copy-start | bytes 62914564 | tf_op jit(solution)/shard_map/while
  328.5 13.1 %copy-start.2 = (f32[8,512,160,8]{1,2,3,0:T(8,128)S(1)}, f32[8,512,160,8]{1,2,3,0:T(8,128)}, u32[]{:S(2)}) copy-start(f32[8,512,160,8]{1,2,3,0:T(8,128)} %get-tuple-element.470) | copy-start | bytes 62914564 | tf_op jit(solution)/shard_map/while
  354.8 6.1 %copy-start.4 = (f32[18,64]{1,0:T(8,128)S(1)}, f32[18,64]{1,0:T(8,128)}, u32[]{:S(2)}) copy-start(f32[18,64]{1,0:T(8,128)} %slice_bitcast_fusion.1) | copy-start | bytes 13828
  354.8 6.1 %copy-start.5 = (f32[18,64]{1,0:T(8,128)S(1)}, f32[18,64]{1,0:T(8,128)}, u32[]{:S(2)}) copy-start(f32[18,64]{1,0:T(8,128)} %slice_bitcast_fusion.2) | copy-start | bytes 13828
  417.9 2.0 copy-start.1
Sparse Core Ops, SparseCore 0:
  10.3 83.1 all-gather.12
  95.2 64.1 all-gather.10
  161.1 72.4 all-gather.14
where the time goes:
time: 429 us; the launch traced here: 426 us
  matrix products  113 us (26%)
  other arithmetic  102 us (24%)
  local copies, waits for them, and re-layouts  97.9 us (23%)
  waiting for transfers between devices  56.6 us (13%)
  blocking collectives  37.7 us (9%)
  between operations  14.1 us (3%)
  loops' own time  4.85 us (1%)
    reduce_sum x5, other arithmetic, block_update(): totals = totals * shrink + jnp.sum(weights, axis=-1)  58.9 us
    dot_general x5, matrix products, block_update(): jnp.einsum('qgre,kge->grqk', queries, key_rows, preferred_element_type=jn...  48.7 us
    all_gather x1, waiting for transfers between devices, body(): gathered = lax.all_gather(pre_kv[None], 'pool', axis=0, tiled=True)  47 us
    dot_general x5, matrix products, block_update(): jnp.einsum('grqk,kge->grqe', weights.astype(jnp.bfloat16), value_rows, pr...  44.9 us
    all_gather x2, blocking collectives, combined_all(): gathered = jax.tree.map(lambda a: lax.all_gather(a, axis), part)  37.7 us
    unnamed x32, local copies, waits for them, and re-layouts  33.4 us
    while x75, local copies, waits for them, and re-layouts  23.6 us
    add x15, other arithmetic, combine_partials(): summed_one.reshape(row_count, head_count, -1) * weight_one[..., None]  22.2 us
  transfers between devices with their start and end apart: 3, of which 2 were waited for; matrix products, arithmetic and copies ran while one was open for 58% of the time, Pallas kernels for 0%

commit v1 on v0

v1 whole, which is shorter than its diff:
```python
import functools
import math

import jax
import jax.numpy as jnp
import numpy as np
from jax import lax
from jax.experimental import pallas as pl
from jax.experimental.pallas import tpu as pltpu
from jax.sharding import PartitionSpec as P

H = 64
KVH = 8
REP = H // KVH
HD = 128
STEPS = 4
MOST = 2
POOL = 8
TP = 16
HALF = KVH // 2
NEGATIVE = -1e30
FLOOR = -1e29
SCALE2 = math.log2(math.e) / math.sqrt(HD)
LOG2E = math.log2(math.e)
TILE = 512
UNIT = 64
COLS = 256
VMEM_BYTES = 48 * 1024 * 1024


def params(limit=VMEM_BYTES):
    return pltpu.CompilerParams(vmem_limit_bytes=limit)


def dot_nt(a, b):
    return lax.dot_general(a, b, (((1,), (1,)), ((), ())), preferred_element_type=jnp.float32)


def dot_nn(a, b):
    return lax.dot_general(a, b, (((1,), (0,)), ((), ())), preferred_element_type=jnp.float32)


def prep_kv_kernel(info, kv_ref, own_ref, sib_ref):
    core = info[1]
    for g in range(HALF):
        for half, ref in ((core, own_ref), (1 - core, sib_ref)):
            at = pl.multiple_of((half * HALF + g) * HD, HD)
            ref[g] = kv_ref[:, :, pl.ds(at, HD)]


def prep_kv(info, pre_kv):
    _, tokens, width = pre_kv.shape
    half = jax.ShapeDtypeStruct((HALF, 2, tokens, HD), jnp.bfloat16)
    return pl.pallas_call(
        prep_kv_kernel,
        out_shape=(half, half),
        grid_spec=pltpu.PrefetchScalarGridSpec(
            num_scalar_prefetch=1,
            grid=(1,),
            in_specs=[pl.BlockSpec((2, tokens, width), lambda i, s: (0, 0, 0))],
            out_specs=(
                pl.BlockSpec((HALF, 2, tokens, HD), lambda i, s: (0, 0, 0, 0)),
                pl.BlockSpec((HALF, 2, tokens, HD), lambda i, s: (0, 0, 0, 0)),
            ),
        ),
        compiler_params=params(),
        name="prep_kv",
    )(info, pre_kv)


def copy_kernel(info, x_ref, out_ref):
    out_ref[...] = x_ref[...]


def other_half(info, pre_q):
    tokens = pre_q.shape[0]
    return pl.pallas_call(
        copy_kernel,
        out_shape=jax.ShapeDtypeStruct((tokens, HALF * REP * HD), jnp.bfloat16),
        grid_spec=pltpu.PrefetchScalarGridSpec(
            num_scalar_prefetch=1,
            grid=(2,),
            in_specs=[
                pl.BlockSpec((tokens, 2 * REP * HD), lambda g, s: (0, (1 - s[1]) * 2 + g))
            ],
            out_specs=pl.BlockSpec((tokens, 2 * REP * HD), lambda g, s: (0, g)),
        ),
        compiler_params=params(),
        name="other_half",
    )(info, pre_q)


def place_kernel(info, kept_ref, x_ref, out_ref):
    del kept_ref
    out_ref[...] = x_ref[...]


def place(info, out, x):
    tokens, width = x.shape
    return pl.pallas_call(
        place_kernel,
        out_shape=jax.ShapeDtypeStruct(out.shape, out.dtype),
        grid_spec=pltpu.PrefetchScalarGridSpec(
            num_scalar_prefetch=1,
            grid=(5,),
            in_specs=[
                pl.BlockSpec(memory_space=pl.ANY),
                pl.BlockSpec((tokens // 5, width), lambda i, s: (i, 0)),
            ],
            out_specs=pl.BlockSpec((tokens // 5, width), lambda i, s: (i, 1 - s[1])),
        ),
        input_output_aliases={1: 0},
        compiler_params=params(),
        name="place",
    )(info, out, x)


def prefill_kernel(info, pos_ref, qa_ref, qb_ref, *refs, kinds, first, last):
    count = len(kinds)
    parts, refs = refs[:count], refs[count:]
    if not first:
        carry, refs = ((refs[0], refs[1]), (refs[2], refs[3])), refs[4:]
    if last:
        outs, refs = refs[:2], refs[2:]
    else:
        outs, refs = ((refs[0], refs[1]), (refs[2], refs[3])), refs[4:]
    k_all, v_all, v_across, q_all, s_all, top_all = refs[:6]
    g = pl.program_id(0)
    heads = pl.num_programs(0) - 1
    core = info[1]
    tokens = parts[0].shape[3]
    shard = 2 * tokens
    keys = count * shard
    blocks = q_all.shape[1] // COLS
    tiles = [(lo, min(lo + TILE, keys)) for lo in range(0, keys, TILE)]
    valid = [None if kind < 0 else info[kind] == 1 for kind in kinds]

    @pl.when(g < heads)
    def _():
        for i, part in enumerate(parts):
            for k in range(2):
                at = i * shard + k * tokens
                k_all[at : at + tokens, :] = part[k, 0, 0]
                v_all[at : at + tokens, :] = part[k, 0, 1]
        if v_all.shape[0] > keys:
            v_all[keys:, :] = jnp.zeros((v_all.shape[0] - keys, HD), jnp.bfloat16)
        for at in range(0, v_all.shape[0], 128):
            v_across[g % 2, :, at : at + 128] = v_all[at : at + 128, :].T
        for h in range(REP):
            at = h * tokens
            q_all[0, at : at + tokens, :] = qa_ref[:, h * HD : (h + 1) * HD]
            q_all[1, at : at + tokens, :] = qb_ref[:, h * HD : (h + 1) * HD]

    def scores(side, n):
        q = q_all[side, n * COLS : (n + 1) * COLS, :]
        top = None
        for lo, hi in tiles:
            s = dot_nt(k_all[lo:hi, :], q)
            for at in range(lo, hi, UNIT):
                piece = s[at - lo : at - lo + UNIT, :]
                which = at // shard
                if valid[which] is None:
                    key = lax.broadcasted_iota(jnp.int32, piece.shape, 0) + (at - which * shard)
                    key = jnp.where(key < tokens, key + core * tokens, key - core * tokens)
                    seen = key <= pos_ref[side, n : n + 1, :]
                    piece = jnp.where(seen, piece, NEGATIVE)
                s_all[side, n, at : at + UNIT, :] = piece
                part = jnp.max(piece.reshape(UNIT // 8, 8, COLS), axis=0)
                if valid[which] is not None:
                    part = jnp.where(valid[which], part, NEGATIVE)
                top = part if top is None else jnp.maximum(top, part)
            yield
        top_all[side, n] = top

    def finish(side, n, slot):
        peak = jnp.max(top_all[side, n], axis=0, keepdims=True)
        if not first:
            acc_in, stat_in = carry[side]
            before = stat_in[0, n, 0:1, :]
            peak = jnp.maximum(before, peak)
            shrink = jnp.exp2((before - peak) * SCALE2)
        total = None
        acc = None
        for lo, hi in tiles:
            rounded = []
            for at in range(lo, hi, UNIT):
                which = at // shard
                base = peak if valid[which] is None else jnp.where(valid[which], peak, -NEGATIVE)
                w = jnp.exp2((s_all[side, n, at : at + UNIT, :] - base) * SCALE2)
                part = jnp.sum(w.reshape(UNIT // 8, 8, COLS), axis=0)
                total = part if total is None else total + part
                rounded.append(w.astype(jnp.bfloat16))
            w = jnp.concatenate(rounded, axis=0)
            part = dot_nn(v_across[slot, :, lo:hi], w)
            acc = part if acc is None else acc + part
            yield
        total = jnp.sum(total, axis=0, keepdims=True)
        if not first:
            acc = acc + acc_in[0, n] * shrink
            total = total + stat_in[0, n, 1:2, :] * shrink
        if last:
            stage = refs[6]
            stage[side, n * COLS : (n + 1) * COLS, :] = (acc / total).T.astype(jnp.bfloat16)
        else:
            acc_out, stat_out = outs[side]
            acc_out[0, n] = acc
            line = lax.broadcasted_iota(jnp.int32, (8, COLS), 0)
            stat_out[0, n] = jnp.where(line == 0, peak, total)

    def drain(steps):
        live = list(steps)
        while live:
            for step in list(live):
                if next(step, live) is live:
                    live.remove(step)

    def both(scored, finished, slot):
        steps = []
        for n in range(blocks):
            if scored is not None:
                steps.append(scores(scored, n))
            if finished is not None:
                steps.append(finish(finished, n, slot))
        drain(steps)
        if last and finished is not None:
            stage = refs[6]
            for h in range(REP):
                at = h * tokens
                outs[finished][:, h * HD : (h + 1) * HD] = stage[finished, at : at + tokens, :]

    before = (g + 1) % 2
    pl.when(g == 0)(lambda: both(0, None, None))
    pl.when(jnp.logical_and(g > 0, g < heads))(lambda: both(0, 1, before))
    pl.when(g == heads)(lambda: both(None, 1, before))
    pl.when(g < heads)(lambda: both(1, 0, g % 2))


def prefill(info, pos, pre_q, q_sib, parts, kinds, carry, last):
    tokens = pre_q.shape[0]
    rows = REP * tokens
    blocks = rows // COLS
    first = carry is None
    keys = len(parts) * 2 * tokens
    room = -(-keys // 128) * 128

    def now(g):
        return jnp.minimum(g, HALF - 1)

    def late(g):
        return jnp.maximum(g - 1, 0)

    in_specs = [
        pl.BlockSpec(pos.shape, lambda g, s: (0, 0, 0)),
        pl.BlockSpec((tokens, REP * HD), lambda g, s: (0, s[1] * HALF + now(g))),
        pl.BlockSpec((tokens, REP * HD), lambda g, s: (0, now(g))),
    ]
    in_specs += [
        pl.BlockSpec((2, 1, 2, tokens, HD), lambda g, s: (0, now(g), 0, 0, 0)) for _ in parts
    ]
    args = [pos, pre_q, q_sib, *parts]
    carry_specs = [
        pl.BlockSpec((1, blocks, HD, COLS), lambda g, s: (now(g), 0, 0, 0)),
        pl.BlockSpec((1, blocks, 8, COLS), lambda g, s: (now(g), 0, 0, 0)),
        pl.BlockSpec((1, blocks, HD, COLS), lambda g, s: (late(g), 0, 0, 0)),
        pl.BlockSpec((1, blocks, 8, COLS), lambda g, s: (late(g), 0, 0, 0)),
    ]
    if not first:
        in_specs += carry_specs
        args += list(carry)
    scratch = [
        pltpu.VMEM((keys, HD), jnp.bfloat16),
        pltpu.VMEM((room, HD), jnp.bfloat16),
        pltpu.VMEM((2, HD, room), jnp.bfloat16),
        pltpu.VMEM((2, rows, HD), jnp.bfloat16),
        pltpu.VMEM((2, blocks, keys, COLS), jnp.float32),
        pltpu.VMEM((2, blocks, 8, COLS), jnp.float32),
    ]
    if last:
        out_shape = [
            jax.ShapeDtypeStruct(pre_q.shape, jnp.bfloat16),
            jax.ShapeDtypeStruct(q_sib.shape, jnp.bfloat16),
        ]
        out_specs = [
            pl.BlockSpec((tokens, REP * HD), lambda g, s: (0, s[1] * HALF + now(g))),
            pl.BlockSpec((tokens, REP * HD), lambda g, s: (0, late(g))),
        ]
        scratch.append(pltpu.VMEM((2, rows, HD), jnp.bfloat16))
    else:
        out_shape = [
            jax.ShapeDtypeStruct((HALF, blocks, HD, COLS), jnp.float32),
            jax.ShapeDtypeStruct((HALF, blocks, 8, COLS), jnp.float32),
        ] * 2
        out_specs = carry_specs
    return pl.pallas_call(
        functools.partial(prefill_kernel, kinds=kinds, first=first, last=last),
        out_shape=out_shape,
        grid_spec=pltpu.PrefetchScalarGridSpec(
            num_scalar_prefetch=1,
            grid=(HALF + 1,),
            in_specs=in_specs,
            out_specs=out_specs,
            scratch_shapes=scratch,
        ),
        compiler_params=params(),
        cost_estimate=pl.CostEstimate(
            flops=16 * HALF * rows * keys * HD,
            bytes_accessed=24 * HALF * rows * HD,
            transcendentals=2 * HALF * rows * keys,
        ),
        name="prefill",
    )(info, *args)


def partial_kernel(info, lens, q_ref, aq_ref, cache_ref, tail_ref, pre_ref, out_ref, lse_ref):
    me = info[0]
    r = pl.program_id(0)
    positions = cache_ref.shape[2]
    fresh = tail_ref.shape[2]
    rows = q_ref.shape[2]
    half = rows // 2
    lane = lax.broadcasted_iota(jnp.int32, (half, 128), 1)

    def store(g, slot, peak, total, summed):
        live = total > 0.0
        safe = jnp.where(live, total, 1.0)
        mean = (summed / safe).astype(jnp.bfloat16)
        lse = jnp.where(live, peak * SCALE2 + jnp.log(safe) * LOG2E, NEGATIVE)
        pick = jnp.logical_and(lane % 8 == slot, lane < 24)
        for k in range(2):
            out_ref[2 * g + k, pl.ds(slot, 1)] = mean[k * half : (k + 1) * half][None]
            lse_ref[2 * g + k] = jnp.where(
                pick, lse[k * half : (k + 1) * half], lse_ref[2 * g + k]
            )

    @pl.when(r == 0)
    def _():
        lse_ref[...] = jnp.zeros_like(lse_ref)
        for g in range(KVH):
            cols = slice(g * HD, (g + 1) * HD)
            s = dot_nt(aq_ref[0, g], pre_ref[0, :, cols])
            peak = jnp.max(s, axis=-1, keepdims=True)
            w = jnp.exp2((s - peak) * SCALE2)
            total = jnp.sum(w, axis=-1, keepdims=True)
            store(g, 4, peak, total, dot_nn(w.astype(jnp.bfloat16), pre_ref[1, :, cols]))

    live_here = lens[r] - me * positions
    shown = lax.broadcasted_iota(jnp.int32, (rows, positions), 1) < live_here
    step = (lax.broadcasted_iota(jnp.int32, (rows, fresh), 0) % half) // (half // STEPS)
    at = lax.broadcasted_iota(jnp.int32, (rows, fresh), 1)
    tail_shown = jnp.logical_and(at <= step, me == 0)
    heads = [slice(g * HD, (g + 1) * HD) for g in range(KVH)]
    old = [dot_nt(q_ref[0, g], cache_ref[0, 0, :, cols]) for g, cols in enumerate(heads)]
    new = [dot_nt(q_ref[0, g], tail_ref[0, 0, :, cols]) for g, cols in enumerate(heads)]
    old = [jnp.where(shown, s, NEGATIVE) for s in old]
    new = [jnp.where(tail_shown, t, NEGATIVE) for t in new]
    peaks = [
        jnp.maximum(jnp.max(s, axis=-1, keepdims=True), jnp.max(t, axis=-1, keepdims=True))
        for s, t in zip(old, new)
    ]
    peaks = [jnp.maximum(peak, FLOOR) for peak in peaks]
    old = [jnp.exp2((s - peak) * SCALE2) for s, peak in zip(old, peaks)]
    new = [jnp.exp2((t - peak) * SCALE2) for t, peak in zip(new, peaks)]
    totals = [
        jnp.sum(w, axis=-1, keepdims=True) + jnp.sum(u, axis=-1, keepdims=True)
        for w, u in zip(old, new)
    ]
    old = [w.astype(jnp.bfloat16) for w in old]
    new = [u.astype(jnp.bfloat16) for u in new]
    sums = [
        dot_nn(old[g], cache_ref[1, 0, :, cols]) + dot_nn(new[g], tail_ref[1, 0, :, cols])
        for g, cols in enumerate(heads)
    ]
    for g in range(KVH):
        store(g, r, peaks[g], totals[g], sums[g])

    @pl.when(r == pl.num_programs(0) - 1)
    def _():
        x = lse_ref[...]
        high = x.astype(jnp.bfloat16)
        rest = x - high.astype(jnp.float32)
        mid = rest.astype(jnp.bfloat16)
        low = (rest - mid.astype(jnp.float32)).astype(jnp.bfloat16)
        at = lax.broadcasted_iota(jnp.int32, x.shape, 2)
        parts = jnp.where(
            at < 8,
            high.astype(jnp.float32),
            jnp.where(at < 16, mid.astype(jnp.float32), low.astype(jnp.float32)),
        )
        out_ref[:, 5] = parts.astype(jnp.bfloat16)


def partials(info, lengths, q, arrival, cache_kv, tail, pre_kv):
    requests = lengths.shape[0]
    positions = cache_kv.shape[2]
    tokens = pre_kv.shape[1]
    fresh = tail.shape[2]
    rows = q.shape[2]
    half = rows // 2
    return pl.pallas_call(
        partial_kernel,
        out_shape=jax.ShapeDtypeStruct((TP, requests + 2, half, HD), jnp.bfloat16),
        grid_spec=pltpu.PrefetchScalarGridSpec(
            num_scalar_prefetch=2,
            grid=(requests,),
            in_specs=[
                pl.BlockSpec((1, KVH, rows, HD), lambda r, *_: (r, 0, 0, 0)),
                pl.BlockSpec((1, KVH, rows, HD), lambda r, *_: (0, 0, 0, 0)),
                pl.BlockSpec((2, 1, positions, KVH * HD), lambda r, *_: (0, r, 0, 0)),
                pl.BlockSpec((2, 1, fresh, KVH * HD), lambda r, *_: (0, r, 0, 0)),
                pl.BlockSpec((2, tokens, KVH * HD), lambda r, *_: (0, 0, 0)),
            ],
            out_specs=pl.BlockSpec((TP, requests + 2, half, HD), lambda r, *_: (0, 0, 0, 0)),
            scratch_shapes=[pltpu.VMEM((TP, half, 128), jnp.float32)],
        ),
        compiler_params=params(),
        cost_estimate=pl.CostEstimate(
            flops=40 * rows * KVH * positions * HD * requests,
            bytes_accessed=4 * requests * positions * KVH * HD,
            transcendentals=rows * KVH * positions * requests,
        ),
        name="partials",
    )(info, lengths, q, arrival, cache_kv, tail, pre_kv)


def merge_kernel(x_ref, dec_ref, arr_ref):
    lse = x_ref[:, 5].astype(jnp.float32)
    lane = lax.broadcasted_iota(jnp.int32, lse.shape, 2)
    for slot in range(5):
        pick = jnp.logical_and(lane % 8 == slot, lane < 24)
        mine = jnp.sum(jnp.where(pick, lse, 0.0), axis=-1, keepdims=True)
        top = jnp.max(mine, axis=0, keepdims=True)
        w = jnp.exp2(mine - top)
        total = jnp.sum(w, axis=0)
        mixed = jnp.sum(w * x_ref[:, slot].astype(jnp.float32), axis=0) / total
        if slot < 4:
            dec_ref[slot] = mixed.astype(jnp.bfloat16)
        else:
            arr_ref[...] = mixed.astype(jnp.bfloat16)


def merge(x):
    half = x.shape[2]
    return pl.pallas_call(
        merge_kernel,
        out_shape=(
            jax.ShapeDtypeStruct((4, half, HD), jnp.bfloat16),
            jax.ShapeDtypeStruct((half, HD), jnp.bfloat16),
        ),
        name="merge",
    )(x)


def receive_kernel(table, same_ref, other_ref, out_ref):
    m = pl.program_id(0)
    held, there = table[MOST + m] == 1, table[2 * MOST + m] == 1
    block = jnp.where(there, other_ref[0], same_ref[0])
    out_ref[:, 0] = jnp.where(held, block, jnp.zeros_like(block))


def receive(table, same, other):
    _, two, tokens, width = same.shape
    block = pl.BlockSpec((1, two, tokens, width), lambda m, t: (t[m], 0, 0, 0))
    return pl.pallas_call(
        receive_kernel,
        out_shape=jax.ShapeDtypeStruct((two, MOST, tokens, width), jnp.bfloat16),
        grid_spec=pltpu.PrefetchScalarGridSpec(
            num_scalar_prefetch=1,
            grid=(MOST,),
            in_specs=[block, block],
            out_specs=pl.BlockSpec((two, 1, tokens, width), lambda m, t: (0, m, 0, 0)),
        ),
        compiler_params=params(60 * 1024 * 1024),
        name="receive",
    )(table, same, other)


def body(pre_q, pre_kv, arrival_q, owner, cache_kv, lengths, dec_q, new_kv):
    tokens = pre_q.shape[0]
    me = lax.axis_index("tp").astype(jnp.int32)
    pool = lax.axis_index("pool").astype(jnp.int32)
    x, y = me // 4, me // 2 % 2
    flags = [x >= 1, x >= 2, x == 3, y == 1]
    info = jnp.stack([me, me % 2] + [f.astype(jnp.int32) for f in flags])
    back1, back2, wrapped, upper = 2, 3, 4, 5

    def permute(a, pairs):
        return lax.ppermute(a, "tp", pairs)

    swap = [(t, t ^ 1) for t in range(TP)]
    across = [(t, t ^ 2) for t in range(TP)]
    forward = [(t, t + 4) for t in range(12)]
    around = [(t, t + 12) for t in range(4)]

    kv_own, kv_send = prep_kv(info, pre_kv)
    own = jnp.stack([kv_own, permute(kv_send, swap)])
    q_send = other_half(info, pre_q)
    a1 = permute(own, forward)
    b0 = permute(own, across)
    w1 = permute(own, around)
    q_sib = permute(q_send, swap)
    a2 = permute(a1, forward[4:])
    b1 = permute(a1, across[4:])
    w2 = permute(b0, around)
    b2 = permute(b1, forward[4:])
    _, info_late = lax.optimization_barrier((own, info))

    at = np.arange(REP * tokens) % tokens
    sides = jnp.stack([me % 2, 1 - me % 2]) * tokens
    pos = (sides[:, None] + at[None]).astype(jnp.int32).reshape(2, -1, COLS)

    planes = [[z * 2 + k for z in range(POOL // 2)] for k in range(2)]
    other = lax.ppermute(pre_kv, "pool", [(p, p ^ 1) for p in range(POOL)])
    same = lax.all_gather(pre_kv, "pool", axis=0, axis_index_groups=planes)
    other = lax.all_gather(other, "pool", axis=0, axis_index_groups=planes)
    prompts = jnp.arange(owner.shape[0])
    earlier = jnp.logical_and(
        owner[:, None] == owner[None, :], prompts[None, :] < prompts[:, None]
    )
    rank = jnp.sum(earlier.astype(jnp.int32), axis=1)
    taken = jnp.logical_and(
        owner[None, :] == pool, rank[None, :] == jnp.arange(MOST)[:, None]
    ).astype(jnp.int32)
    prompt_of = jnp.sum(taken * prompts, axis=1)
    held = jnp.sum(taken, axis=1)
    table = jnp.concatenate([prompt_of // 2, held, (prompt_of - pool) % 2]).astype(jnp.int32)
    received = receive(table, same, other)

    requests = lengths.shape[0]
    dec_rows = dec_q.reshape(STEPS, requests, KVH, 2, REP // 2, HD)
    dec_rows = jnp.transpose(dec_rows, (1, 2, 3, 0, 4, 5)).reshape(requests, KVH, STEPS * REP, HD)
    arrival = lax.dynamic_index_in_dim(arrival_q, pool, 0, False)
    arrival = arrival.reshape(KVH, 2, 1, REP // 2, HD)
    arrival = jnp.pad(arrival, ((0, 0), (0, 0), (0, STEPS - 1), (0, 0), (0, 0)))
    arrival = arrival.reshape(1, KVH, STEPS * REP, HD)
    tail = jnp.pad(jnp.transpose(new_kv, (0, 2, 1, 3)), ((0, 0), (0, 0), (0, 12), (0, 0)))
    part = partials(info_late, lengths, dec_rows, arrival, cache_kv, tail, pre_kv)
    part, info_first = lax.optimization_barrier((part, info))
    part = lax.all_to_all(part, "tp", 0, 0)
    decoded, arrived = merge(part)
    arrived, info_next = lax.optimization_barrier((arrived, info))
    decode_out = jnp.transpose(
        decoded.reshape(requests, STEPS, REP // 2, HD), (1, 0, 2, 3)
    ).reshape(STEPS, requests, REP // 2 * HD)

    goes = jnp.logical_and(
        owner[pool] == jnp.arange(POOL)[:, None], rank[pool] == jnp.arange(MOST)[None, :]
    )
    row = arrived[: REP // 2].reshape(1, 1, REP // 2 * HD)
    rows = lax.all_to_all(jnp.where(goes[..., None], row, jnp.zeros_like(row)), "pool", 0, 0)
    arrival_out = jnp.sum(rows.astype(jnp.float32), axis=0).astype(jnp.bfloat16)

    def take(order, parts, kinds, carry, last):
        return prefill(order, pos, pre_q, q_sib, parts, kinds, carry, last)

    carry = take(info_first, [own, a1, b0, w1], [-1, back1, upper, wrapped], None, False)
    carry = take(info_next, [a2, b1, w2], [back2, back1, wrapped], carry, False)
    out, out_send = take(info, [b2], [back2], carry, True)
    prefill_out = place(info, out, permute(out_send, swap))
    return (prefill_out, received, decode_out, arrival_out)


def solution(mesh):
    in_specs = (
        P(("pool", "tp"), None),
        P(None, ("pool", "tp"), None),
        P(),
        P(),
        P(None, "pool", "tp", None),
        P("pool"),
        P(None, "pool", None),
        P(None, None, "pool", None),
    )
    out_specs = (
        P(("pool", "tp"), None),
        P(None, "pool", "tp", None),
        P(None, "pool", "tp"),
        P("pool", "tp"),
    )
    return jax.shard_map(body, mesh=mesh, in_specs=in_specs, out_specs=out_specs, check_vma=False)
```

time: 429 us -> 135 us (0.31)
  matrix products: 113 us -> 0 us
  other arithmetic: 102 us -> 4.87 us
  local copies, waits for them, and re-layouts: 97.9 us -> 4.87 us
  Pallas kernels: 0 us -> 64 us
  waiting for transfers between devices: 56.6 us -> 13.4 us
  blocking collectives: 37.7 us -> 0 us
  starting transfers between devices: 0.11 us -> 32.7 us
  loops' own time: 4.85 us -> 0 us
    dot_general x18 -> x0, matrix products: 113 us -> none  [the longest x5 48.7 us: block_update(): jnp.einsum('qgre,kge->grqk', queries, key_rows, preferred_element_type=jn...]
    pallas_call x0 -> x9, Pallas kernels: none -> 64 us  [the longest x3 44.9 us: prefill(): pl.pallas_call(functools.partial(prefill_kernel, kinds=kinds, first=first...]
    reduce_sum x9 -> x3, other arithmetic: 61.8 us -> 0.93 us  [the longest x1 0.6 us: body(): arrival_out = jnp.sum(rows.astype(jnp.float32), axis=0).astype(jnp.bfloat16)]
    all_gather x3 -> x2, waiting for transfers between devices: 55.2 us -> 0.01 us  [the longest x1 0.01 us: body(): same = lax.all_gather(pre_kv, 'pool', axis=0, axis_index_groups=planes)]
    all_gather x2 -> x0, blocking collectives: 37.7 us -> none  [combined_all(): gathered = jax.tree.map(lambda a: lax.all_gather(a, axis), part)]
    add x47 -> x1, other arithmetic: 33.7 us -> 0.07 us  [body(): pos = (sides[:, None] + at[None]).astype(jnp.int32).reshape(2, -1, COLS)]
    unnamed x32 -> x19, local copies, waits for them, and re-layouts: 33.4 us -> 1.82 us
    while x75 -> x0, local copies, waits for them, and re-layouts: 23.6 us -> none
  transfers between devices with their start and end apart: 3 -> 15, of which waited for: 2 -> 2; matrix products, arithmetic and copies ran while one was open for 58% -> 6% of each run, Pallas kernels for 0% -> 45%
where the time goes in v1:
time: 135 us; the launch traced here: 134 us
  Pallas kernels  64 us (47%)
  starting transfers between devices  32.7 us (24%)
  between operations  14.3 us (11%)
  waiting for transfers between devices  13.4 us (10%)
  local copies, waits for them, and re-layouts  4.87 us (4%)
  other arithmetic  4.87 us (4%)
    pallas_call x3, Pallas kernels, prefill(): pl.pallas_call(functools.partial(prefill_kernel, kinds=kinds, first=first...  44.9 us
    ppermute x10, starting transfers between devices, permute(): return lax.ppermute(a, 'tp', pairs)  19.3 us
    pallas_call x1, Pallas kernels, partials(): pl.pallas_call(partial_kernel, out_shape=jax.ShapeDtypeStruct((TP, reques...  9.6 us
    all_to_all x1, waiting for transfers between devices, body(): part = lax.all_to_all(part, 'tp', 0, 0)  7.35 us
    all_to_all x1, waiting for transfers between devices, body(): lax.all_to_all(jnp.where(goes[..., None], row, jnp.zeros_like(row)), 'poo...  5.27 us
    all_to_all x1, starting transfers between devices, body(): part = lax.all_to_all(part, 'tp', 0, 0)  5.24 us
    all_to_all x1, starting transfers between devices, body(): lax.all_to_all(jnp.where(goes[..., None], row, jnp.zeros_like(row)), 'poo...  5.04 us
    pallas_call x1, Pallas kernels, receive(): pl.pallas_call(receive_kernel, out_shape=jax.ShapeDtypeStruct((two, MOST,...  3.28 us
  transfers between devices with their start and end apart: 15, of which 2 were waited for; matrix products, arithmetic and copies ran while one was open for 6% of the time, Pallas kernels for 45%

profile of v1, /device:TPU:1, one launch (start us, length us, event | category | flops | bytes accessed | tf_op | source)
XLA Modules:
  0.0 134.2 jit_solution(9853729344018303565)
XLA Ops:
  7.2 0.0 all-gather.5.cloned.1.call-start
  7.2 0.7 all-gather.5.cloned.1.call-update
  8.0 0.1 stack.59.info
  8.1 1.7 %copy-done.2 = bf16[160,8192]{1,0:T(8,128)(2,1)S(1)} copy-done((bf16[160,8192]{1,0:T(8,128)(2,1)S(1)}, bf16[160,8192]{1,0:T(8,128)(2,1)}, u32[]{:S(2)}) %copy-start.2) | copy-done | bytes 2621464
  9.8 0.9 other_half.1
  10.7 1.5 %collective-permute-start = (bf16[160,4096]{1,0:T(8,128)(2,1)S(1)}, bf16[160,4096]{1,0:T(8,128)(2,1)}, u32[]{:S(2)}, u32[]{:S(2)}) collective-permute-start(bf16[160,4096]{1,0:T(8,128)(2,1)S(1)} %other_half.1), channel_id=1, source_target_pairs={{0,1},{1,0},{2,3},{3,2},{4,5},{5,4},{6,7},{7,6},{8,9},{9,8},{10,11... | collective-permute-start | bytes 3932168 | tf_op jit(solution)/shard_map/ppermute | solution.py:487
  12.2 0.7 prep_kv.1
  12.9 0.1 collective-permute-start.1
  13.0 3.1 %collective-permute-start.10 = (bf16[2,160,1024]{2,1,0:T(8,128)(2,1)S(1)}, bf16[2,160,1024]{2,1,0:T(8,128)(2,1)}, u32[]{:S(2)}, u32[]{:S(2)}) collective-permute-start(bf16[2,160,1024]{2,1,0:T(8,128)(2,1)S(1)} %copy-done.1), channel_id=1, source_target_pairs={{0,16},{16,0},{32,48},{48,32},{64,80},{80,64},{96,112},{112,96},{1... | collective-permute-start | bytes 1966088 | tf_op jit(solution)/shard_map/ppermute | solution.py:512
  16.1 0.3 reshape.99
  16.4 0.1 copy.23
  16.6 0.1 dynamic-slice_reduce_fusion
  16.8 0.2 convert_reduce_fusion
  16.9 0.6 dynamic_slice.12
  17.5 0.1 add_multiply_fusion
  17.6 1.0 pad_maximum_fusion.refs_0_
  18.6 4.0 %collective-permute-start.2 = (bf16[2,4,2,160,128]{4,3,2,1,0:T(8,128)(2,1)S(1)}, bf16[2,4,2,160,128]{4,3,2,1,0:T(8,128)(2,1)}, u32[]{:S(2)}, u32[]{:S(2)}) collective-permute-start(bf16[2,4,2,160,128]{4,3,2,1,0:T(8,128)(2,1)S(1)} %pad_maximum_fusion.refs_0_), channel_id=1, source_target_pairs={{0,4},{1,5},{2,6},{3,7},{4,8},{5,9},{6,10},{7,11},{8,12},{9,13},{1... | collective-permute-start | bytes 1966088 | tf_op jit(solution)/shard_map/ppermute | solution.py:487
  22.7 0.4 collective-permute-start.6
  23.1 2.6 %collective-permute-start.8 = (bf16[2,4,2,160,128]{4,3,2,1,0:T(8,128)(2,1)S(1)}, bf16[2,4,2,160,128]{4,3,2,1,0:T(8,128)(2,1)}, u32[]{:S(2)}, u32[]{:S(2)}) collective-permute-start(bf16[2,4,2,160,128]{4,3,2,1,0:T(8,128)(2,1)S(1)} %pad_maximum_fusion.refs_0_), channel_id=1, source_target_pairs={{0,12},{1,13},{2,14},{3,15},{16,28},{17,29},{18,30},{19,31},{32,44... | collective-permute-start | bytes 1966088 | tf_op jit(solution)/shard_map/ppermute | solution.py:487
  25.6 9.6 %partials.1 = bf16[16,6,16,128]{3,2,1,0:T(8,128)(2,1)} custom-call(s32[6]{0:T(128)S(1)} %stack.59.info, s32[4]{0:T(128)S(1)} %copy-done.3, bf16[4,8,32,128]{3,2,1,0:T(8,128)(2,1)S(1)} %bitcast.28, bf16[1,8,32,128]{3,2,1,0:T(8,128)(2,1)S(1)} %bitcast.30, bf16[2,4,512,1024]{3,2,1,0:T(8,128)(2,1)} %cache_ref.1, bf16[2,4,16,1024]{3,2,1,0:T(8,128)(2,1)S(1)} %pad.9.tail_ref, ...), custom_call_target="tpu_custom_call" | custom-call | flops 2684354560 | bytes 8388608 | tf_op jit(solution)/shard_map/partials/pallas_call | solution.py:399
  35.2 5.2 %all-to-all-start = ((bf16[16,6,16,128]{3,2,1,0:T(8,128)(2,1)}), bf16[16,6,16,128]{3,2,1,0:T(8,128)(2,1)}, u32[]{:S(2)}, u32[]{:S(2)}) async-start(bf16[16,6,16,128]{3,2,1,0:T(8,128)(2,1)} %partials.1), calls=%async_computation | async-start | bytes 786432 | tf_op jit(solution)/shard_map/all_to_all | solution.py:538
  40.5 0.0 all-gather.7.cloned.1.call-start
  40.5 0.7 iota_compare_fusion.1
  41.2 0.6 dynamic_slice.11
  41.8 0.1 broadcast_add_fusion.pos_ref
  41.9 0.0 all-gather.7.cloned.1.call-update
  41.9 0.7 iota_compare_fusion.2
  42.5 7.4 %all-to-all-done.x_ref = bf16[16,6,16,128]{3,2,1,0:T(8,128)(2,1)} async-done(((bf16[16,6,16,128]{3,2,1,0:T(8,128)(2,1)}), bf16[16,6,16,128]{3,2,1,0:T(8,128)(2,1)}, u32[]{:S(2)}, u32[]{:S(2)}) %all-to-all-start) | async-done | bytes 393248 | tf_op jit(solution)/shard_map/all_to_all | solution.py:538
  49.9 1.9 %merge.1 = (bf16[4,16,128]{2,1,0:T(8,128)(2,1)}, bf16[16,128]{1,0:T(8,128)(2,1)}) custom-call(bf16[16,6,16,128]{3,2,1,0:T(8,128)(2,1)} %all-to-all-done.x_ref), custom_call_target="tpu_custom_call" | custom-call | tf_op jit(solution)/shard_map/merge/pallas_call | solution.py:443
  51.8 0.7 collective-permute-start.3
  52.5 0.7 collective-permute-start.5
  53.2 7.0 %collective-permute-start.7 = (bf16[2,4,2,160,128]{4,3,2,1,0:T(8,128)(2,1)}, bf16[2,4,2,160,128]{4,3,2,1,0:T(8,128)(2,1)S(1)}, u32[]{:S(2)}, u32[]{:S(2)}) collective-permute-start(bf16[2,4,2,160,128]{4,3,2,1,0:T(8,128)(2,1)} %collective-permute-done.6.refs_2_), channel_id=1, source_target_pairs={{0,12},{1,13},{2,14},{3,15},{16,28},{17,29},{18,30},{19,31},{32,44... | collective-permute-start | bytes 1966088 | tf_op jit(solution)/shard_map/ppermute | solution.py:487
  60.3 18.6 %prefill.3 = (f32[4,5,128,256]{3,2,1,0:T(8,128)}, f32[4,5,8,256]{3,2,1,0:T(8,128)S(1)}, f32[4,5,128,256]{3,2,1,0:T(8,128)}, f32[4,5,8,256]{3,2,1,0:T(8,128)S(1)}) custom-call(s32[6]{0:T(128)S(1)} %stack.59.info, s32[2,5,256]{2,1,0:T(8,128)S(1)} %broadcast_add_fusion.pos_ref, bf16[160,8192]{1,0:T(8,128)(2,1)} %qa_ref.5, ...), custom_call_target="tpu_custom_call" | custom-call | flops 13421772800 | bytes 15728640 | tf_op jit(solution)/shard_map/prefill/pallas_call | solution.py:294
  78.8 0.9 collective-permute-start.4
  79.8 16.2 %prefill.4 = (f32[4,5,128,256]{3,2,1,0:T(8,128)}, f32[4,5,8,256]{3,2,1,0:T(8,128)S(1)}, f32[4,5,128,256]{3,2,1,0:T(8,128)}, f32[4,5,8,256]{3,2,1,0:T(8,128)S(1)}) custom-call(s32[6]{0:T(128)S(1)} %stack.59.info, s32[2,5,256]{2,1,0:T(8,128)S(1)} %broadcast_add_fusion.pos_ref, bf16[160,8192]{1,0:T(8,128)(2,1)} %qa_ref.5, ...), custom_call_target="tpu_custom_call" | custom-call | flops 10066329600 | bytes 15728640 | tf_op jit(solution)/shard_map/prefill/pallas_call | solution.py:294
  96.0 10.1 %prefill.5 = (bf16[160,8192]{1,0:T(8,128)(2,1)}, bf16[160,4096]{1,0:T(8,128)(2,1)}) custom-call(s32[6]{0:T(128)S(1)} %stack.59.info, s32[2,5,256]{2,1,0:T(8,128)S(1)} %broadcast_add_fusion.pos_ref, bf16[160,8192]{1,0:T(8,128)(2,1)} %qa_ref.5, bf16[160,4096]{1,0:T(8,128)(2,1)} %collective-permute-done.qb_ref, ...), custom_call_target="tpu_custom_call" | custom-call | flops 3355443200 | bytes 15728640 | tf_op jit(solution)/shard_map/prefill/pallas_call | solution.py:294
  106.1 1.4 %collective-permute-start.9 = (bf16[160,4096]{1,0:T(8,128)(2,1)}, bf16[160,4096]{1,0:T(8,128)(2,1)S(1)}, u32[]{:S(2)}, u32[]{:S(2)}) collective-permute-start(bf16[160,4096]{1,0:T(8,128)(2,1)} %get-tuple-element.39), channel_id=1, source_target_pairs={{0,1},{1,0},{2,3},{3,2},{4,5},{5,4},{6,7},{7,6},{8,9},{9,8},{10,11... | collective-permute-start | bytes 3932168 | tf_op jit(solution)/shard_map/ppermute | solution.py:487
  107.5 0.1 convert_reduce_fusion.1
  107.7 0.1 broadcast_and_fusion
  107.8 0.6 slice_bitcast_fusion
  108.4 0.7 broadcast_select_fusion
  109.1 5.0 %all-to-all-start.1 = ((bf16[8,2,512]{2,1,0:T(2,128)(2,1)}), bf16[8,2,512]{2,1,0:T(2,128)(2,1)S(1)}, u32[]{:S(2)}, u32[]{:S(2)}) async-start(bf16[8,2,512]{2,1,0:T(2,128)(2,1)} %broadcast_select_fusion), calls=%async_computation.1 | async-start | bytes 32768 | tf_op jit(solution)/shard_map/all_to_all | solution.py:549
  114.1 0.7 pad_add_fusion.table
  114.8 0.6 copy.27
  115.4 5.3 %all-to-all-done.1 = bf16[8,2,512]{2,1,0:T(2,128)(2,1)S(1)} async-done(((bf16[8,2,512]{2,1,0:T(2,128)(2,1)}), bf16[8,2,512]{2,1,0:T(2,128)(2,1)S(1)}, u32[]{:S(2)}, u32[]{:S(2)}) %all-to-all-start.1) | async-done | bytes 16416 | tf_op jit(solution)/shard_map/all_to_all | solution.py:549
  120.7 0.6 reduce_sum.42
  121.3 2.7 %place.1 = bf16[160,8192]{1,0:T(8,128)(2,1)} custom-call(s32[6]{0:T(128)S(1)} %stack.59.info, bf16[160,8192]{1,0:T(8,128)(2,1)} %get-tuple-element.38.kept_ref, bf16[160,4096]{1,0:T(8,128)(2,1)S(1)} %collective-permute-done.9.x_ref), custom_call_target="tpu_custom_call", output_to_operand_aliasing={{}: (1, {})} | custom-call | tf_op jit(solution)/shard_map/place/pallas_call | solution.py:100
  124.0 3.3 %receive.1 = bf16[2,2,160,1024]{3,2,1,0:T(8,128)(2,1)} custom-call(s32[6]{0:T(128)} %pad_add_fusion.table, bf16[4,2,160,1024]{3,2,1,0:T(8,128)(2,1)} %bitcast.31, bf16[4,2,160,1024]{3,2,1,0:T(8,128)(2,1)} %bitcast.32), custom_call_target="tpu_custom_call" | custom-call | tf_op jit(solution)/shard_map/receive/pallas_call | solution.py:463
  (36 shorter events, 0.2 us)
Async XLA Ops:
  7.2 9.4 %copy-start = (bf16[8,8192]{1,0:T(8,128)(2,1)S(1)}, bf16[8,8192]{1,0:T(8,128)(2,1)}, u32[]{:S(2)}) copy-start(bf16[8,8192]{1,0:T(8,128)(2,1)} %param.11) | copy-start | bytes 393220
  7.2 5.0 %copy-start.1 = (bf16[2,160,1024]{2,1,0:T(8,128)(2,1)S(1)}, bf16[2,160,1024]{2,1,0:T(8,128)(2,1)}, u32[]{:S(2)}) copy-start(bf16[2,160,1024]{2,1,0:T(8,128)(2,1)} %pre_ref.1) | copy-start | bytes 1966084
  7.2 116.8 %all-gather.5.cloned.1.call-start = ((), (), s32[]{:S(2)}) async-start(), calls=%async_computation.2 | async-start | bytes 3276800 | tf_op jit(solution)/shard_map/all_gather | solution.py:513
  8.1 1.7 %copy-start.2 = (bf16[160,8192]{1,0:T(8,128)(2,1)S(1)}, bf16[160,8192]{1,0:T(8,128)(2,1)}, u32[]{:S(2)}) copy-start(bf16[160,8192]{1,0:T(8,128)(2,1)} %qa_ref.5) | copy-start | bytes 7864324
  9.8 6.3 %copy-start.4 = (bf16[4,4,8192]{2,1,0:T(4,128)(2,1)S(1)}, bf16[4,4,8192]{2,1,0:T(4,128)(2,1)}, u32[]{:S(2)}) copy-start(bf16[4,4,8192]{2,1,0:T(4,128)(2,1)} %param.15) | copy-start | bytes 786436
  9.8 6.7 %copy-start.5 = (bf16[2,4,4,1024]{3,2,1,0:T(4,128)(2,1)S(1)}, bf16[2,4,4,1024]{3,2,1,0:T(4,128)(2,1)}, u32[]{:S(2)}) copy-start(bf16[2,4,4,1024]{3,2,1,0:T(4,128)(2,1)} %param.16) | copy-start | bytes 196612
  9.8 6.9 %copy-start.8 = (s32[8]{0:T(128)S(1)}, s32[8]{0:T(128)}, u32[]{:S(2)}) copy-start(s32[8]{0:T(128)} %param.12) | copy-start | bytes 100
  10.7 14.9 %copy-start.3 = (s32[4]{0:T(128)S(1)}, s32[4]{0:T(128)}, u32[]{:S(2)}) copy-start(s32[4]{0:T(128)} %lens.1) | copy-start | bytes 52
  10.7 49.6 %collective-permute-start = (bf16[160,4096]{1,0:T(8,128)(2,1)S(1)}, bf16[160,4096]{1,0:T(8,128)(2,1)}, u32[]{:S(2)}, u32[]{:S(2)}) collective-permute-start(bf16[160,4096]{1,0:T(8,128)(2,1)S(1)} %other_half.1), channel_id=1, source_target_pairs={{0,1},{1,0},{2,3},{3,2},{4,5},{5,4},{6,7},{7,6},{8,9},{9,8},{10,11... | collective-permute-start | bytes 3932168 | tf_op jit(solution)/shard_map/ppermute | solution.py:487
  12.9 4.7 %collective-permute-start.1 = (bf16[4,2,160,128]{3,2,1,0:T(8,128)(2,1)S(1)}, bf16[4,2,160,128]{3,2,1,0:T(8,128)(2,1)}, u32[]{:S(2)}, u32[]{:S(2)}) collective-permute-start(bf16[4,2,160,128]{3,2,1,0:T(8,128)(2,1)S(1)} %get-tuple-element.24), channel_id=1, source_target_pairs={{0,1},{1,0},{2,3},{3,2},{4,5},{5,4},{6,7},{7,6},{8,9},{9,8},{10,11... | collective-permute-start | bytes 983048 | tf_op jit(solution)/shard_map/ppermute | solution.py:487
  13.0 28.8 %collective-permute-start.10 = (bf16[2,160,1024]{2,1,0:T(8,128)(2,1)S(1)}, bf16[2,160,1024]{2,1,0:T(8,128)(2,1)}, u32[]{:S(2)}, u32[]{:S(2)}) collective-permute-start(bf16[2,160,1024]{2,1,0:T(8,128)(2,1)S(1)} %copy-done.1), channel_id=1, source_target_pairs={{0,16},{16,0},{32,48},{48,32},{64,80},{80,64},{96,112},{112,96},{1... | collective-permute-start | bytes 1966088 | tf_op jit(solution)/shard_map/ppermute | solution.py:512
  18.6 33.2 %collective-permute-start.2 = (bf16[2,4,2,160,128]{4,3,2,1,0:T(8,128)(2,1)S(1)}, bf16[2,4,2,160,128]{4,3,2,1,0:T(8,128)(2,1)}, u32[]{:S(2)}, u32[]{:S(2)}) collective-permute-start(bf16[2,4,2,160,128]{4,3,2,1,0:T(8,128)(2,1)S(1)} %pad_maximum_fusion.refs_0_), channel_id=1, source_target_pairs={{0,4},{1,5},{2,6},{3,7},{4,8},{5,9},{6,10},{7,11},{8,12},{9,13},{1... | collective-permute-start | bytes 1966088 | tf_op jit(solution)/shard_map/ppermute | solution.py:487
  22.7 30.6 %collective-permute-start.6 = (bf16[2,4,2,160,128]{4,3,2,1,0:T(8,128)(2,1)S(1)}, bf16[2,4,2,160,128]{4,3,2,1,0:T(8,128)(2,1)}, u32[]{:S(2)}, u32[]{:S(2)}) collective-permute-start(bf16[2,4,2,160,128]{4,3,2,1,0:T(8,128)(2,1)S(1)} %pad_maximum_fusion.refs_0_), channel_id=1, source_target_pairs={{0,2},{1,3},{2,0},{3,1},{4,6},{5,7},{6,4},{7,5},{8,10},{9,11},{10,... | collective-permute-start | bytes 1966088 | tf_op jit(solution)/shard_map/ppermute | solution.py:487
  23.1 37.2 %collective-permute-start.8 = (bf16[2,4,2,160,128]{4,3,2,1,0:T(8,128)(2,1)S(1)}, bf16[2,4,2,160,128]{4,3,2,1,0:T(8,128)(2,1)}, u32[]{:S(2)}, u32[]{:S(2)}) collective-permute-start(bf16[2,4,2,160,128]{4,3,2,1,0:T(8,128)(2,1)S(1)} %pad_maximum_fusion.refs_0_), channel_id=1, source_target_pairs={{0,12},{1,13},{2,14},{3,15},{16,28},{17,29},{18,30},{19,31},{32,44... | collective-permute-start | bytes 1966088 | tf_op jit(solution)/shard_map/ppermute | solution.py:487
  25.6 16.1 %copy-start.7 = (s32[5,256]{1,0:T(8,128)S(1)}, s32[5,256]{1,0:T(8,128)}, u32[]{:S(2)}) copy-start(s32[5,256]{1,0:T(8,128)} %constant.98) | copy-start | bytes 15364
  35.2 14.7 %all-to-all-start = ((bf16[16,6,16,128]{3,2,1,0:T(8,128)(2,1)}), bf16[16,6,16,128]{3,2,1,0:T(8,128)(2,1)}, u32[]{:S(2)}, u32[]{:S(2)}) async-start(bf16[16,6,16,128]{3,2,1,0:T(8,128)(2,1)} %partials.1), calls=%async_computation | async-start | bytes 786432 | tf_op jit(solution)/shard_map/all_to_all | solution.py:538
  40.5 83.6 %all-gather.7.cloned.1.call-start = ((), (), s32[]{:S(2)}) async-start(), calls=%async_computation.3 | async-start | bytes 3276800 | tf_op jit(solution)/shard_map/all_gather | solution.py:514
  51.8 27.0 %collective-permute-start.3 = (bf16[2,4,2,160,128]{4,3,2,1,0:T(8,128)(2,1)}, bf16[2,4,2,160,128]{4,3,2,1,0:T(8,128)(2,1)S(1)}, u32[]{:S(2)}, u32[]{:S(2)}) collective-permute-start(bf16[2,4,2,160,128]{4,3,2,1,0:T(8,128)(2,1)} %collective-permute-done.2.refs_1_), channel_id=1, source_target_pairs={{4,6},{5,7},{6,4},{7,5},{8,10},{9,11},{10,8},{11,9},{12,14},{13,15... | collective-permute-start | bytes 1966088 | tf_op jit(solution)/shard_map/ppermute | solution.py:487
  52.5 27.2 %collective-permute-start.5 = (bf16[2,4,2,160,128]{4,3,2,1,0:T(8,128)(2,1)}, bf16[2,4,2,160,128]{4,3,2,1,0:T(8,128)(2,1)S(1)}, u32[]{:S(2)}, u32[]{:S(2)}) collective-permute-start(bf16[2,4,2,160,128]{4,3,2,1,0:T(8,128)(2,1)} %collective-permute-done.2.refs_1_), channel_id=1, source_target_pairs={{4,8},{5,9},{6,10},{7,11},{8,12},{9,13},{10,14},{11,15},{20,24},{2... | collective-permute-start | bytes 1966088 | tf_op jit(solution)/shard_map/ppermute | solution.py:487
  53.2 26.5 %collective-permute-start.7 = (bf16[2,4,2,160,128]{4,3,2,1,0:T(8,128)(2,1)}, bf16[2,4,2,160,128]{4,3,2,1,0:T(8,128)(2,1)S(1)}, u32[]{:S(2)}, u32[]{:S(2)}) collective-permute-start(bf16[2,4,2,160,128]{4,3,2,1,0:T(8,128)(2,1)} %collective-permute-done.6.refs_2_), channel_id=1, source_target_pairs={{0,12},{1,13},{2,14},{3,15},{16,28},{17,29},{18,30},{19,31},{32,44... | collective-permute-start | bytes 1966088 | tf_op jit(solution)/shard_map/ppermute | solution.py:487
  78.8 17.2 %collective-permute-start.4 = (bf16[2,4,2,160,128]{4,3,2,1,0:T(8,128)(2,1)S(1)}, bf16[2,4,2,160,128]{4,3,2,1,0:T(8,128)(2,1)S(1)}, u32[]{:S(2)}, u32[]{:S(2)}) collective-permute-start(bf16[2,4,2,160,128]{4,3,2,1,0:T(8,128)(2,1)S(1)} %collective-permute-done.3.refs_1_), channel_id=1, source_target_pairs={{4,8},{5,9},{6,10},{7,11},{8,12},{9,13},{10,14},{11,15},{20,24},{2... | collective-permute-start | bytes 1966088 | tf_op jit(solution)/shard_map/ppermute | solution.py:487
  96.0 18.8 %copy-start.6 = (bf16[4,16,128]{2,1,0:T(8,128)(2,1)S(1)}, bf16[4,16,128]{2,1,0:T(8,128)(2,1)}, u32[]{:S(2)}) copy-start(bf16[4,16,128]{2,1,0:T(8,128)(2,1)} %get-tuple-element.40) | copy-start | bytes 49156
  106.1 15.2 %collective-permute-start.9 = (bf16[160,4096]{1,0:T(8,128)(2,1)}, bf16[160,4096]{1,0:T(8,128)(2,1)S(1)}, u32[]{:S(2)}, u32[]{:S(2)}) collective-permute-start(bf16[160,4096]{1,0:T(8,128)(2,1)} %get-tuple-element.39), channel_id=1, source_target_pairs={{0,1},{1,0},{2,3},{3,2},{4,5},{5,4},{6,7},{7,6},{8,9},{9,8},{10,11... | collective-permute-start | bytes 3932168 | tf_op jit(solution)/shard_map/ppermute | solution.py:487
  109.1 11.6 %all-to-all-start.1 = ((bf16[8,2,512]{2,1,0:T(2,128)(2,1)}), bf16[8,2,512]{2,1,0:T(2,128)(2,1)S(1)}, u32[]{:S(2)}, u32[]{:S(2)}) async-start(bf16[8,2,512]{2,1,0:T(2,128)(2,1)} %broadcast_select_fusion), calls=%async_computation.1 | async-start | bytes 32768 | tf_op jit(solution)/shard_map/all_to_all | solution.py:549
Sparse Core Ops, SparseCore 0:
  9.7 38.6 all-gather.4
  50.0 35.3 all-gather.6

commit v2 on v1

--- a/solution.py
+++ b/solution.py
@@ -40,12 +40,16 @@
     return lax.dot_general(a, b, (((1,), (0,)), ((), ())), preferred_element_type=jnp.float32)
 
 
-def prep_kv_kernel(info, kv_ref, own_ref, sib_ref):
+def prep_kv_kernel(info, kv_ref, own_ref, sib_ref, piece_ref):
     core = info[1]
     for g in range(HALF):
         for half, ref in ((core, own_ref), (1 - core, sib_ref)):
             at = pl.multiple_of((half * HALF + g) * HD, HD)
             ref[g] = kv_ref[:, :, pl.ds(at, HD)]
+    width = piece_ref.shape[2]
+    for i in range(POOL):
+        at = i % 4 * width
+        piece_ref[i] = kv_ref[i // 4, :, at : at + width]
 
 
 def prep_kv(info, pre_kv):
@@ -53,7 +57,7 @@
     half = jax.ShapeDtypeStruct((HALF, 2, tokens, HD), jnp.bfloat16)
     return pl.pallas_call(
         prep_kv_kernel,
-        out_shape=(half, half),
+        out_shape=(half, half, jax.ShapeDtypeStruct((POOL, tokens, width // 4), jnp.bfloat16)),
         grid_spec=pltpu.PrefetchScalarGridSpec(
             num_scalar_prefetch=1,
             grid=(1,),
@@ -61,6 +65,7 @@
             out_specs=(
                 pl.BlockSpec((HALF, 2, tokens, HD), lambda i, s: (0, 0, 0, 0)),
                 pl.BlockSpec((HALF, 2, tokens, HD), lambda i, s: (0, 0, 0, 0)),
+                pl.BlockSpec((POOL, tokens, width // 4), lambda i, s: (0, 0, 0)),
             ),
         ),
         compiler_params=params(),
@@ -135,8 +140,11 @@
     tiles = [(lo, min(lo + TILE, keys)) for lo in range(0, keys, TILE)]
     valid = [None if kind < 0 else info[kind] == 1 for kind in kinds]
 
-    @pl.when(g < heads)
-    def _():
+    def load():
+        for h in range(REP):
+            at = h * tokens
+            q_all[0, at : at + tokens, :] = qa_ref[:, h * HD : (h + 1) * HD]
+            q_all[1, at : at + tokens, :] = qb_ref[:, h * HD : (h + 1) * HD]
         for i, part in enumerate(parts):
             for k in range(2):
                 at = i * shard + k * tokens
@@ -146,10 +154,6 @@
             v_all[keys:, :] = jnp.zeros((v_all.shape[0] - keys, HD), jnp.bfloat16)
         for at in range(0, v_all.shape[0], 128):
             v_across[g % 2, :, at : at + 128] = v_all[at : at + 128, :].T
-        for h in range(REP):
-            at = h * tokens
-            q_all[0, at : at + tokens, :] = qa_ref[:, h * HD : (h + 1) * HD]
-            q_all[1, at : at + tokens, :] = qb_ref[:, h * HD : (h + 1) * HD]
 
     def scores(side, n):
         q = q_all[side, n * COLS : (n + 1) * COLS, :]
@@ -200,7 +204,7 @@
             total = total + stat_in[0, n, 1:2, :] * shrink
         if last:
             stage = refs[6]
-            stage[side, n * COLS : (n + 1) * COLS, :] = (acc / total).T.astype(jnp.bfloat16)
+            stage[side, n * COLS : (n + 1) * COLS, :] = (acc * (1.0 / total)).T.astype(jnp.bfloat16)
         else:
             acc_out, stat_out = outs[side]
             acc_out[0, n] = acc
@@ -216,6 +220,8 @@
 
     def both(scored, finished, slot):
         steps = []
+        if scored == 0:
+            load()
         for n in range(blocks):
             if scored is not None:
                 steps.append(scores(scored, n))
@@ -311,82 +317,113 @@
     )(info, *args)
 
 
-def partial_kernel(info, lens, q_ref, aq_ref, cache_ref, tail_ref, pre_ref, out_ref, lse_ref):
+def partial_kernel(
+    info, lens, q_ref, aq_ref, cache, tail_ref, pre_ref, out_ref, q_wide, lse_ref, held, sems
+):
     me = info[0]
     r = pl.program_id(0)
-    positions = cache_ref.shape[2]
+    requests, _, positions, _ = held.shape
     fresh = tail_ref.shape[2]
     rows = q_ref.shape[2]
+    wide = KVH * rows
     half = rows // 2
-    lane = lax.broadcasted_iota(jnp.int32, (half, 128), 1)
-
-    def store(g, slot, peak, total, summed):
+
+    chunk = positions // 2
+
+    def copy(i, j, k):
+        some = pl.ds(k * chunk, chunk)
+        return pltpu.make_async_copy(
+            cache.at[j, i, some], held.at[i, j, some], sems.at[i, j, k]
+        )
+
+    @pl.when(r == 0)
+    def _():
+        for i in range(requests):
+            for j in range(2):
+                for k in range(2):
+                    copy(i, j, k).start()
+        q_wide[...] = jnp.zeros_like(q_wide)
+        lse_ref[...] = jnp.zeros_like(lse_ref)
+
+    def spread(ref):
+        lane = lax.broadcasted_iota(jnp.int32, (HD, 128), 1) // rows
+        per = 128 // rows
+        for i in range(KVH // per):
+            turned = ref[0, i * per : (i + 1) * per].reshape(128, HD).T
+            for j in range(per):
+                g = i * per + j
+                q_wide[g * HD : (g + 1) * HD, i * 128 : (i + 1) * 128] = jnp.where(
+                    lane == j, turned, jnp.zeros_like(turned)
+                )
+
+    def fold(w):
+        return w.reshape(w.shape[0] // 8, 8, wide)
+
+    def weigh(s, t, slot):
+        peak = jnp.max(jnp.max(fold(s), axis=0), axis=0, keepdims=True)
+        if t is not None:
+            peak = jnp.maximum(peak, jnp.max(t, axis=0, keepdims=True))
+            peak = jnp.maximum(peak, FLOOR)
+        s = jnp.exp2((s - peak) * SCALE2)
+        total = jnp.sum(jnp.sum(fold(s), axis=0), axis=0, keepdims=True)
+        if t is not None:
+            t = jnp.exp2((t - peak) * SCALE2)
+            total = total + jnp.sum(t, axis=0, keepdims=True)
         live = total > 0.0
         safe = jnp.where(live, total, 1.0)
-        mean = (summed / safe).astype(jnp.bfloat16)
-        lse = jnp.where(live, peak * SCALE2 + jnp.log(safe) * LOG2E, NEGATIVE)
-        pick = jnp.logical_and(lane % 8 == slot, lane < 24)
+        lse_ref[pl.ds(slot, 1), :] = jnp.where(
+            live, peak * SCALE2 + jnp.log(safe) * LOG2E, NEGATIVE
+        )
+        share = jnp.where(live, 1.0 / safe, 0.0)
+        s = (s * share).astype(jnp.bfloat16)
+        return s, None if t is None else t * share
+
+    def store(g, slot, mean):
+        mean = mean.astype(jnp.bfloat16)
         for k in range(2):
             out_ref[2 * g + k, pl.ds(slot, 1)] = mean[k * half : (k + 1) * half][None]
-            lse_ref[2 * g + k] = jnp.where(
-                pick, lse[k * half : (k + 1) * half], lse_ref[2 * g + k]
-            )
 
     @pl.when(r == 0)
     def _():
-        lse_ref[...] = jnp.zeros_like(lse_ref)
+        spread(aq_ref)
+        tokens = pre_ref.shape[1]
+        w, _ = weigh(dot_nn(pre_ref[0], q_wide[...]), None, 4)
+        w = jnp.concatenate([w, jnp.zeros((256 - tokens, wide), jnp.bfloat16)], axis=0).T
         for g in range(KVH):
-            cols = slice(g * HD, (g + 1) * HD)
-            s = dot_nt(aq_ref[0, g], pre_ref[0, :, cols])
-            peak = jnp.max(s, axis=-1, keepdims=True)
-            w = jnp.exp2((s - peak) * SCALE2)
-            total = jnp.sum(w, axis=-1, keepdims=True)
-            store(g, 4, peak, total, dot_nn(w.astype(jnp.bfloat16), pre_ref[1, :, cols]))
-
-    live_here = lens[r] - me * positions
-    shown = lax.broadcasted_iota(jnp.int32, (rows, positions), 1) < live_here
-    step = (lax.broadcasted_iota(jnp.int32, (rows, fresh), 0) % half) // (half // STEPS)
-    at = lax.broadcasted_iota(jnp.int32, (rows, fresh), 1)
+            values = pre_ref[1, :, g * HD : (g + 1) * HD]
+            store(g, 4, dot_nn(w[g * rows : (g + 1) * rows, :tokens], values))
+
+    spread(q_ref)
+    q = q_wide[...]
+    for j in range(2):
+        for k in range(2):
+            copy(r, j, k).wait()
+    shown = lax.broadcasted_iota(jnp.int32, (positions, wide), 0) < lens[r] - me * positions
+    s = jnp.where(shown, dot_nn(held[r, 0], q), NEGATIVE)
+    step = lax.broadcasted_iota(jnp.int32, (fresh, wide), 1) % half // (half // STEPS)
+    at = lax.broadcasted_iota(jnp.int32, (fresh, wide), 0)
     tail_shown = jnp.logical_and(at <= step, me == 0)
-    heads = [slice(g * HD, (g + 1) * HD) for g in range(KVH)]
-    old = [dot_nt(q_ref[0, g], cache_ref[0, 0, :, cols]) for g, cols in enumerate(heads)]
-    new = [dot_nt(q_ref[0, g], tail_ref[0, 0, :, cols]) for g, cols in enumerate(heads)]
-    old = [jnp.where(shown, s, NEGATIVE) for s in old]
-    new = [jnp.where(tail_shown, t, NEGATIVE) for t in new]
-    peaks = [
-        jnp.maximum(jnp.max(s, axis=-1, keepdims=True), jnp.max(t, axis=-1, keepdims=True))
-        for s, t in zip(old, new)
-    ]
-    peaks = [jnp.maximum(peak, FLOOR) for peak in peaks]
-    old = [jnp.exp2((s - peak) * SCALE2) for s, peak in zip(old, peaks)]
-    new = [jnp.exp2((t - peak) * SCALE2) for t, peak in zip(new, peaks)]
-    totals = [
-        jnp.sum(w, axis=-1, keepdims=True) + jnp.sum(u, axis=-1, keepdims=True)
-        for w, u in zip(old, new)
-    ]
-    old = [w.astype(jnp.bfloat16) for w in old]
-    new = [u.astype(jnp.bfloat16) for u in new]
-    sums = [
-        dot_nn(old[g], cache_ref[1, 0, :, cols]) + dot_nn(new[g], tail_ref[1, 0, :, cols])
-        for g, cols in enumerate(heads)
-    ]
+    t = jnp.where(tail_shown, dot_nn(tail_ref[0, 0], q), NEGATIVE)
+    w, u = weigh(s, t, r)
+    w = w.T
+    u = jnp.concatenate([u, jnp.zeros((128 - fresh, wide), jnp.float32)], axis=0).T
+    u = u.astype(jnp.bfloat16)
     for g in range(KVH):
-        store(g, r, peaks[g], totals[g], sums[g])
+        cols = slice(g * HD, (g + 1) * HD)
+        mine = slice(g * rows, (g + 1) * rows)
+        mean = dot_nn(w[mine, :], held[r, 1, :, cols])
+        store(g, r, mean + dot_nn(u[mine, :fresh], tail_ref[1, 0, :, cols]))
 
     @pl.when(r == pl.num_programs(0) - 1)
     def _():
         x = lse_ref[...]
-        high = x.astype(jnp.bfloat16)
-        rest = x - high.astype(jnp.float32)
-        mid = rest.astype(jnp.bfloat16)
-        low = (rest - mid.astype(jnp.float32)).astype(jnp.bfloat16)
-        at = lax.broadcasted_iota(jnp.int32, x.shape, 2)
-        parts = jnp.where(
-            at < 8,
-            high.astype(jnp.float32),
-            jnp.where(at < 16, mid.astype(jnp.float32), low.astype(jnp.float32)),
-        )
-        out_ref[:, 5] = parts.astype(jnp.bfloat16)
+        high = x.astype(jnp.bfloat16).astype(jnp.float32)
+        mid = (x - high).astype(jnp.bfloat16).astype(jnp.float32)
+        low = x - high - mid
+        rest = jnp.zeros((128 - 3 * x.shape[0], wide), jnp.float32)
+        lines = jnp.concatenate([high, mid, low, rest], axis=0).T.astype(jnp.bfloat16)
+        for d in range(TP):
+            out_ref[d, 5] = lines[d * half : (d + 1) * half, :]
 
 
 def partials(info, lengths, q, arrival, cache_kv, tail, pre_kv):
@@ -405,12 +442,17 @@
             in_specs=[
                 pl.BlockSpec((1, KVH, rows, HD), lambda r, *_: (r, 0, 0, 0)),
                 pl.BlockSpec((1, KVH, rows, HD), lambda r, *_: (0, 0, 0, 0)),
-                pl.BlockSpec((2, 1, positions, KVH * HD), lambda r, *_: (0, r, 0, 0)),
+                pl.BlockSpec(memory_space=pl.ANY),
                 pl.BlockSpec((2, 1, fresh, KVH * HD), lambda r, *_: (0, r, 0, 0)),
                 pl.BlockSpec((2, tokens, KVH * HD), lambda r, *_: (0, 0, 0)),
             ],
             out_specs=pl.BlockSpec((TP, requests + 2, half, HD), lambda r, *_: (0, 0, 0, 0)),
-            scratch_shapes=[pltpu.VMEM((TP, half, 128), jnp.float32)],
+            scratch_shapes=[
+                pltpu.VMEM((KVH * HD, KVH * rows), jnp.bfloat16),
+                pltpu.VMEM((8, KVH * rows), jnp.float32),
+                pltpu.VMEM((requests, 2, positions, KVH * HD), jnp.bfloat16),
+                pltpu.SemaphoreType.DMA((requests, 2, 2)),
+            ],
         ),
         compiler_params=params(),
         cost_estimate=pl.CostEstimate(
@@ -450,28 +492,72 @@
     )(x)
 
 
-def receive_kernel(table, same_ref, other_ref, out_ref):
-    m = pl.program_id(0)
-    held, there = table[MOST + m] == 1, table[2 * MOST + m] == 1
-    block = jnp.where(there, other_ref[0], same_ref[0])
-    out_ref[:, 0] = jnp.where(held, block, jnp.zeros_like(block))
-
-
-def receive(table, same, other):
-    _, two, tokens, width = same.shape
-    block = pl.BlockSpec((1, two, tokens, width), lambda m, t: (t[m], 0, 0, 0))
-    return pl.pallas_call(
-        receive_kernel,
-        out_shape=jax.ShapeDtypeStruct((two, MOST, tokens, width), jnp.bfloat16),
-        grid_spec=pltpu.PrefetchScalarGridSpec(
-            num_scalar_prefetch=1,
-            grid=(MOST,),
-            in_specs=[block, block],
-            out_specs=pl.BlockSpec((two, 1, tokens, width), lambda m, t: (0, m, 0, 0)),
-        ),
-        compiler_params=params(60 * 1024 * 1024),
-        name="receive",
-    )(table, same, other)
+def select_kernel(table, x_ref, arr_ref, out_ref):
+    tokens = x_ref.shape[1]
+    pool = table[2 * POOL * MOST]
+    extra = arr_ref.shape[0]
+    for d in range(POOL):
+        for m in range(MOST):
+            prompt = table[d * MOST + m]
+            held = table[POOL * MOST + d * MOST + m] == 1
+            x = x_ref[pl.ds(prompt, 1)]
+            out_ref[d, m, :tokens] = jnp.where(held, x, jnp.zeros_like(x))[0]
+            row = jnp.where(
+                jnp.logical_and(held, prompt == pool), arr_ref[...], jnp.zeros_like(arr_ref)
+            )
+            out_ref[d, m, tokens:, :HD] = row
+            out_ref[d, m, tokens:, HD:] = jnp.zeros((extra, x.shape[2] - HD), jnp.bfloat16)
+
+
+def select(table, pieces, arrived):
+    _, tokens, width = pieces.shape
+    extra = arrived.shape[0]
+    return pl.pallas_call(
+        select_kernel,
+        out_shape=jax.ShapeDtypeStruct((POOL, MOST, tokens + extra, width), jnp.bfloat16),
+        in_specs=[
+            pl.BlockSpec(memory_space=pltpu.SMEM),
+            pl.BlockSpec(memory_space=pltpu.VMEM),
+            pl.BlockSpec(memory_space=pltpu.VMEM),
+        ],
+        out_specs=pl.BlockSpec(memory_space=pltpu.VMEM),
+        compiler_params=params(),
+        name="select",
+    )(table, pieces, arrived)
+
+
+def settle_kernel(table, x_ref, kv_ref, arr_ref):
+    tokens = kv_ref.shape[2]
+    width = x_ref.shape[3]
+    pool = table[2 * POOL * MOST]
+    for m in range(MOST):
+        for i in range(POOL):
+            at = i % 4 * width
+            kv_ref[i // 4, m, :, at : at + width] = x_ref[i, m, :tokens]
+        prompt = table[pool * MOST + m]
+        arr_ref[m] = x_ref[pl.ds(prompt, 1), m, tokens:, :HD][0]
+
+
+def settle(table, x):
+    _, _, rows, width = x.shape
+    tokens = rows - 16
+    return pl.pallas_call(
+        settle_kernel,
+        out_shape=(
+            jax.ShapeDtypeStruct((2, MOST, tokens, KVH * HD), jnp.bfloat16),
+            jax.ShapeDtypeStruct((MOST, rows - tokens, HD), jnp.bfloat16),
+        ),
+        in_specs=[
+            pl.BlockSpec(memory_space=pltpu.SMEM),
+            pl.BlockSpec(memory_space=pltpu.VMEM),
+        ],
+        out_specs=(
+            pl.BlockSpec(memory_space=pltpu.VMEM),
+            pl.BlockSpec(memory_space=pltpu.VMEM),
+        ),
+        compiler_params=params(),
+        name="settle",
+    )(table, x)
 
 
 def body(pre_q, pre_kv, arrival_q, owner, cache_kv, lengths, dec_q, new_kv):
@@ -491,39 +577,22 @@
     forward = [(t, t + 4) for t in range(12)]
     around = [(t, t + 12) for t in range(4)]
 
-    kv_own, kv_send = prep_kv(info, pre_kv)
-    own = jnp.stack([kv_own, permute(kv_send, swap)])
-    q_send = other_half(info, pre_q)
-    a1 = permute(own, forward)
-    b0 = permute(own, across)
-    w1 = permute(own, around)
-    q_sib = permute(q_send, swap)
-    a2 = permute(a1, forward[4:])
-    b1 = permute(a1, across[4:])
-    w2 = permute(b0, around)
-    b2 = permute(b1, forward[4:])
-    _, info_late = lax.optimization_barrier((own, info))
-
     at = np.arange(REP * tokens) % tokens
     sides = jnp.stack([me % 2, 1 - me % 2]) * tokens
     pos = (sides[:, None] + at[None]).astype(jnp.int32).reshape(2, -1, COLS)
 
-    planes = [[z * 2 + k for z in range(POOL // 2)] for k in range(2)]
-    other = lax.ppermute(pre_kv, "pool", [(p, p ^ 1) for p in range(POOL)])
-    same = lax.all_gather(pre_kv, "pool", axis=0, axis_index_groups=planes)
-    other = lax.all_gather(other, "pool", axis=0, axis_index_groups=planes)
     prompts = jnp.arange(owner.shape[0])
     earlier = jnp.logical_and(
         owner[:, None] == owner[None, :], prompts[None, :] < prompts[:, None]
     )
     rank = jnp.sum(earlier.astype(jnp.int32), axis=1)
-    taken = jnp.logical_and(
-        owner[None, :] == pool, rank[None, :] == jnp.arange(MOST)[:, None]
-    ).astype(jnp.int32)
-    prompt_of = jnp.sum(taken * prompts, axis=1)
-    held = jnp.sum(taken, axis=1)
-    table = jnp.concatenate([prompt_of // 2, held, (prompt_of - pool) % 2]).astype(jnp.int32)
-    received = receive(table, same, other)
+    hit = jnp.logical_and(
+        owner[None, None, :] == jnp.arange(POOL)[:, None, None],
+        rank[None, None, :] == jnp.arange(MOST)[None, :, None],
+    )
+    held = jnp.any(hit, axis=-1).astype(jnp.int32)
+    prompt_of = jnp.sum(hit.astype(jnp.int32) * prompts, axis=-1).astype(jnp.int32)
+    table = jnp.concatenate([prompt_of.reshape(-1), held.reshape(-1), pool[None]])
 
     requests = lengths.shape[0]
     dec_rows = dec_q.reshape(STEPS, requests, KVH, 2, REP // 2, HD)
@@ -533,29 +602,48 @@
     arrival = jnp.pad(arrival, ((0, 0), (0, 0), (0, STEPS - 1), (0, 0), (0, 0)))
     arrival = arrival.reshape(1, KVH, STEPS * REP, HD)
     tail = jnp.pad(jnp.transpose(new_kv, (0, 2, 1, 3)), ((0, 0), (0, 0), (0, 12), (0, 0)))
-    part = partials(info_late, lengths, dec_rows, arrival, cache_kv, tail, pre_kv)
-    part, info_first = lax.optimization_barrier((part, info))
+
+    kv_own, kv_send, pieces = prep_kv(info, pre_kv)
+    kv_swapped = permute(kv_send, swap)
+    pieces = lax.all_to_all(pieces, "pool", 0, 0)
+    q_send = other_half(info, pre_q)
+    own = jnp.stack([kv_own, kv_swapped])
+    own, q_send, info_decode = lax.optimization_barrier((own, q_send, info))
+
+    a1 = permute(own, forward)
+    b0 = permute(own, across)
+    w1 = permute(own, around)
+    q_sib = permute(q_send, swap)
+    part = partials(info_decode, lengths, dec_rows, arrival, cache_kv, tail, pre_kv)
     part = lax.all_to_all(part, "tp", 0, 0)
+    part, a1, b0, w1, own, q_sib, info = lax.optimization_barrier(
+        (part, a1, b0, w1, own, q_sib, info)
+    )
+
+    def take(order, parts, kinds, carry, last):
+        return prefill(order, pos, pre_q, q_sib, parts, kinds, carry, last)
+
+    a2 = permute(a1, forward[4:])
+    b1 = permute(a1, across[4:])
+    w2 = permute(b0, around)
+    carry = take(info, [own, a1, b0, w1], [-1, back1, upper, wrapped], None, False)
     decoded, arrived = merge(part)
-    arrived, info_next = lax.optimization_barrier((arrived, info))
+    arrived, pieces, carry, a2, b1, w2, info = lax.optimization_barrier(
+        (arrived, pieces, carry, a2, b1, w2, info)
+    )
+
+    b2 = permute(b1, forward[4:])
+    landed = lax.all_to_all(select(table, pieces, arrived), "pool", 0, 0)
+    carry = take(info, [a2, b1, w2], [back2, back1, wrapped], carry, False)
+    carry, b2, landed, info = lax.optimization_barrier((carry, b2, landed, info))
+
+    out, out_send = take(info, [b2], [back2], carry, True)
+    received, arrival_rows = settle(table, landed)
+    prefill_out = place(info, out, permute(out_send, swap))
+    arrival_out = arrival_rows[:, : REP // 2].reshape(MOST, REP // 2 * HD)
     decode_out = jnp.transpose(
         decoded.reshape(requests, STEPS, REP // 2, HD), (1, 0, 2, 3)
     ).reshape(STEPS, requests, REP // 2 * HD)
-
-    goes = jnp.logical_and(
-        owner[pool] == jnp.arange(POOL)[:, None], rank[pool] == jnp.arange(MOST)[None, :]
-    )
-    row = arrived[: REP // 2].reshape(1, 1, REP // 2 * HD)
-    rows = lax.all_to_all(jnp.where(goes[..., None], row, jnp.zeros_like(row)), "pool", 0, 0)
-    arrival_out = jnp.sum(rows.astype(jnp.float32), axis=0).astype(jnp.bfloat16)
-
-    def take(order, parts, kinds, carry, last):
-        return prefill(order, pos, pre_q, q_sib, parts, kinds, carry, last)
-
-    carry = take(info_first, [own, a1, b0, w1], [-1, back1, upper, wrapped], None, False)
-    carry = take(info_next, [a2, b1, w2], [back2, back1, wrapped], carry, False)
-    out, out_send = take(info, [b2], [back2], carry, True)
-    prefill_out = place(info, out, permute(out_send, swap))
     return (prefill_out, received, decode_out, arrival_out)
 
 

time: 135 us -> 127 us (0.941)
  between operations: 14.3 us -> 0.92 us
  starting transfers between devices: 32.7 us -> 39.5 us
  local copies, waits for them, and re-layouts: 4.87 us -> 11.2 us
  other arithmetic: 4.87 us -> 0.78 us
  waiting for transfers between devices: 13.4 us -> 9.89 us
    all_to_all x1 -> x2, starting transfers between devices: 5.04 us -> 14.7 us  [the longest x1 7.37 us: body(): pieces = lax.all_to_all(pieces, 'pool', 0, 0)]
    unnamed x19 -> x35, local copies, waits for them, and re-layouts: 1.82 us -> 8.66 us
    all_to_all x1 -> x2, waiting for transfers between devices: 5.27 us -> 1.8 us  [the longest x1 1.79 us: body(): landed = lax.all_to_all(select(table, pieces, arrived), 'pool', 0, 0)]
    ppermute x1 -> x0, starting transfers between devices: 3.07 us -> none  [body(): other = lax.ppermute(pre_kv, 'pool', [(p, p ^ 1) for p in range(POOL)])]
    pallas_call x2 -> x3, Pallas kernels: 3.99 us -> 5.16 us  [the longest x1 1.83 us: select(): pl.pallas_call(select_kernel, out_shape=jax.ShapeDtypeStruct((POOL, MOST,...]
  transfers between devices with their start and end apart: 15 -> 13, of which waited for: 2 -> 2; matrix products, arithmetic and copies ran while one was open for 6% -> 4% of each run, Pallas kernels for 45% -> 38%
where the time goes in v2:
time: 127 us; the launch traced here: 126 us
  Pallas kernels  63.9 us (50%)
  starting transfers between devices  39.5 us (31%)
  local copies, waits for them, and re-layouts  11.2 us (9%)
  waiting for transfers between devices  9.89 us (8%)
    pallas_call x3, Pallas kernels, prefill(): pl.pallas_call(functools.partial(prefill_kernel, kinds=kinds, first=first...  44.5 us
    ppermute x10, starting transfers between devices, permute(): return lax.ppermute(a, 'tp', pairs)  20.4 us
    pallas_call x1, Pallas kernels, partials(): pl.pallas_call(partial_kernel, out_shape=jax.ShapeDtypeStruct((TP, reques...  8.7 us
    unnamed x35, local copies, waits for them, and re-layouts  8.66 us
    all_to_all x1, waiting for transfers between devices, body(): part = lax.all_to_all(part, 'tp', 0, 0)  8.07 us
    all_to_all x1, starting transfers between devices, body(): pieces = lax.all_to_all(pieces, 'pool', 0, 0)  7.37 us
    all_to_all x1, starting transfers between devices, body(): landed = lax.all_to_all(select(table, pieces, arrived), 'pool', 0, 0)  7.37 us
    all_to_all x1, starting transfers between devices, body(): part = lax.all_to_all(part, 'tp', 0, 0)  4.4 us
  transfers between devices with their start and end apart: 13, of which 2 were waited for; matrix products, arithmetic and copies ran while one was open for 4% of the time, Pallas kernels for 38%

profile of v2, /device:TPU:1, one launch (start us, length us, event | category | flops | bytes accessed | tf_op | source)
XLA Modules:
  0.0 126.2 jit_solution(15954349992573156042)
XLA Ops:
  0.7 0.1 stack.59.info
  0.8 1.1 copy-done.2
  1.9 1.6 %prep_kv.1 = (bf16[4,2,160,128]{3,2,1,0:T(8,128)(2,1)S(1)}, bf16[4,2,160,128]{3,2,1,0:T(8,128)(2,1)S(1)}, bf16[8,160,256]{2,1,0:T(8,128)(2,1)}) custom-call(s32[6]{0:T(128)S(1)} %stack.59.info, bf16[2,160,1024]{2,1,0:T(8,128)(2,1)S(1)} %copy-done.2), custom_call_target="tpu_custom_call" | custom-call | tf_op jit(solution)/shard_map/prep_kv/pallas_call | solution.py:58
  3.5 1.4 %collective-permute-start = (bf16[4,2,160,128]{3,2,1,0:T(8,128)(2,1)S(1)}, bf16[4,2,160,128]{3,2,1,0:T(8,128)(2,1)S(1)}, u32[]{:S(2)}, u32[]{:S(2)}) collective-permute-start(bf16[4,2,160,128]{3,2,1,0:T(8,128)(2,1)S(1)} %get-tuple-element.49), channel_id=1, source_target_pairs={{0,1},{1,0},{2,3},{3,2},{4,5},{5,4},{6,7},{7,6},{8,9},{9,8},{10,11... | collective-permute-start | bytes 983048 | tf_op jit(solution)/shard_map/ppermute | solution.py:573
  4.9 0.9 copy.29
  5.8 0.1 dynamic-slice_reduce_fusion
  6.0 1.2 reshape.113
  7.2 0.1 copy.20
  7.3 1.7 %copy-done.1 = bf16[160,8192]{1,0:T(8,128)(2,1)S(1)} copy-done((bf16[160,8192]{1,0:T(8,128)(2,1)S(1)}, bf16[160,8192]{1,0:T(8,128)(2,1)}, u32[]{:S(2)}) %copy-start.1) | copy-done | bytes 2621464
  9.0 0.9 other_half.1
  9.9 0.2 convert_reduce_fusion
  10.2 0.1 collective-permute-start.4
  10.3 0.1 and_reduce_fusion
  10.5 0.2 fusion
  10.6 5.3 %collective-permute-start.3 = (bf16[2,4,2,160,128]{4,3,2,1,0:T(8,128)(2,1)S(1)}, bf16[2,4,2,160,128]{4,3,2,1,0:T(8,128)(2,1)}, u32[]{:S(2)}, u32[]{:S(2)}) collective-permute-start(bf16[2,4,2,160,128]{4,3,2,1,0:T(8,128)(2,1)S(1)} %pad_maximum_fusion.refs_0_), channel_id=1, source_target_pairs={{0,12},{1,13},{2,14},{3,15},{16,28},{17,29},{18,30},{19,31},{32,44... | collective-permute-start | bytes 1966088 | tf_op jit(solution)/shard_map/ppermute | solution.py:573
  15.9 1.3 %collective-permute-start.2 = (bf16[2,4,2,160,128]{4,3,2,1,0:T(8,128)(2,1)S(1)}, bf16[2,4,2,160,128]{4,3,2,1,0:T(8,128)(2,1)}, u32[]{:S(2)}, u32[]{:S(2)}) collective-permute-start(bf16[2,4,2,160,128]{4,3,2,1,0:T(8,128)(2,1)S(1)} %pad_maximum_fusion.refs_0_), channel_id=1, source_target_pairs={{0,2},{1,3},{2,0},{3,1},{4,6},{5,7},{6,4},{7,5},{8,10},{9,11},{10,... | collective-permute-start | bytes 1966088 | tf_op jit(solution)/shard_map/ppermute | solution.py:573
  17.2 2.1 %collective-permute-start.1 = (bf16[2,4,2,160,128]{4,3,2,1,0:T(8,128)(2,1)S(1)}, bf16[2,4,2,160,128]{4,3,2,1,0:T(8,128)(2,1)}, u32[]{:S(2)}, u32[]{:S(2)}) collective-permute-start(bf16[2,4,2,160,128]{4,3,2,1,0:T(8,128)(2,1)S(1)} %pad_maximum_fusion.refs_0_), channel_id=1, source_target_pairs={{0,4},{1,5},{2,6},{3,7},{4,8},{5,9},{6,10},{7,11},{8,12},{9,13},{1... | collective-permute-start | bytes 1966088 | tf_op jit(solution)/shard_map/ppermute | solution.py:573
  19.4 8.7 %partials.1 = bf16[16,6,16,128]{3,2,1,0:T(8,128)(2,1)} custom-call(s32[6]{0:T(128)S(1)} %stack.59.info, s32[4]{0:T(128)S(1)} %copy-done.5, bf16[4,8,32,128]{3,2,1,0:T(8,128)(2,1)S(1)} %bitcast.28, bf16[1,8,32,128]{3,2,1,0:T(8,128)(2,1)S(1)} %bitcast.30, bf16[2,4,512,1024]{3,2,1,0:T(8,128)(2,1)} %cache.1, bf16[2,4,16,1024]{3,2,1,0:T(8,128)(2,1)S(1)} %pad.9.tail_ref, ...), custom_call_target="tpu_custom_call" | custom-call | flops 2684354560 | bytes 8388608 | tf_op jit(solution)/shard_map/partials/pallas_call | solution.py:436
  28.1 4.4 %all-to-all-start = ((bf16[16,6,16,128]{3,2,1,0:T(8,128)(2,1)}), bf16[16,6,16,128]{3,2,1,0:T(8,128)(2,1)S(1)}, u32[]{:S(2)}, u32[]{:S(2)}) async-start(bf16[16,6,16,128]{3,2,1,0:T(8,128)(2,1)} %partials.1), calls=%async_computation | async-start | bytes 786432 | tf_op jit(solution)/shard_map/all_to_all | solution.py:618
  32.6 0.1 copy.23
  32.6 0.1 reshape.125
  32.7 0.1 copy.22
  32.8 0.1 reshape.117
  32.9 0.1 pad_add_fusion.table
  33.0 8.1 %all-to-all-done.x_ref = bf16[16,6,16,128]{3,2,1,0:T(8,128)(2,1)S(1)} async-done(((bf16[16,6,16,128]{3,2,1,0:T(8,128)(2,1)}), bf16[16,6,16,128]{3,2,1,0:T(8,128)(2,1)S(1)}, u32[]{:S(2)}, u32[]{:S(2)}) %all-to-all-start) | async-done | bytes 393248 | tf_op jit(solution)/shard_map/all_to_all | solution.py:618
  41.1 0.7 copy-done.12
  41.9 7.4 %all-to-all-start.1 = ((bf16[8,160,256]{2,1,0:T(8,128)(2,1)}), bf16[8,160,256]{2,1,0:T(8,128)(2,1)S(1)}, u32[]{:S(2)}, u32[]{:S(2)}) async-start(bf16[8,160,256]{2,1,0:T(8,128)(2,1)} %get-tuple-element.55), calls=%async_computation.1 | async-start | bytes 1310720 | tf_op jit(solution)/shard_map/all_to_all | solution.py:608
  49.3 0.7 collective-permute-start.6
  50.0 1.5 %collective-permute-start.5 = (bf16[2,4,2,160,128]{4,3,2,1,0:T(8,128)(2,1)}, bf16[2,4,2,160,128]{4,3,2,1,0:T(8,128)(2,1)}, u32[]{:S(2)}, u32[]{:S(2)}) collective-permute-start(bf16[2,4,2,160,128]{4,3,2,1,0:T(8,128)(2,1)} %collective-permute-done.1.refs_1_), channel_id=1, source_target_pairs={{4,8},{5,9},{6,10},{7,11},{8,12},{9,13},{10,14},{11,15},{20,24},{2... | collective-permute-start | bytes 1966088 | tf_op jit(solution)/shard_map/ppermute | solution.py:573
  51.5 4.3 %collective-permute-start.7 = (bf16[2,4,2,160,128]{4,3,2,1,0:T(8,128)(2,1)}, bf16[2,4,2,160,128]{4,3,2,1,0:T(8,128)(2,1)}, u32[]{:S(2)}, u32[]{:S(2)}) collective-permute-start(bf16[2,4,2,160,128]{4,3,2,1,0:T(8,128)(2,1)} %collective-permute-done.2.refs_2_), channel_id=1, source_target_pairs={{0,12},{1,13},{2,14},{3,15},{16,28},{17,29},{18,30},{19,31},{32,44... | collective-permute-start | bytes 1966088 | tf_op jit(solution)/shard_map/ppermute | solution.py:573
  55.8 18.3 %prefill.3 = (f32[4,5,128,256]{3,2,1,0:T(8,128)}, f32[4,5,8,256]{3,2,1,0:T(8,128)S(1)}, f32[4,5,128,256]{3,2,1,0:T(8,128)}, f32[4,5,8,256]{3,2,1,0:T(8,128)S(1)}) custom-call(s32[6]{0:T(128)S(1)} %stack.59.info, s32[2,5,256]{2,1,0:T(8,128)S(1)} %broadcast_add_fusion.pos_ref, bf16[160,8192]{1,0:T(8,128)(2,1)} %qa_ref.5, ...), custom_call_target="tpu_custom_call" | custom-call | flops 13421772800 | bytes 15728640 | tf_op jit(solution)/shard_map/prefill/pallas_call | solution.py:300
  74.1 0.7 copy-done.8
  74.7 0.7 copy-done.10
  75.4 1.9 %merge.1 = (bf16[4,16,128]{2,1,0:T(8,128)(2,1)}, bf16[16,128]{1,0:T(8,128)(2,1)}) custom-call(bf16[16,6,16,128]{3,2,1,0:T(8,128)(2,1)} %copy-done.12), custom_call_target="tpu_custom_call" | custom-call | tf_op jit(solution)/shard_map/merge/pallas_call | solution.py:485
  77.4 0.7 copy-done.4
  78.0 1.8 %select.16 = bf16[8,2,176,256]{3,2,1,0:T(8,128)(2,1)} custom-call(s32[33]{0:T(128)S(1)} %pad_add_fusion.table, bf16[8,160,256]{2,1,0:T(8,128)(2,1)S(1)} %all-to-all-done.1.x_ref, bf16[16,128]{1,0:T(8,128)(2,1)S(1)} %copy-done.4), custom_call_target="tpu_custom_call" | custom-call | tf_op jit(solution)/shard_map/select/pallas_call | solution.py:515
  79.9 7.4 %all-to-all-start.2 = ((bf16[8,2,176,256]{3,2,1,0:T(8,128)(2,1)}), bf16[8,2,176,256]{3,2,1,0:T(8,128)(2,1)S(1)}, u32[]{:S(2)}, u32[]{:S(2)}) async-start(bf16[8,2,176,256]{3,2,1,0:T(8,128)(2,1)} %select.16), calls=%async_computation.2 | async-start | bytes 2883584 | tf_op jit(solution)/shard_map/all_to_all | solution.py:636
  87.2 0.9 collective-permute-start.8
  88.1 16.2 %prefill.4 = (f32[4,5,128,256]{3,2,1,0:T(8,128)}, f32[4,5,8,256]{3,2,1,0:T(8,128)S(1)}, f32[4,5,128,256]{3,2,1,0:T(8,128)}, f32[4,5,8,256]{3,2,1,0:T(8,128)S(1)}) custom-call(s32[6]{0:T(128)S(1)} %stack.59.info, s32[2,5,256]{2,1,0:T(8,128)S(1)} %broadcast_add_fusion.pos_ref, bf16[160,8192]{1,0:T(8,128)(2,1)} %qa_ref.5, ...), custom_call_target="tpu_custom_call" | custom-call | flops 10066329600 | bytes 15728640 | tf_op jit(solution)/shard_map/prefill/pallas_call | solution.py:300
  104.4 0.7 copy-done.6
  105.1 1.8 %all-to-all-done.2.x_ref = bf16[8,2,176,256]{3,2,1,0:T(8,128)(2,1)S(1)} async-done(((bf16[8,2,176,256]{3,2,1,0:T(8,128)(2,1)}), bf16[8,2,176,256]{3,2,1,0:T(8,128)(2,1)S(1)}, u32[]{:S(2)}, u32[]{:S(2)}) %all-to-all-start.2) | async-done | bytes 1441824 | tf_op jit(solution)/shard_map/all_to_all | solution.py:636
  106.9 0.9 copy-done.7
  107.8 10.0 %prefill.5 = (bf16[160,8192]{1,0:T(8,128)(2,1)}, bf16[160,4096]{1,0:T(8,128)(2,1)}) custom-call(s32[6]{0:T(128)S(1)} %stack.59.info, s32[2,5,256]{2,1,0:T(8,128)S(1)} %broadcast_add_fusion.pos_ref, bf16[160,8192]{1,0:T(8,128)(2,1)} %qa_ref.5, bf16[160,4096]{1,0:T(8,128)(2,1)} %collective-permute-done.4.qb_ref, ...), custom_call_target="tpu_custom_call" | custom-call | flops 3355443200 | bytes 15728640 | tf_op jit(solution)/shard_map/prefill/pallas_call | solution.py:300
  117.7 2.8 %collective-permute-start.9 = (bf16[160,4096]{1,0:T(8,128)(2,1)}, bf16[160,4096]{1,0:T(8,128)(2,1)S(1)}, u32[]{:S(2)}, u32[]{:S(2)}) collective-permute-start(bf16[160,4096]{1,0:T(8,128)(2,1)} %get-tuple-element.87), channel_id=1, source_target_pairs={{0,1},{1,0},{2,3},{3,2},{4,5},{5,4},{6,7},{7,6},{8,9},{9,8},{10,11... | collective-permute-start | bytes 3932168 | tf_op jit(solution)/shard_map/ppermute | solution.py:573
  120.5 0.6 copy.25
  121.1 1.7 %settle.1 = (bf16[2,2,160,1024]{3,2,1,0:T(8,128)(2,1)}, bf16[2,16,128]{2,1,0:T(8,128)(2,1)S(1)}) custom-call(s32[33]{0:T(128)S(1)} %pad_add_fusion.table, bf16[8,2,176,256]{3,2,1,0:T(8,128)(2,1)S(1)} %all-to-all-done.2.x_ref), custom_call_target="tpu_custom_call" | custom-call | tf_op jit(solution)/shard_map/settle/pallas_call | solution.py:544
  122.9 0.6 copy.30
  123.5 2.7 %place.1 = bf16[160,8192]{1,0:T(8,128)(2,1)} custom-call(s32[6]{0:T(128)S(1)} %stack.59.info, bf16[160,8192]{1,0:T(8,128)(2,1)} %get-tuple-element.86.kept_ref, bf16[160,4096]{1,0:T(8,128)(2,1)S(1)} %collective-permute-done.9.x_ref), custom_call_target="tpu_custom_call", output_to_operand_aliasing={{}: (1, {})} | custom-call | tf_op jit(solution)/shard_map/place/pallas_call | solution.py:105
  (45 shorter events, 0.4 us)
Async XLA Ops:
  0.6 5.1 %copy-start = (bf16[8,8192]{1,0:T(8,128)(2,1)S(1)}, bf16[8,8192]{1,0:T(8,128)(2,1)}, u32[]{:S(2)}) copy-start(bf16[8,8192]{1,0:T(8,128)(2,1)} %param.11) | copy-start | bytes 393220
  0.8 1.1 copy-start.2
  3.5 6.7 %collective-permute-start = (bf16[4,2,160,128]{3,2,1,0:T(8,128)(2,1)S(1)}, bf16[4,2,160,128]{3,2,1,0:T(8,128)(2,1)S(1)}, u32[]{:S(2)}, u32[]{:S(2)}) collective-permute-start(bf16[4,2,160,128]{3,2,1,0:T(8,128)(2,1)S(1)} %get-tuple-element.49), channel_id=1, source_target_pairs={{0,1},{1,0},{2,3},{3,2},{4,5},{5,4},{6,7},{7,6},{8,9},{9,8},{10,11... | collective-permute-start | bytes 983048 | tf_op jit(solution)/shard_map/ppermute | solution.py:573
  5.9 4.0 %copy-start.15 = (s32[8]{0:T(128)S(1)}, s32[8]{0:T(128)}, u32[]{:S(2)}) copy-start(s32[8]{0:T(128)} %param.12) | copy-start | bytes 100
  7.3 1.7 %copy-start.1 = (bf16[160,8192]{1,0:T(8,128)(2,1)S(1)}, bf16[160,8192]{1,0:T(8,128)(2,1)}, u32[]{:S(2)}) copy-start(bf16[160,8192]{1,0:T(8,128)(2,1)} %qa_ref.5) | copy-start | bytes 7864324
  9.0 10.3 %copy-start.3 = (bf16[2,160,1024]{2,1,0:T(8,128)(2,1)S(1)}, bf16[2,160,1024]{2,1,0:T(8,128)(2,1)}, u32[]{:S(2)}) copy-start(bf16[2,160,1024]{2,1,0:T(8,128)(2,1)} %pre_ref.1) | copy-start | bytes 1966084
  9.0 10.3 %copy-start.5 = (s32[4]{0:T(128)S(1)}, s32[4]{0:T(128)}, u32[]{:S(2)}) copy-start(s32[4]{0:T(128)} %lens.1) | copy-start | bytes 52
  10.2 39.1 %collective-permute-start.4 = (bf16[160,4096]{1,0:T(8,128)(2,1)S(1)}, bf16[160,4096]{1,0:T(8,128)(2,1)}, u32[]{:S(2)}, u32[]{:S(2)}) collective-permute-start(bf16[160,4096]{1,0:T(8,128)(2,1)S(1)} %other_half.1), channel_id=1, source_target_pairs={{0,1},{1,0},{2,3},{3,2},{4,5},{5,4},{6,7},{7,6},{8,9},{9,8},{10,11... | collective-permute-start | bytes 3932168 | tf_op jit(solution)/shard_map/ppermute | solution.py:573
  10.6 38.6 %collective-permute-start.3 = (bf16[2,4,2,160,128]{4,3,2,1,0:T(8,128)(2,1)S(1)}, bf16[2,4,2,160,128]{4,3,2,1,0:T(8,128)(2,1)}, u32[]{:S(2)}, u32[]{:S(2)}) collective-permute-start(bf16[2,4,2,160,128]{4,3,2,1,0:T(8,128)(2,1)S(1)} %pad_maximum_fusion.refs_0_), channel_id=1, source_target_pairs={{0,12},{1,13},{2,14},{3,15},{16,28},{17,29},{18,30},{19,31},{32,44... | collective-permute-start | bytes 1966088 | tf_op jit(solution)/shard_map/ppermute | solution.py:573
  15.9 33.3 %collective-permute-start.2 = (bf16[2,4,2,160,128]{4,3,2,1,0:T(8,128)(2,1)S(1)}, bf16[2,4,2,160,128]{4,3,2,1,0:T(8,128)(2,1)}, u32[]{:S(2)}, u32[]{:S(2)}) collective-permute-start(bf16[2,4,2,160,128]{4,3,2,1,0:T(8,128)(2,1)S(1)} %pad_maximum_fusion.refs_0_), channel_id=1, source_target_pairs={{0,2},{1,3},{2,0},{3,1},{4,6},{5,7},{6,4},{7,5},{8,10},{9,11},{10,... | collective-permute-start | bytes 1966088 | tf_op jit(solution)/shard_map/ppermute | solution.py:573
  17.2 32.0 %collective-permute-start.1 = (bf16[2,4,2,160,128]{4,3,2,1,0:T(8,128)(2,1)S(1)}, bf16[2,4,2,160,128]{4,3,2,1,0:T(8,128)(2,1)}, u32[]{:S(2)}, u32[]{:S(2)}) collective-permute-start(bf16[2,4,2,160,128]{4,3,2,1,0:T(8,128)(2,1)S(1)} %pad_maximum_fusion.refs_0_), channel_id=1, source_target_pairs={{0,4},{1,5},{2,6},{3,7},{4,8},{5,9},{6,10},{7,11},{8,12},{9,13},{1... | collective-permute-start | bytes 1966088 | tf_op jit(solution)/shard_map/ppermute | solution.py:573
  19.4 13.6 %copy-start.14 = (s32[5,256]{1,0:T(8,128)S(1)}, s32[5,256]{1,0:T(8,128)}, u32[]{:S(2)}) copy-start(s32[5,256]{1,0:T(8,128)} %constant.79) | copy-start | bytes 15364
  28.1 13.0 %all-to-all-start = ((bf16[16,6,16,128]{3,2,1,0:T(8,128)(2,1)}), bf16[16,6,16,128]{3,2,1,0:T(8,128)(2,1)S(1)}, u32[]{:S(2)}, u32[]{:S(2)}) async-start(bf16[16,6,16,128]{3,2,1,0:T(8,128)(2,1)} %partials.1), calls=%async_computation | async-start | bytes 786432 | tf_op jit(solution)/shard_map/all_to_all | solution.py:618
  41.1 0.8 copy-start.12
  41.9 35.5 %all-to-all-start.1 = ((bf16[8,160,256]{2,1,0:T(8,128)(2,1)}), bf16[8,160,256]{2,1,0:T(8,128)(2,1)S(1)}, u32[]{:S(2)}, u32[]{:S(2)}) async-start(bf16[8,160,256]{2,1,0:T(8,128)(2,1)} %get-tuple-element.55), calls=%async_computation.1 | async-start | bytes 1310720 | tf_op jit(solution)/shard_map/all_to_all | solution.py:608
  49.3 28.1 %collective-permute-start.6 = (bf16[2,4,2,160,128]{4,3,2,1,0:T(8,128)(2,1)}, bf16[2,4,2,160,128]{4,3,2,1,0:T(8,128)(2,1)S(1)}, u32[]{:S(2)}, u32[]{:S(2)}) collective-permute-start(bf16[2,4,2,160,128]{4,3,2,1,0:T(8,128)(2,1)} %collective-permute-done.1.refs_1_), channel_id=1, source_target_pairs={{4,6},{5,7},{6,4},{7,5},{8,10},{9,11},{10,8},{11,9},{12,14},{13,15... | collective-permute-start | bytes 1966088 | tf_op jit(solution)/shard_map/ppermute | solution.py:573
  50.0 27.4 %collective-permute-start.5 = (bf16[2,4,2,160,128]{4,3,2,1,0:T(8,128)(2,1)}, bf16[2,4,2,160,128]{4,3,2,1,0:T(8,128)(2,1)}, u32[]{:S(2)}, u32[]{:S(2)}) collective-permute-start(bf16[2,4,2,160,128]{4,3,2,1,0:T(8,128)(2,1)} %collective-permute-done.1.refs_1_), channel_id=1, source_target_pairs={{4,8},{5,9},{6,10},{7,11},{8,12},{9,13},{10,14},{11,15},{20,24},{2... | collective-permute-start | bytes 1966088 | tf_op jit(solution)/shard_map/ppermute | solution.py:573
  51.5 25.8 %collective-permute-start.7 = (bf16[2,4,2,160,128]{4,3,2,1,0:T(8,128)(2,1)}, bf16[2,4,2,160,128]{4,3,2,1,0:T(8,128)(2,1)}, u32[]{:S(2)}, u32[]{:S(2)}) collective-permute-start(bf16[2,4,2,160,128]{4,3,2,1,0:T(8,128)(2,1)} %collective-permute-done.2.refs_2_), channel_id=1, source_target_pairs={{0,12},{1,13},{2,14},{3,15},{16,28},{17,29},{18,30},{19,31},{32,44... | collective-permute-start | bytes 1966088 | tf_op jit(solution)/shard_map/ppermute | solution.py:573
  74.1 0.7 copy-start.8
  74.7 0.7 copy-start.10
  77.4 0.7 copy-start.4
  78.0 10.1 %copy-start.11 = (f32[4,5,8,256]{3,2,1,0:T(8,128)S(1)}, f32[4,5,8,256]{3,2,1,0:T(8,128)}, u32[]{:S(2)}) copy-start(f32[4,5,8,256]{3,2,1,0:T(8,128)} %copy-done.10) | copy-start | bytes 491524
  79.9 8.3 %copy-start.9 = (f32[4,5,8,256]{3,2,1,0:T(8,128)S(1)}, f32[4,5,8,256]{3,2,1,0:T(8,128)}, u32[]{:S(2)}) copy-start(f32[4,5,8,256]{3,2,1,0:T(8,128)} %copy-done.8) | copy-start | bytes 491524
  79.9 27.0 %all-to-all-start.2 = ((bf16[8,2,176,256]{3,2,1,0:T(8,128)(2,1)}), bf16[8,2,176,256]{3,2,1,0:T(8,128)(2,1)S(1)}, u32[]{:S(2)}, u32[]{:S(2)}) async-start(bf16[8,2,176,256]{3,2,1,0:T(8,128)(2,1)} %select.16), calls=%async_computation.2 | async-start | bytes 2883584 | tf_op jit(solution)/shard_map/all_to_all | solution.py:636
  87.2 17.8 %collective-permute-start.8 = (bf16[2,4,2,160,128]{4,3,2,1,0:T(8,128)(2,1)S(1)}, bf16[2,4,2,160,128]{4,3,2,1,0:T(8,128)(2,1)S(1)}, u32[]{:S(2)}, u32[]{:S(2)}) collective-permute-start(bf16[2,4,2,160,128]{4,3,2,1,0:T(8,128)(2,1)S(1)} %collective-permute-done.6.refs_1_), channel_id=1, source_target_pairs={{4,8},{5,9},{6,10},{7,11},{8,12},{9,13},{10,14},{11,15},{20,24},{2... | collective-permute-start | bytes 1966088 | tf_op jit(solution)/shard_map/ppermute | solution.py:573
  104.4 0.7 copy-start.6
  106.9 0.9 copy-start.7
  107.8 12.7 %copy-start.13 = (bf16[4,16,128]{2,1,0:T(8,128)(2,1)S(1)}, bf16[4,16,128]{2,1,0:T(8,128)(2,1)}, u32[]{:S(2)}) copy-start(bf16[4,16,128]{2,1,0:T(8,128)(2,1)} %get-tuple-element.90) | copy-start | bytes 49156
  117.7 5.7 %collective-permute-start.9 = (bf16[160,4096]{1,0:T(8,128)(2,1)}, bf16[160,4096]{1,0:T(8,128)(2,1)S(1)}, u32[]{:S(2)}, u32[]{:S(2)}) collective-permute-start(bf16[160,4096]{1,0:T(8,128)(2,1)} %get-tuple-element.87), channel_id=1, source_target_pairs={{0,1},{1,0},{2,3},{3,2},{4,5},{5,4},{6,7},{7,6},{8,9},{9,8},{10,11... | collective-permute-start | bytes 3932168 | tf_op jit(solution)/shard_map/ppermute | solution.py:573

commit v3 on v2

--- a/solution.py
+++ b/solution.py
@@ -200,14 +200,14 @@
             yield
         total = jnp.sum(total, axis=0, keepdims=True)
         if not first:
-            acc = acc + acc_in[0, n] * shrink
+            acc = acc + acc_in[0, n].astype(jnp.float32) * shrink
             total = total + stat_in[0, n, 1:2, :] * shrink
         if last:
             stage = refs[6]
             stage[side, n * COLS : (n + 1) * COLS, :] = (acc * (1.0 / total)).T.astype(jnp.bfloat16)
         else:
             acc_out, stat_out = outs[side]
-            acc_out[0, n] = acc
+            acc_out[0, n] = acc.astype(jnp.bfloat16)
             line = lax.broadcasted_iota(jnp.int32, (8, COLS), 0)
             stat_out[0, n] = jnp.where(line == 0, peak, total)
 
@@ -219,15 +219,13 @@
                     live.remove(step)
 
     def both(scored, finished, slot):
-        steps = []
         if scored == 0:
             load()
         for n in range(blocks):
-            if scored is not None:
-                steps.append(scores(scored, n))
+            steps = [] if scored is None else [scores(scored, n)]
             if finished is not None:
                 steps.append(finish(finished, n, slot))
-        drain(steps)
+            drain(steps)
         if last and finished is not None:
             stage = refs[6]
             for h in range(REP):
@@ -293,7 +291,7 @@
         scratch.append(pltpu.VMEM((2, rows, HD), jnp.bfloat16))
     else:
         out_shape = [
-            jax.ShapeDtypeStruct((HALF, blocks, HD, COLS), jnp.float32),
+            jax.ShapeDtypeStruct((HALF, blocks, HD, COLS), jnp.bfloat16),
             jax.ShapeDtypeStruct((HALF, blocks, 8, COLS), jnp.float32),
         ] * 2
         out_specs = carry_specs
@@ -608,7 +606,7 @@
     pieces = lax.all_to_all(pieces, "pool", 0, 0)
     q_send = other_half(info, pre_q)
     own = jnp.stack([kv_own, kv_swapped])
-    own, q_send, info_decode = lax.optimization_barrier((own, q_send, info))
+    own, q_send, pieces, info_decode = lax.optimization_barrier((own, q_send, pieces, info))
 
     a1 = permute(own, forward)
     b0 = permute(own, across)

time: 127 us -> 131 us (1.031)
  local copies, waits for them, and re-layouts: 11.2 us -> 20.1 us
  Pallas kernels: 63.9 us -> 58.4 us
  starting transfers between devices: 39.5 us -> 36.1 us
  waiting for transfers between devices: 9.89 us -> 13 us
    unnamed x35 -> x57, local copies, waits for them, and re-layouts: 8.66 us -> 14.5 us
    pallas_call x3, Pallas kernels: 44.5 us -> 39.9 us  [prefill(): pl.pallas_call(functools.partial(prefill_kernel, kinds=kinds, first=first...]
    all_to_all x1, starting transfers between devices: 7.37 us -> 3.58 us  [body(): landed = lax.all_to_all(select(table, pieces, arrived), 'pool', 0, 0)]
    all_to_all x1, waiting for transfers between devices: 0.01 us -> 2.94 us  [body(): pieces = lax.all_to_all(pieces, 'pool', 0, 0)]
    reshape x2, local copies, waits for them, and re-layouts: 1.33 us -> 3.68 us  [body(): dec_rows = dec_q.reshape(STEPS, requests, KVH, 2, REP // 2, HD)]
    all_to_all x1, starting transfers between devices: 7.37 us -> 8.76 us  [body(): pieces = lax.all_to_all(pieces, 'pool', 0, 0)]
  transfers between devices with their start and end apart: 13 -> 13, of which waited for: 2 -> 3; matrix products, arithmetic and copies ran while one was open for 4% -> 6% of each run, Pallas kernels for 38% -> 34%
where the time goes in v3:
time: 131 us; the launch traced here: 130 us
  Pallas kernels  58.4 us (45%)
  starting transfers between devices  36.1 us (28%)
  local copies, waits for them, and re-layouts  20.1 us (15%)
  waiting for transfers between devices  13 us (10%)
  other arithmetic  1.86 us (1%)
    pallas_call x3, Pallas kernels, prefill(): pl.pallas_call(functools.partial(prefill_kernel, kinds=kinds, first=first...  39.9 us
    ppermute x10, starting transfers between devices, permute(): return lax.ppermute(a, 'tp', pairs)  19.8 us
    unnamed x57, local copies, waits for them, and re-layouts  14.5 us
    all_to_all x1, starting transfers between devices, body(): pieces = lax.all_to_all(pieces, 'pool', 0, 0)  8.76 us
    pallas_call x1, Pallas kernels, partials(): pl.pallas_call(partial_kernel, out_shape=jax.ShapeDtypeStruct((TP, reques...  8.71 us
    all_to_all x1, waiting for transfers between devices, body(): part = lax.all_to_all(part, 'tp', 0, 0)  8.07 us
    all_to_all x1, starting transfers between devices, body(): part = lax.all_to_all(part, 'tp', 0, 0)  3.92 us
    reshape x2, local copies, waits for them, and re-layouts, body(): dec_rows = dec_q.reshape(STEPS, requests, KVH, 2, REP // 2, HD)  3.68 us
  transfers between devices with their start and end apart: 13, of which 3 were waited for; matrix products, arithmetic and copies ran while one was open for 6% of the time, Pallas kernels for 34%

profile of v3, /device:TPU:1, one launch (start us, length us, event | category | flops | bytes accessed | tf_op | source)
XLA Modules:
  0.0 130.3 jit_solution(7477780509663295467)
XLA Ops:
  0.8 1.1 copy-done.2
  1.9 0.8 prep_kv.1
  2.7 0.8 copy-done.7
  3.5 0.7 copy-done.8
  4.2 0.7 copy-done.16
  4.9 8.8 %all-to-all-start = ((bf16[8,160,256]{2,1,0:T(8,128)(2,1)}), bf16[8,160,256]{2,1,0:T(8,128)(2,1)S(1)}, u32[]{:S(2)}, u32[]{:S(2)}) async-start(bf16[8,160,256]{2,1,0:T(8,128)(2,1)} %copy-done.7), calls=%async_computation | async-start | bytes 1310720 | tf_op jit(solution)/shard_map/all_to_all | solution.py:606
  13.7 0.9 collective-permute-start
  14.8 0.7 pad.9.tail_ref
  15.6 1.9 %reshape.113 = bf16[4,4,8,2,4,128]{5,4,3,2,1,0:T(4,128)(2,1)} reshape(bf16[4,4,8192]{2,1,0:T(4,128)(2,1)} %param.15) | data formatting | bytes 524288 | tf_op jit(solution)/shard_map/reshape | solution.py:596
  17.5 1.7 %copy.20 = bf16[4,4,8,2,4,128]{5,4,0,3,2,1:T(4,128)(2,1)} copy(bf16[4,4,8,2,4,128]{5,4,3,2,1,0:T(4,128)(2,1)} %reshape.113) | data formatting | bytes 524288 | tf_op jit(solution)/shard_map/reshape | solution.py:596
  19.3 0.9 other_half.1
  20.2 1.0 copy-done.4
  21.2 0.2 convert_reduce_fusion
  21.4 1.1 pad_maximum_fusion.refs_0_
  22.6 2.9 %all-to-all-done.x_ref = bf16[8,160,256]{2,1,0:T(8,128)(2,1)S(1)} async-done(((bf16[8,160,256]{2,1,0:T(8,128)(2,1)}), bf16[8,160,256]{2,1,0:T(8,128)(2,1)S(1)}, u32[]{:S(2)}, u32[]{:S(2)}) %all-to-all-start) | async-done | bytes 655392 | tf_op jit(solution)/shard_map/all_to_all | solution.py:606
  25.5 2.1 %collective-permute-start.4 = (bf16[160,4096]{1,0:T(8,128)(2,1)}, bf16[160,4096]{1,0:T(8,128)(2,1)}, u32[]{:S(2)}, u32[]{:S(2)}) collective-permute-start(bf16[160,4096]{1,0:T(8,128)(2,1)} %copy-done.4), channel_id=1, source_target_pairs={{0,1},{1,0},{2,3},{3,2},{4,5},{5,4},{6,7},{7,6},{8,9},{9,8},{10,11... | collective-permute-start | bytes 3932168 | tf_op jit(solution)/shard_map/ppermute | solution.py:571
  27.8 0.2 fusion
  28.0 5.2 %collective-permute-start.3 = (bf16[2,4,2,160,128]{4,3,2,1,0:T(8,128)(2,1)S(1)}, bf16[2,4,2,160,128]{4,3,2,1,0:T(8,128)(2,1)}, u32[]{:S(2)}, u32[]{:S(2)}) collective-permute-start(bf16[2,4,2,160,128]{4,3,2,1,0:T(8,128)(2,1)S(1)} %pad_maximum_fusion.refs_0_), channel_id=1, source_target_pairs={{0,12},{1,13},{2,14},{3,15},{16,28},{17,29},{18,30},{19,31},{32,44... | collective-permute-start | bytes 1966088 | tf_op jit(solution)/shard_map/ppermute | solution.py:571
  33.2 0.4 collective-permute-start.2
  33.6 2.1 %collective-permute-start.1 = (bf16[2,4,2,160,128]{4,3,2,1,0:T(8,128)(2,1)S(1)}, bf16[2,4,2,160,128]{4,3,2,1,0:T(8,128)(2,1)}, u32[]{:S(2)}, u32[]{:S(2)}) collective-permute-start(bf16[2,4,2,160,128]{4,3,2,1,0:T(8,128)(2,1)S(1)} %pad_maximum_fusion.refs_0_), channel_id=1, source_target_pairs={{0,4},{1,5},{2,6},{3,7},{4,8},{5,9},{6,10},{7,11},{8,12},{9,13},{1... | collective-permute-start | bytes 1966088 | tf_op jit(solution)/shard_map/ppermute | solution.py:571
  35.8 8.7 %partials.1 = bf16[16,6,16,128]{3,2,1,0:T(8,128)(2,1)} custom-call(s32[6]{0:T(128)S(1)} %stack.59.info, s32[4]{0:T(128)S(1)} %copy-done.11, bf16[4,8,32,128]{3,2,1,0:T(8,128)(2,1)S(1)} %bitcast.28, bf16[1,8,32,128]{3,2,1,0:T(8,128)(2,1)S(1)} %bitcast.30, bf16[2,4,512,1024]{3,2,1,0:T(8,128)(2,1)} %cache.1, bf16[2,4,16,1024]{3,2,1,0:T(8,128)(2,1)S(1)} %copy-done.5, ...), custom_call_target="tpu_custom_call" | custom-call | flops 2684354560 | bytes 8388608 | tf_op jit(solution)/shard_map/partials/pallas_call | solution.py:434
  44.5 3.9 %all-to-all-start.1 = ((bf16[16,6,16,128]{3,2,1,0:T(8,128)(2,1)}), bf16[16,6,16,128]{3,2,1,0:T(8,128)(2,1)S(1)}, u32[]{:S(2)}, u32[]{:S(2)}) async-start(bf16[16,6,16,128]{3,2,1,0:T(8,128)(2,1)} %partials.1), calls=%async_computation.1 | async-start | bytes 786432 | tf_op jit(solution)/shard_map/all_to_all | solution.py:616
  48.9 8.1 %all-to-all-done.1.x_ref = bf16[16,6,16,128]{3,2,1,0:T(8,128)(2,1)S(1)} async-done(((bf16[16,6,16,128]{3,2,1,0:T(8,128)(2,1)}), bf16[16,6,16,128]{3,2,1,0:T(8,128)(2,1)S(1)}, u32[]{:S(2)}, u32[]{:S(2)}) %all-to-all-start.1) | async-done | bytes 393248 | tf_op jit(solution)/shard_map/all_to_all | solution.py:616
  57.1 0.7 collective-permute-start.6
  57.8 1.5 %collective-permute-start.5 = (bf16[2,4,2,160,128]{4,3,2,1,0:T(8,128)(2,1)}, bf16[2,4,2,160,128]{4,3,2,1,0:T(8,128)(2,1)}, u32[]{:S(2)}, u32[]{:S(2)}) collective-permute-start(bf16[2,4,2,160,128]{4,3,2,1,0:T(8,128)(2,1)} %collective-permute-done.1.refs_1_), channel_id=1, source_target_pairs={{4,8},{5,9},{6,10},{7,11},{8,12},{9,13},{10,14},{11,15},{20,24},{2... | collective-permute-start | bytes 1966088 | tf_op jit(solution)/shard_map/ppermute | solution.py:571
  59.3 1.9 %merge.1 = (bf16[4,16,128]{2,1,0:T(8,128)(2,1)}, bf16[16,128]{1,0:T(8,128)(2,1)}) custom-call(bf16[16,6,16,128]{3,2,1,0:T(8,128)(2,1)} %copy-done.22), custom_call_target="tpu_custom_call" | custom-call | tf_op jit(solution)/shard_map/merge/pallas_call | solution.py:483
  61.2 4.2 %collective-permute-start.7 = (bf16[2,4,2,160,128]{4,3,2,1,0:T(8,128)(2,1)}, bf16[2,4,2,160,128]{4,3,2,1,0:T(8,128)(2,1)S(1)}, u32[]{:S(2)}, u32[]{:S(2)}) collective-permute-start(bf16[2,4,2,160,128]{4,3,2,1,0:T(8,128)(2,1)} %collective-permute-done.2.refs_2_), channel_id=1, source_target_pairs={{0,12},{1,13},{2,14},{3,15},{16,28},{17,29},{18,30},{19,31},{32,44... | collective-permute-start | bytes 1966088 | tf_op jit(solution)/shard_map/ppermute | solution.py:571
  65.4 16.9 %prefill.3 = (bf16[4,5,128,256]{3,2,1,0:T(8,128)(2,1)S(1)}, f32[4,5,8,256]{3,2,1,0:T(8,128)S(1)}, bf16[4,5,128,256]{3,2,1,0:T(8,128)(2,1)S(1)}, f32[4,5,8,256]{3,2,1,0:T(8,128)S(1)}) custom-call(s32[6]{0:T(128)S(1)} %stack.59.info, s32[2,5,256]{2,1,0:T(8,128)S(1)} %broadcast_add_fusion.pos_ref, bf16[160,8192]{1,0:T(8,128)(2,1)} %qa_ref.5, ...), custom_call_target="tpu_custom_call" | custom-call | flops 13421772800 | bytes 15728640 | tf_op jit(solution)/shard_map/prefill/pallas_call | solution.py:298
  82.3 1.0 copy-done.20
  83.4 1.1 copy-done.21
  84.4 0.8 copy-done.12
  85.3 1.7 %select.16 = bf16[8,2,176,256]{3,2,1,0:T(8,128)(2,1)} custom-call(s32[33]{0:T(128)S(1)} %pad_add_fusion.table, bf16[8,160,256]{2,1,0:T(8,128)(2,1)S(1)} %all-to-all-done.x_ref, bf16[16,128]{1,0:T(8,128)(2,1)S(1)} %copy-done.10), custom_call_target="tpu_custom_call" | custom-call | tf_op jit(solution)/shard_map/select/pallas_call | solution.py:513
  87.0 3.6 %all-to-all-start.2 = ((bf16[8,2,176,256]{3,2,1,0:T(8,128)(2,1)}), bf16[8,2,176,256]{3,2,1,0:T(8,128)(2,1)S(1)}, u32[]{:S(2)}, u32[]{:S(2)}) async-start(bf16[8,2,176,256]{3,2,1,0:T(8,128)(2,1)} %select.16), calls=%async_computation.2 | async-start | bytes 2883584 | tf_op jit(solution)/shard_map/all_to_all | solution.py:634
  90.6 0.9 collective-permute-start.8
  91.5 1.1 copy-done.13
  92.6 13.8 %prefill.4 = (bf16[4,5,128,256]{3,2,1,0:T(8,128)(2,1)S(1)}, f32[4,5,8,256]{3,2,1,0:T(8,128)S(1)}, bf16[4,5,128,256]{3,2,1,0:T(8,128)(2,1)S(1)}, f32[4,5,8,256]{3,2,1,0:T(8,128)S(1)}) custom-call(s32[6]{0:T(128)S(1)} %stack.59.info, s32[2,5,256]{2,1,0:T(8,128)S(1)} %broadcast_add_fusion.pos_ref, bf16[160,8192]{1,0:T(8,128)(2,1)} %qa_ref.5, ...), custom_call_target="tpu_custom_call" | custom-call | flops 10066329600 | bytes 15728640 | tf_op jit(solution)/shard_map/prefill/pallas_call | solution.py:298
  106.4 1.0 copy-done.17
  107.5 1.1 copy-done.19
  108.6 0.8 copy-done.14
  109.4 1.9 %all-to-all-done.2.x_ref = bf16[8,2,176,256]{3,2,1,0:T(8,128)(2,1)S(1)} async-done(((bf16[8,2,176,256]{3,2,1,0:T(8,128)(2,1)}), bf16[8,2,176,256]{3,2,1,0:T(8,128)(2,1)S(1)}, u32[]{:S(2)}, u32[]{:S(2)}) %all-to-all-start.2) | async-done | bytes 1441824 | tf_op jit(solution)/shard_map/all_to_all | solution.py:634
  111.3 1.1 copy-done.15
  112.4 1.3 %copy-done.18 = bf16[4,5,128,256]{3,2,1,0:T(8,128)(2,1)S(1)} copy-done((bf16[4,5,128,256]{3,2,1,0:T(8,128)(2,1)S(1)}, bf16[4,5,128,256]{3,2,1,0:T(8,128)(2,1)}, u32[]{:S(2)}) %copy-start.18) | copy-done | bytes 1310744
  113.7 9.2 %prefill.5 = (bf16[160,8192]{1,0:T(8,128)(2,1)}, bf16[160,4096]{1,0:T(8,128)(2,1)}) custom-call(s32[6]{0:T(128)S(1)} %stack.59.info, s32[2,5,256]{2,1,0:T(8,128)S(1)} %broadcast_add_fusion.pos_ref, bf16[160,8192]{1,0:T(8,128)(2,1)} %qa_ref.5, bf16[160,4096]{1,0:T(8,128)(2,1)} %collective-permute-done.4.qb_ref, bf16[2,4,2,160,128]{4,3,2,1,0:T(8,128)(2,1)S(1)} %copy-done.15, ...), custom_call_target="tpu_custom_call" | custom-call | flops 3355443200 | bytes 15728640 | tf_op jit(solution)/shard_map/prefill/pallas_call | solution.py:298
  123.0 1.6 %collective-permute-start.9 = (bf16[160,4096]{1,0:T(8,128)(2,1)}, bf16[160,4096]{1,0:T(8,128)(2,1)S(1)}, u32[]{:S(2)}, u32[]{:S(2)}) collective-permute-start(bf16[160,4096]{1,0:T(8,128)(2,1)} %get-tuple-element.89), channel_id=1, source_target_pairs={{0,1},{1,0},{2,3},{3,2},{4,5},{5,4},{6,7},{7,6},{8,9},{9,8},{10,11... | collective-permute-start | bytes 3932168 | tf_op jit(solution)/shard_map/ppermute | solution.py:571
  124.6 0.6 copy.25
  125.2 1.7 %settle.1 = (bf16[2,2,160,1024]{3,2,1,0:T(8,128)(2,1)}, bf16[2,16,128]{2,1,0:T(8,128)(2,1)S(1)}) custom-call(s32[33]{0:T(128)S(1)} %pad_add_fusion.table, bf16[8,2,176,256]{3,2,1,0:T(8,128)(2,1)S(1)} %all-to-all-done.2.x_ref), custom_call_target="tpu_custom_call" | custom-call | tf_op jit(solution)/shard_map/settle/pallas_call | solution.py:542
  127.0 0.6 copy.30
  127.6 2.7 %place.1 = bf16[160,8192]{1,0:T(8,128)(2,1)} custom-call(s32[6]{0:T(128)S(1)} %stack.59.info, bf16[160,8192]{1,0:T(8,128)(2,1)} %get-tuple-element.88.kept_ref, bf16[160,4096]{1,0:T(8,128)(2,1)S(1)} %collective-permute-done.9.x_ref), custom_call_target="tpu_custom_call", output_to_operand_aliasing={{}: (1, {})} | custom-call | tf_op jit(solution)/shard_map/place/pallas_call | solution.py:105
  (67 shorter events, 1.1 us)
Async XLA Ops:
  0.6 14.0 %copy-start = (bf16[8,8192]{1,0:T(8,128)(2,1)S(1)}, bf16[8,8192]{1,0:T(8,128)(2,1)}, u32[]{:S(2)}) copy-start(bf16[8,8192]{1,0:T(8,128)(2,1)} %param.11) | copy-start | bytes 393220
  0.6 14.0 %copy-start.23 = (bf16[2,4,4,1024]{3,2,1,0:T(4,128)(2,1)S(1)}, bf16[2,4,4,1024]{3,2,1,0:T(4,128)(2,1)}, u32[]{:S(2)}) copy-start(bf16[2,4,4,1024]{3,2,1,0:T(4,128)(2,1)} %param.16) | copy-start | bytes 196612
  0.8 1.1 copy-start.2
  2.6 0.8 copy-start.7
  3.5 0.7 copy-start.8
  4.2 0.7 copy-start.16
  4.9 14.3 %copy-start.1 = (bf16[160,8192]{1,0:T(8,128)(2,1)S(1)}, bf16[160,8192]{1,0:T(8,128)(2,1)}, u32[]{:S(2)}) copy-start(bf16[160,8192]{1,0:T(8,128)(2,1)} %qa_ref.5) | copy-start | bytes 7864324
  4.9 20.6 %all-to-all-start = ((bf16[8,160,256]{2,1,0:T(8,128)(2,1)}), bf16[8,160,256]{2,1,0:T(8,128)(2,1)S(1)}, u32[]{:S(2)}, u32[]{:S(2)}) async-start(bf16[8,160,256]{2,1,0:T(8,128)(2,1)} %copy-done.7), calls=%async_computation | async-start | bytes 1310720 | tf_op jit(solution)/shard_map/all_to_all | solution.py:606
  13.7 7.7 %collective-permute-start = (bf16[4,2,160,128]{3,2,1,0:T(8,128)(2,1)}, bf16[4,2,160,128]{3,2,1,0:T(8,128)(2,1)}, u32[]{:S(2)}, u32[]{:S(2)}) collective-permute-start(bf16[4,2,160,128]{3,2,1,0:T(8,128)(2,1)} %copy-done.16), channel_id=1, source_target_pairs={{0,1},{1,0},{2,3},{3,2},{4,5},{5,4},{6,7},{7,6},{8,9},{9,8},{10,11... | collective-permute-start | bytes 983048 | tf_op jit(solution)/shard_map/ppermute | solution.py:571
  19.2 2.0 %copy-start.26 = (s32[8]{0:T(128)S(1)}, s32[8]{0:T(128)}, u32[]{:S(2)}) copy-start(s32[8]{0:T(128)} %param.12) | copy-start | bytes 100
  19.3 2.2 %copy-start.9 = (bf16[4,2,160,128]{3,2,1,0:T(8,128)(2,1)S(1)}, bf16[4,2,160,128]{3,2,1,0:T(8,128)(2,1)}, u32[]{:S(2)}) copy-start(bf16[4,2,160,128]{3,2,1,0:T(8,128)(2,1)} %copy-done.8) | copy-start | bytes 983044
  20.1 1.1 copy-start.4
  21.2 14.5 %copy-start.3 = (bf16[2,160,1024]{2,1,0:T(8,128)(2,1)S(1)}, bf16[2,160,1024]{2,1,0:T(8,128)(2,1)}, u32[]{:S(2)}) copy-start(bf16[2,160,1024]{2,1,0:T(8,128)(2,1)} %pre_ref.1) | copy-start | bytes 1966084
  21.2 14.5 %copy-start.5 = (bf16[2,4,16,1024]{3,2,1,0:T(8,128)(2,1)S(1)}, bf16[2,4,16,1024]{3,2,1,0:T(8,128)(2,1)}, u32[]{:S(2)}) copy-start(bf16[2,4,16,1024]{3,2,1,0:T(8,128)(2,1)} %pad.9.tail_ref) | copy-start | bytes 786436
  21.2 14.5 %copy-start.6 = (bf16[4,4,8,2,4,128]{5,4,0,3,2,1:T(4,128)(2,1)S(1)}, bf16[4,4,8,2,4,128]{5,4,0,3,2,1:T(4,128)(2,1)}, u32[]{:S(2)}) copy-start(bf16[4,4,8,2,4,128]{5,4,0,3,2,1:T(4,128)(2,1)} %copy.20) | copy-start | bytes 786436
  21.2 14.5 %copy-start.11 = (s32[4]{0:T(128)S(1)}, s32[4]{0:T(128)}, u32[]{:S(2)}) copy-start(s32[4]{0:T(128)} %lens.1) | copy-start | bytes 52
  25.5 31.5 %collective-permute-start.4 = (bf16[160,4096]{1,0:T(8,128)(2,1)}, bf16[160,4096]{1,0:T(8,128)(2,1)}, u32[]{:S(2)}, u32[]{:S(2)}) collective-permute-start(bf16[160,4096]{1,0:T(8,128)(2,1)} %copy-done.4), channel_id=1, source_target_pairs={{0,1},{1,0},{2,3},{3,2},{4,5},{5,4},{6,7},{7,6},{8,9},{9,8},{10,11... | collective-permute-start | bytes 3932168 | tf_op jit(solution)/shard_map/ppermute | solution.py:571
  28.0 29.1 %collective-permute-start.3 = (bf16[2,4,2,160,128]{4,3,2,1,0:T(8,128)(2,1)S(1)}, bf16[2,4,2,160,128]{4,3,2,1,0:T(8,128)(2,1)}, u32[]{:S(2)}, u32[]{:S(2)}) collective-permute-start(bf16[2,4,2,160,128]{4,3,2,1,0:T(8,128)(2,1)S(1)} %pad_maximum_fusion.refs_0_), channel_id=1, source_target_pairs={{0,12},{1,13},{2,14},{3,15},{16,28},{17,29},{18,30},{19,31},{32,44... | collective-permute-start | bytes 1966088 | tf_op jit(solution)/shard_map/ppermute | solution.py:571
  33.2 23.8 %collective-permute-start.2 = (bf16[2,4,2,160,128]{4,3,2,1,0:T(8,128)(2,1)S(1)}, bf16[2,4,2,160,128]{4,3,2,1,0:T(8,128)(2,1)}, u32[]{:S(2)}, u32[]{:S(2)}) collective-permute-start(bf16[2,4,2,160,128]{4,3,2,1,0:T(8,128)(2,1)S(1)} %pad_maximum_fusion.refs_0_), channel_id=1, source_target_pairs={{0,2},{1,3},{2,0},{3,1},{4,6},{5,7},{6,4},{7,5},{8,10},{9,11},{10,... | collective-permute-start | bytes 1966088 | tf_op jit(solution)/shard_map/ppermute | solution.py:571
  33.6 23.4 %collective-permute-start.1 = (bf16[2,4,2,160,128]{4,3,2,1,0:T(8,128)(2,1)S(1)}, bf16[2,4,2,160,128]{4,3,2,1,0:T(8,128)(2,1)}, u32[]{:S(2)}, u32[]{:S(2)}) collective-permute-start(bf16[2,4,2,160,128]{4,3,2,1,0:T(8,128)(2,1)S(1)} %pad_maximum_fusion.refs_0_), channel_id=1, source_target_pairs={{0,4},{1,5},{2,6},{3,7},{4,8},{5,9},{6,10},{7,11},{8,12},{9,13},{1... | collective-permute-start | bytes 1966088 | tf_op jit(solution)/shard_map/ppermute | solution.py:571
  35.7 13.1 %copy-start.25 = (s32[5,256]{1,0:T(8,128)S(1)}, s32[5,256]{1,0:T(8,128)}, u32[]{:S(2)}) copy-start(s32[5,256]{1,0:T(8,128)} %constant.79) | copy-start | bytes 15364
  44.5 12.6 %all-to-all-start.1 = ((bf16[16,6,16,128]{3,2,1,0:T(8,128)(2,1)}), bf16[16,6,16,128]{3,2,1,0:T(8,128)(2,1)S(1)}, u32[]{:S(2)}, u32[]{:S(2)}) async-start(bf16[16,6,16,128]{3,2,1,0:T(8,128)(2,1)} %partials.1), calls=%async_computation.1 | async-start | bytes 786432 | tf_op jit(solution)/shard_map/all_to_all | solution.py:616
  57.0 2.2 %copy-start.22 = (bf16[16,6,16,128]{3,2,1,0:T(8,128)(2,1)}, bf16[16,6,16,128]{3,2,1,0:T(8,128)(2,1)S(1)}, u32[]{:S(2)}) copy-start(bf16[16,6,16,128]{3,2,1,0:T(8,128)(2,1)S(1)} %all-to-all-done.1.x_ref) | copy-start | bytes 1179652
  57.1 28.2 %collective-permute-start.6 = (bf16[2,4,2,160,128]{4,3,2,1,0:T(8,128)(2,1)}, bf16[2,4,2,160,128]{4,3,2,1,0:T(8,128)(2,1)S(1)}, u32[]{:S(2)}, u32[]{:S(2)}) collective-permute-start(bf16[2,4,2,160,128]{4,3,2,1,0:T(8,128)(2,1)} %collective-permute-done.1.refs_1_), channel_id=1, source_target_pairs={{4,6},{5,7},{6,4},{7,5},{8,10},{9,11},{10,8},{11,9},{12,14},{13,15... | collective-permute-start | bytes 1966088 | tf_op jit(solution)/shard_map/ppermute | solution.py:571
  57.8 27.5 %collective-permute-start.5 = (bf16[2,4,2,160,128]{4,3,2,1,0:T(8,128)(2,1)}, bf16[2,4,2,160,128]{4,3,2,1,0:T(8,128)(2,1)}, u32[]{:S(2)}, u32[]{:S(2)}) collective-permute-start(bf16[2,4,2,160,128]{4,3,2,1,0:T(8,128)(2,1)} %collective-permute-done.1.refs_1_), channel_id=1, source_target_pairs={{4,8},{5,9},{6,10},{7,11},{8,12},{9,13},{10,14},{11,15},{20,24},{2... | collective-permute-start | bytes 1966088 | tf_op jit(solution)/shard_map/ppermute | solution.py:571
  61.2 24.1 %copy-start.10 = (bf16[16,128]{1,0:T(8,128)(2,1)S(1)}, bf16[16,128]{1,0:T(8,128)(2,1)}, u32[]{:S(2)}) copy-start(bf16[16,128]{1,0:T(8,128)(2,1)} %get-tuple-element.81.arr_ref) | copy-start | bytes 12292
  61.2 23.2 %collective-permute-start.7 = (bf16[2,4,2,160,128]{4,3,2,1,0:T(8,128)(2,1)}, bf16[2,4,2,160,128]{4,3,2,1,0:T(8,128)(2,1)S(1)}, u32[]{:S(2)}, u32[]{:S(2)}) collective-permute-start(bf16[2,4,2,160,128]{4,3,2,1,0:T(8,128)(2,1)} %collective-permute-done.2.refs_2_), channel_id=1, source_target_pairs={{0,12},{1,13},{2,14},{3,15},{16,28},{17,29},{18,30},{19,31},{32,44... | collective-permute-start | bytes 1966088 | tf_op jit(solution)/shard_map/ppermute | solution.py:571
  82.3 1.1 copy-start.20
  83.4 1.1 copy-start.21
  84.4 0.8 copy-start.12
  87.0 24.3 %all-to-all-start.2 = ((bf16[8,2,176,256]{3,2,1,0:T(8,128)(2,1)}), bf16[8,2,176,256]{3,2,1,0:T(8,128)(2,1)S(1)}, u32[]{:S(2)}, u32[]{:S(2)}) async-start(bf16[8,2,176,256]{3,2,1,0:T(8,128)(2,1)} %select.16), calls=%async_computation.2 | async-start | bytes 2883584 | tf_op jit(solution)/shard_map/all_to_all | solution.py:634
  90.6 17.9 %collective-permute-start.8 = (bf16[2,4,2,160,128]{4,3,2,1,0:T(8,128)(2,1)S(1)}, bf16[2,4,2,160,128]{4,3,2,1,0:T(8,128)(2,1)S(1)}, u32[]{:S(2)}, u32[]{:S(2)}) collective-permute-start(bf16[2,4,2,160,128]{4,3,2,1,0:T(8,128)(2,1)S(1)} %collective-permute-done.6.refs_1_), channel_id=1, source_target_pairs={{4,8},{5,9},{6,10},{7,11},{8,12},{9,13},{10,14},{11,15},{20,24},{2... | collective-permute-start | bytes 1966088 | tf_op jit(solution)/shard_map/ppermute | solution.py:571
  91.5 1.1 copy-start.13
  106.4 1.1 copy-start.17
  107.5 1.1 copy-start.19
  108.6 0.9 copy-start.14
  111.3 1.1 copy-start.15
  112.4 1.3 %copy-start.18 = (bf16[4,5,128,256]{3,2,1,0:T(8,128)(2,1)S(1)}, bf16[4,5,128,256]{3,2,1,0:T(8,128)(2,1)}, u32[]{:S(2)}) copy-start(bf16[4,5,128,256]{3,2,1,0:T(8,128)(2,1)} %copy-done.17) | copy-start | bytes 3932164
  113.7 10.9 %copy-start.24 = (bf16[4,16,128]{2,1,0:T(8,128)(2,1)S(1)}, bf16[4,16,128]{2,1,0:T(8,128)(2,1)}, u32[]{:S(2)}) copy-start(bf16[4,16,128]{2,1,0:T(8,128)(2,1)} %get-tuple-element.92) | copy-start | bytes 49156
  123.0 4.6 %collective-permute-start.9 = (bf16[160,4096]{1,0:T(8,128)(2,1)}, bf16[160,4096]{1,0:T(8,128)(2,1)S(1)}, u32[]{:S(2)}, u32[]{:S(2)}) collective-permute-start(bf16[160,4096]{1,0:T(8,128)(2,1)} %get-tuple-element.89), channel_id=1, source_target_pairs={{0,1},{1,0},{2,3},{3,2},{4,5},{5,4},{6,7},{7,6},{8,9},{9,8},{10,11... | collective-permute-start | bytes 3932168 | tf_op jit(solution)/shard_map/ppermute | solution.py:571

commit v4 on v3

--- a/solution.py
+++ b/solution.py
@@ -305,7 +305,7 @@
             out_specs=out_specs,
             scratch_shapes=scratch,
         ),
-        compiler_params=params(),
+        compiler_params=params(60 * 1024 * 1024),
         cost_estimate=pl.CostEstimate(
             flops=16 * HALF * rows * keys * HD,
             bytes_accessed=24 * HALF * rows * HD,
@@ -603,17 +603,15 @@
 
     kv_own, kv_send, pieces = prep_kv(info, pre_kv)
     kv_swapped = permute(kv_send, swap)
-    pieces = lax.all_to_all(pieces, "pool", 0, 0)
     q_send = other_half(info, pre_q)
     own = jnp.stack([kv_own, kv_swapped])
-    own, q_send, pieces, info_decode = lax.optimization_barrier((own, q_send, pieces, info))
+    own, q_send, info_decode = lax.optimization_barrier((own, q_send, info))
 
     a1 = permute(own, forward)
     b0 = permute(own, across)
     w1 = permute(own, around)
     q_sib = permute(q_send, swap)
     part = partials(info_decode, lengths, dec_rows, arrival, cache_kv, tail, pre_kv)
-    part = lax.all_to_all(part, "tp", 0, 0)
     part, a1, b0, w1, own, q_sib, info = lax.optimization_barrier(
         (part, a1, b0, w1, own, q_sib, info)
     )
@@ -624,11 +622,14 @@
     a2 = permute(a1, forward[4:])
     b1 = permute(a1, across[4:])
     w2 = permute(b0, around)
+    part = lax.all_to_all(part, "tp", 0, 0)
+    part, pieces, info = lax.optimization_barrier((part, pieces, info))
+    pieces = lax.all_to_all(pieces, "pool", 0, 0)
     carry = take(info, [own, a1, b0, w1], [-1, back1, upper, wrapped], None, False)
+    part, pieces, carry, a2, b1, w2, info = lax.optimization_barrier(
+        (part, pieces, carry, a2, b1, w2, info)
+    )
     decoded, arrived = merge(part)
-    arrived, pieces, carry, a2, b1, w2, info = lax.optimization_barrier(
-        (arrived, pieces, carry, a2, b1, w2, info)
-    )
 
     b2 = permute(b1, forward[4:])
     landed = lax.all_to_all(select(table, pieces, arrived), "pool", 0, 0)

time: 131 us -> 123 us (0.939)
  local copies, waits for them, and re-layouts: 20.1 us -> 8.69 us
  waiting for transfers between devices: 13 us -> 8.07 us
  starting transfers between devices: 36.1 us -> 40.6 us
  Pallas kernels: 58.4 us -> 62.4 us
    unnamed x57 -> x45, local copies, waits for them, and re-layouts: 14.5 us -> 6.16 us
    all_to_all x1, waiting for transfers between devices: 8.07 us -> 0.01 us  [body(): part = lax.all_to_all(part, 'tp', 0, 0)]
    ppermute x10, waiting for transfers between devices: 0.03 us -> 4.72 us  [permute(): return lax.ppermute(a, 'tp', pairs)]
    all_to_all x1, starting transfers between devices: 3.58 us -> 6.65 us  [body(): landed = lax.all_to_all(select(table, pieces, arrived), 'pool', 0, 0)]
    all_to_all x1, waiting for transfers between devices: 2.94 us -> 0.01 us  [body(): pieces = lax.all_to_all(pieces, 'pool', 0, 0)]
    pallas_call x3, Pallas kernels: 39.9 us -> 42.8 us  [prefill(): pl.pallas_call(functools.partial(prefill_kernel, kinds=kinds, first=first...]
    reshape x2, local copies, waits for them, and re-layouts: 3.68 us -> 1.33 us  [body(): dec_rows = dec_q.reshape(STEPS, requests, KVH, 2, REP // 2, HD)]
    ppermute x10, starting transfers between devices: 19.8 us -> 21.6 us  [permute(): return lax.ppermute(a, 'tp', pairs)]
  transfers between devices with their start and end apart: 13 -> 13, of which waited for: 3 -> 4; matrix products, arithmetic and copies ran while one was open for 6% -> 4% of each run, Pallas kernels for 34% -> 36%
where the time goes in v4:
time: 123 us; the launch traced here: 122 us
  Pallas kernels  62.4 us (51%)
  starting transfers between devices  40.6 us (33%)
  local copies, waits for them, and re-layouts  8.69 us (7%)
  waiting for transfers between devices  8.07 us (7%)
  other arithmetic  1.4 us (1%)
    pallas_call x3, Pallas kernels, prefill(): pl.pallas_call(functools.partial(prefill_kernel, kinds=kinds, first=first...  42.8 us
    ppermute x10, starting transfers between devices, permute(): return lax.ppermute(a, 'tp', pairs)  21.6 us
    pallas_call x1, Pallas kernels, partials(): pl.pallas_call(partial_kernel, out_shape=jax.ShapeDtypeStruct((TP, reques...  8.71 us
    all_to_all x1, starting transfers between devices, body(): pieces = lax.all_to_all(pieces, 'pool', 0, 0)  7.38 us
    all_to_all x1, starting transfers between devices, body(): landed = lax.all_to_all(select(table, pieces, arrived), 'pool', 0, 0)  6.65 us
    unnamed x45, local copies, waits for them, and re-layouts  6.16 us
    all_to_all x1, starting transfers between devices, body(): part = lax.all_to_all(part, 'tp', 0, 0)  4.96 us
    ppermute x10, waiting for transfers between devices, permute(): return lax.ppermute(a, 'tp', pairs)  4.72 us
  transfers between devices with their start and end apart: 13, of which 4 were waited for; matrix products, arithmetic and copies ran while one was open for 4% of the time, Pallas kernels for 36%

profile of v4, /device:TPU:1, one launch (start us, length us, event | category | flops | bytes accessed | tf_op | source)
XLA Modules:
  0.0 122.1 jit_solution(16387534894547316641)
XLA Ops:
  0.7 0.1 stack.59.info
  0.8 1.1 copy-done.2
  1.9 1.6 %prep_kv.1 = (bf16[4,2,160,128]{3,2,1,0:T(8,128)(2,1)S(1)}, bf16[4,2,160,128]{3,2,1,0:T(8,128)(2,1)S(1)}, bf16[8,160,256]{2,1,0:T(8,128)(2,1)}) custom-call(s32[6]{0:T(128)S(1)} %stack.59.info, bf16[2,160,1024]{2,1,0:T(8,128)(2,1)S(1)} %copy-done.2), custom_call_target="tpu_custom_call" | custom-call | tf_op jit(solution)/shard_map/prep_kv/pallas_call | solution.py:58
  3.5 1.4 %collective-permute-start = (bf16[4,2,160,128]{3,2,1,0:T(8,128)(2,1)S(1)}, bf16[4,2,160,128]{3,2,1,0:T(8,128)(2,1)S(1)}, u32[]{:S(2)}, u32[]{:S(2)}) collective-permute-start(bf16[4,2,160,128]{3,2,1,0:T(8,128)(2,1)S(1)} %get-tuple-element.52), channel_id=1, source_target_pairs={{0,1},{1,0},{2,3},{3,2},{4,5},{5,4},{6,7},{7,6},{8,9},{9,8},{10,11... | collective-permute-start | bytes 983048 | tf_op jit(solution)/shard_map/ppermute | solution.py:571
  4.9 1.7 %copy-done.1 = bf16[160,8192]{1,0:T(8,128)(2,1)S(1)} copy-done((bf16[160,8192]{1,0:T(8,128)(2,1)S(1)}, bf16[160,8192]{1,0:T(8,128)(2,1)}, u32[]{:S(2)}) %copy-start.1) | copy-done | bytes 2621464
  6.6 0.9 other_half.1
  7.7 0.1 collective-permute-start.4
  7.8 0.6 copy-done.10
  8.4 0.1 dynamic-slice_reduce_fusion
  8.6 1.2 %reshape.113 = bf16[4,4,8,2,4,128]{5,4,3,2,1,0:T(4,128)(2,1)S(1)} reshape(bf16[4,4,8192]{2,1,0:T(4,128)(2,1)} %param.15) | data formatting | bytes 524288 | tf_op jit(solution)/shard_map/reshape | solution.py:596
  9.8 0.1 copy.20
  9.9 0.2 convert_reduce_fusion
  10.1 4.5 %collective-permute-start.3 = (bf16[2,4,2,160,128]{4,3,2,1,0:T(8,128)(2,1)S(1)}, bf16[2,4,2,160,128]{4,3,2,1,0:T(8,128)(2,1)S(1)}, u32[]{:S(2)}, u32[]{:S(2)}) collective-permute-start(bf16[2,4,2,160,128]{4,3,2,1,0:T(8,128)(2,1)S(1)} %pad_maximum_fusion.refs_0_), channel_id=1, source_target_pairs={{0,12},{1,13},{2,14},{3,15},{16,28},{17,29},{18,30},{19,31},{32,44... | collective-permute-start | bytes 1966088 | tf_op jit(solution)/shard_map/ppermute | solution.py:571
  14.6 1.4 %collective-permute-start.2 = (bf16[2,4,2,160,128]{4,3,2,1,0:T(8,128)(2,1)S(1)}, bf16[2,4,2,160,128]{4,3,2,1,0:T(8,128)(2,1)S(1)}, u32[]{:S(2)}, u32[]{:S(2)}) collective-permute-start(bf16[2,4,2,160,128]{4,3,2,1,0:T(8,128)(2,1)S(1)} %pad_maximum_fusion.refs_0_), channel_id=1, source_target_pairs={{0,2},{1,3},{2,0},{3,1},{4,6},{5,7},{6,4},{7,5},{8,10},{9,11},{10,... | collective-permute-start | bytes 1966088 | tf_op jit(solution)/shard_map/ppermute | solution.py:571
  16.0 1.3 %collective-permute-start.1 = (bf16[2,4,2,160,128]{4,3,2,1,0:T(8,128)(2,1)S(1)}, bf16[2,4,2,160,128]{4,3,2,1,0:T(8,128)(2,1)S(1)}, u32[]{:S(2)}, u32[]{:S(2)}) collective-permute-start(bf16[2,4,2,160,128]{4,3,2,1,0:T(8,128)(2,1)S(1)} %pad_maximum_fusion.refs_0_), channel_id=1, source_target_pairs={{0,4},{1,5},{2,6},{3,7},{4,8},{5,9},{6,10},{7,11},{8,12},{9,13},{1... | collective-permute-start | bytes 1966088 | tf_op jit(solution)/shard_map/ppermute | solution.py:571
  17.4 0.1 and_reduce_fusion
  17.5 0.2 fusion
  17.7 8.7 %partials.1 = bf16[16,6,16,128]{3,2,1,0:T(8,128)(2,1)} custom-call(s32[6]{0:T(128)S(1)} %stack.59.info, s32[4]{0:T(128)S(1)} %copy-done.7, bf16[4,8,32,128]{3,2,1,0:T(8,128)(2,1)S(1)} %bitcast.28, bf16[1,8,32,128]{3,2,1,0:T(8,128)(2,1)S(1)} %bitcast.30, bf16[2,4,512,1024]{3,2,1,0:T(8,128)(2,1)} %cache.1, bf16[2,4,16,1024]{3,2,1,0:T(8,128)(2,1)S(1)} %pad.9.tail_ref, ...), custom_call_target="tpu_custom_call" | custom-call | flops 2684354560 | bytes 8388608 | tf_op jit(solution)/shard_map/partials/pallas_call | solution.py:434
  26.4 2.3 %collective-permute-done.3.refs_3_ = bf16[2,4,2,160,128]{4,3,2,1,0:T(8,128)(2,1)S(1)} collective-permute-done((bf16[2,4,2,160,128]{4,3,2,1,0:T(8,128)(2,1)S(1)}, bf16[2,4,2,160,128]{4,3,2,1,0:T(8,128)(2,1)S(1)}, u32[]{:S(2)}, u32[]{:S(2)}) %collective-permute-start.3) | collective-permute-done | bytes 655392 | tf_op jit(solution)/shard_map/ppermute | solution.py:571
  28.7 2.0 %collective-permute-done.2.refs_2_ = bf16[2,4,2,160,128]{4,3,2,1,0:T(8,128)(2,1)S(1)} collective-permute-done((bf16[2,4,2,160,128]{4,3,2,1,0:T(8,128)(2,1)S(1)}, bf16[2,4,2,160,128]{4,3,2,1,0:T(8,128)(2,1)S(1)}, u32[]{:S(2)}, u32[]{:S(2)}) %collective-permute-start.2) | collective-permute-done | bytes 655392 | tf_op jit(solution)/shard_map/ppermute | solution.py:571
  30.8 0.4 collective-permute-done.1.refs_1_
  31.1 0.5 copy-done.15
  31.6 0.8 copy-done.14
  32.5 5.0 %all-to-all-start = ((bf16[16,6,16,128]{3,2,1,0:T(8,128)(2,1)}), bf16[16,6,16,128]{3,2,1,0:T(8,128)(2,1)S(1)}, u32[]{:S(2)}, u32[]{:S(2)}) async-start(bf16[16,6,16,128]{3,2,1,0:T(8,128)(2,1)} %partials.1), calls=%async_computation | async-start | bytes 786432 | tf_op jit(solution)/shard_map/all_to_all | solution.py:625
  37.5 0.1 copy.23
  37.6 0.1 reshape.125
  37.7 0.1 copy.22
  37.8 0.1 reshape.117
  37.8 0.1 pad_add_fusion.table
  37.9 0.7 broadcast_add_fusion.pos_ref
  38.6 0.7 collective-permute-start.6
  39.3 0.7 collective-permute-start.5
  40.0 7.5 %collective-permute-start.7 = (bf16[2,4,2,160,128]{4,3,2,1,0:T(8,128)(2,1)}, bf16[2,4,2,160,128]{4,3,2,1,0:T(8,128)(2,1)S(1)}, u32[]{:S(2)}, u32[]{:S(2)}) collective-permute-start(bf16[2,4,2,160,128]{4,3,2,1,0:T(8,128)(2,1)} %copy-done.15), channel_id=1, source_target_pairs={{0,12},{1,13},{2,14},{3,15},{16,28},{17,29},{18,30},{19,31},{32,44... | collective-permute-start | bytes 1966088 | tf_op jit(solution)/shard_map/ppermute | solution.py:571
  47.6 7.4 %all-to-all-start.1 = ((bf16[8,160,256]{2,1,0:T(8,128)(2,1)}), bf16[8,160,256]{2,1,0:T(8,128)(2,1)S(1)}, u32[]{:S(2)}, u32[]{:S(2)}) async-start(bf16[8,160,256]{2,1,0:T(8,128)(2,1)} %get-tuple-element.60), calls=%async_computation.1 | async-start | bytes 1310720 | tf_op jit(solution)/shard_map/all_to_all | solution.py:627
  54.9 18.1 %prefill.3 = (bf16[4,5,128,256]{3,2,1,0:T(8,128)(2,1)}, f32[4,5,8,256]{3,2,1,0:T(8,128)}, bf16[4,5,128,256]{3,2,1,0:T(8,128)(2,1)}, f32[4,5,8,256]{3,2,1,0:T(8,128)}) custom-call(s32[6]{0:T(128)} %copy-done.4, s32[2,5,256]{2,1,0:T(8,128)} %broadcast_add_fusion.pos_ref, bf16[160,8192]{1,0:T(8,128)(2,1)} %qa_ref.5, ...), custom_call_target="tpu_custom_call" | custom-call | flops 13421772800 | bytes 15728640 | tf_op jit(solution)/shard_map/prefill/pallas_call | solution.py:298
  73.1 2.2 %merge.1 = (bf16[4,16,128]{2,1,0:T(8,128)(2,1)}, bf16[16,128]{1,0:T(8,128)(2,1)}) custom-call(bf16[16,6,16,128]{3,2,1,0:T(8,128)(2,1)} %copy-done.8), custom_call_target="tpu_custom_call" | custom-call | tf_op jit(solution)/shard_map/merge/pallas_call | solution.py:483
  75.3 0.7 copy-done.6
  76.0 1.7 %select.16 = bf16[8,2,176,256]{3,2,1,0:T(8,128)(2,1)} custom-call(s32[33]{0:T(128)S(1)} %pad_add_fusion.table, bf16[8,160,256]{2,1,0:T(8,128)(2,1)S(1)} %all-to-all-done.1.x_ref, bf16[16,128]{1,0:T(8,128)(2,1)S(1)} %copy-done.6), custom_call_target="tpu_custom_call" | custom-call | tf_op jit(solution)/shard_map/select/pallas_call | solution.py:513
  77.7 6.6 %all-to-all-start.2 = ((bf16[8,2,176,256]{3,2,1,0:T(8,128)(2,1)}), bf16[8,2,176,256]{3,2,1,0:T(8,128)(2,1)S(1)}, u32[]{:S(2)}, u32[]{:S(2)}) async-start(bf16[8,2,176,256]{3,2,1,0:T(8,128)(2,1)} %select.16), calls=%async_computation.2 | async-start | bytes 2883584 | tf_op jit(solution)/shard_map/all_to_all | solution.py:635
  84.4 0.9 collective-permute-start.8
  85.3 15.1 %prefill.4 = (bf16[4,5,128,256]{3,2,1,0:T(8,128)(2,1)}, f32[4,5,8,256]{3,2,1,0:T(8,128)}, bf16[4,5,128,256]{3,2,1,0:T(8,128)(2,1)}, f32[4,5,8,256]{3,2,1,0:T(8,128)}) custom-call(s32[6]{0:T(128)} %copy-done.4, s32[2,5,256]{2,1,0:T(8,128)} %broadcast_add_fusion.pos_ref, bf16[160,8192]{1,0:T(8,128)(2,1)} %qa_ref.5, ...), custom_call_target="tpu_custom_call" | custom-call | flops 10066329600 | bytes 15728640 | tf_op jit(solution)/shard_map/prefill/pallas_call | solution.py:298
  100.4 3.3 %all-to-all-done.2.x_ref = bf16[8,2,176,256]{3,2,1,0:T(8,128)(2,1)S(1)} async-done(((bf16[8,2,176,256]{3,2,1,0:T(8,128)(2,1)}), bf16[8,2,176,256]{3,2,1,0:T(8,128)(2,1)S(1)}, u32[]{:S(2)}, u32[]{:S(2)}) %all-to-all-start.2) | async-done | bytes 1441824 | tf_op jit(solution)/shard_map/all_to_all | solution.py:635
  103.8 9.6 %prefill.5 = (bf16[160,8192]{1,0:T(8,128)(2,1)}, bf16[160,4096]{1,0:T(8,128)(2,1)}) custom-call(s32[6]{0:T(128)} %copy-done.4, s32[2,5,256]{2,1,0:T(8,128)} %broadcast_add_fusion.pos_ref, bf16[160,8192]{1,0:T(8,128)(2,1)} %qa_ref.5, bf16[160,4096]{1,0:T(8,128)(2,1)} %collective-permute-done.4.qb_ref, bf16[2,4,2,160,128]{4,3,2,1,0:T(8,128)(2,1)} %copy-done.19, ...), custom_call_target="tpu_custom_call" | custom-call | flops 3355443200 | bytes 15728640 | tf_op jit(solution)/shard_map/prefill/pallas_call | solution.py:298
  113.4 3.1 %collective-permute-start.9 = (bf16[160,4096]{1,0:T(8,128)(2,1)}, bf16[160,4096]{1,0:T(8,128)(2,1)S(1)}, u32[]{:S(2)}, u32[]{:S(2)}) collective-permute-start(bf16[160,4096]{1,0:T(8,128)(2,1)} %get-tuple-element.93), channel_id=1, source_target_pairs={{0,1},{1,0},{2,3},{3,2},{4,5},{5,4},{6,7},{7,6},{8,9},{9,8},{10,11... | collective-permute-start | bytes 3932168 | tf_op jit(solution)/shard_map/ppermute | solution.py:571
  116.5 0.6 copy.25
  117.1 1.7 %settle.1 = (bf16[2,2,160,1024]{3,2,1,0:T(8,128)(2,1)}, bf16[2,16,128]{2,1,0:T(8,128)(2,1)S(1)}) custom-call(s32[33]{0:T(128)S(1)} %pad_add_fusion.table, bf16[8,2,176,256]{3,2,1,0:T(8,128)(2,1)S(1)} %all-to-all-done.2.x_ref), custom_call_target="tpu_custom_call" | custom-call | tf_op jit(solution)/shard_map/settle/pallas_call | solution.py:542
  118.8 0.6 copy.30
  119.4 2.7 %place.1 = bf16[160,8192]{1,0:T(8,128)(2,1)} custom-call(s32[6]{0:T(128)S(1)} %copy-done.5, bf16[160,8192]{1,0:T(8,128)(2,1)} %get-tuple-element.92.kept_ref, bf16[160,4096]{1,0:T(8,128)(2,1)S(1)} %collective-permute-done.9.x_ref), custom_call_target="tpu_custom_call", output_to_operand_aliasing={{}: (1, {})} | custom-call | tf_op jit(solution)/shard_map/place/pallas_call | solution.py:105
  (55 shorter events, 0.4 us)
Async XLA Ops:
  0.6 7.8 %copy-start = (bf16[8,8192]{1,0:T(8,128)(2,1)S(1)}, bf16[8,8192]{1,0:T(8,128)(2,1)}, u32[]{:S(2)}) copy-start(bf16[8,8192]{1,0:T(8,128)(2,1)} %param.11) | copy-start | bytes 393220
  0.8 1.1 copy-start.2
  1.9 15.8 %copy-start.4 = (s32[6]{0:T(128)}, s32[6]{0:T(128)S(1)}, u32[]{:S(2)}) copy-start(s32[6]{0:T(128)S(1)} %stack.59.info) | copy-start | bytes 76
  3.5 4.1 %collective-permute-start = (bf16[4,2,160,128]{3,2,1,0:T(8,128)(2,1)S(1)}, bf16[4,2,160,128]{3,2,1,0:T(8,128)(2,1)S(1)}, u32[]{:S(2)}, u32[]{:S(2)}) collective-permute-start(bf16[4,2,160,128]{3,2,1,0:T(8,128)(2,1)S(1)} %get-tuple-element.52), channel_id=1, source_target_pairs={{0,1},{1,0},{2,3},{3,2},{4,5},{5,4},{6,7},{7,6},{8,9},{9,8},{10,11... | collective-permute-start | bytes 983048 | tf_op jit(solution)/shard_map/ppermute | solution.py:571
  4.9 1.7 %copy-start.1 = (bf16[160,8192]{1,0:T(8,128)(2,1)S(1)}, bf16[160,8192]{1,0:T(8,128)(2,1)}, u32[]{:S(2)}) copy-start(bf16[160,8192]{1,0:T(8,128)(2,1)} %qa_ref.5) | copy-start | bytes 7864324
  7.5 0.8 copy-start.10
  7.5 2.4 %copy-start.20 = (s32[8]{0:T(128)S(1)}, s32[8]{0:T(128)}, u32[]{:S(2)}) copy-start(s32[8]{0:T(128)} %param.12) | copy-start | bytes 100
  7.5 10.1 %copy-start.3 = (bf16[2,160,1024]{2,1,0:T(8,128)(2,1)S(1)}, bf16[2,160,1024]{2,1,0:T(8,128)(2,1)}, u32[]{:S(2)}) copy-start(bf16[2,160,1024]{2,1,0:T(8,128)(2,1)} %pre_ref.1) | copy-start | bytes 1966084
  7.6 10.1 %copy-start.7 = (s32[4]{0:T(128)S(1)}, s32[4]{0:T(128)}, u32[]{:S(2)}) copy-start(s32[4]{0:T(128)} %lens.1) | copy-start | bytes 52
  7.6 18.8 %copy-start.9 = (bf16[2,4,2,160,128]{4,3,2,1,0:T(8,128)(2,1)}, bf16[2,4,2,160,128]{4,3,2,1,0:T(8,128)(2,1)S(1)}, u32[]{:S(2)}) copy-start(bf16[2,4,2,160,128]{4,3,2,1,0:T(8,128)(2,1)S(1)} %pad_maximum_fusion.refs_0_) | copy-start | bytes 1966084
  7.7 24.8 %collective-permute-start.4 = (bf16[160,4096]{1,0:T(8,128)(2,1)S(1)}, bf16[160,4096]{1,0:T(8,128)(2,1)}, u32[]{:S(2)}, u32[]{:S(2)}) collective-permute-start(bf16[160,4096]{1,0:T(8,128)(2,1)S(1)} %other_half.1), channel_id=1, source_target_pairs={{0,1},{1,0},{2,3},{3,2},{4,5},{5,4},{6,7},{7,6},{8,9},{9,8},{10,11... | collective-permute-start | bytes 3932168 | tf_op jit(solution)/shard_map/ppermute | solution.py:571
  10.1 18.6 %collective-permute-start.3 = (bf16[2,4,2,160,128]{4,3,2,1,0:T(8,128)(2,1)S(1)}, bf16[2,4,2,160,128]{4,3,2,1,0:T(8,128)(2,1)S(1)}, u32[]{:S(2)}, u32[]{:S(2)}) collective-permute-start(bf16[2,4,2,160,128]{4,3,2,1,0:T(8,128)(2,1)S(1)} %pad_maximum_fusion.refs_0_), channel_id=1, source_target_pairs={{0,12},{1,13},{2,14},{3,15},{16,28},{17,29},{18,30},{19,31},{32,44... | collective-permute-start | bytes 1966088 | tf_op jit(solution)/shard_map/ppermute | solution.py:571
  14.6 16.1 %collective-permute-start.2 = (bf16[2,4,2,160,128]{4,3,2,1,0:T(8,128)(2,1)S(1)}, bf16[2,4,2,160,128]{4,3,2,1,0:T(8,128)(2,1)S(1)}, u32[]{:S(2)}, u32[]{:S(2)}) collective-permute-start(bf16[2,4,2,160,128]{4,3,2,1,0:T(8,128)(2,1)S(1)} %pad_maximum_fusion.refs_0_), channel_id=1, source_target_pairs={{0,2},{1,3},{2,0},{3,1},{4,6},{5,7},{6,4},{7,5},{8,10},{9,11},{10,... | collective-permute-start | bytes 1966088 | tf_op jit(solution)/shard_map/ppermute | solution.py:571
  16.0 15.1 %collective-permute-start.1 = (bf16[2,4,2,160,128]{4,3,2,1,0:T(8,128)(2,1)S(1)}, bf16[2,4,2,160,128]{4,3,2,1,0:T(8,128)(2,1)S(1)}, u32[]{:S(2)}, u32[]{:S(2)}) collective-permute-start(bf16[2,4,2,160,128]{4,3,2,1,0:T(8,128)(2,1)S(1)} %pad_maximum_fusion.refs_0_), channel_id=1, source_target_pairs={{0,4},{1,5},{2,6},{3,7},{4,8},{5,9},{6,10},{7,11},{8,12},{9,13},{1... | collective-permute-start | bytes 1966088 | tf_op jit(solution)/shard_map/ppermute | solution.py:571
  17.7 20.2 %copy-start.12 = (s32[5,256]{1,0:T(8,128)S(1)}, s32[5,256]{1,0:T(8,128)}, u32[]{:S(2)}) copy-start(s32[5,256]{1,0:T(8,128)} %constant.79) | copy-start | bytes 15364
  28.7 2.4 %copy-start.13 = (bf16[2,4,2,160,128]{4,3,2,1,0:T(8,128)(2,1)}, bf16[2,4,2,160,128]{4,3,2,1,0:T(8,128)(2,1)S(1)}, u32[]{:S(2)}) copy-start(bf16[2,4,2,160,128]{4,3,2,1,0:T(8,128)(2,1)S(1)} %collective-permute-done.3.refs_3_) | copy-start | bytes 1966084
  30.8 0.9 copy-start.15
  31.6 0.8 copy-start.14
  32.5 15.1 %all-to-all-start = ((bf16[16,6,16,128]{3,2,1,0:T(8,128)(2,1)}), bf16[16,6,16,128]{3,2,1,0:T(8,128)(2,1)S(1)}, u32[]{:S(2)}, u32[]{:S(2)}) async-start(bf16[16,6,16,128]{3,2,1,0:T(8,128)(2,1)} %partials.1), calls=%async_computation | async-start | bytes 786432 | tf_op jit(solution)/shard_map/all_to_all | solution.py:625
  38.6 34.4 %collective-permute-start.6 = (bf16[2,4,2,160,128]{4,3,2,1,0:T(8,128)(2,1)}, bf16[2,4,2,160,128]{4,3,2,1,0:T(8,128)(2,1)S(1)}, u32[]{:S(2)}, u32[]{:S(2)}) collective-permute-start(bf16[2,4,2,160,128]{4,3,2,1,0:T(8,128)(2,1)} %copy-done.14), channel_id=1, source_target_pairs={{4,6},{5,7},{6,4},{7,5},{8,10},{9,11},{10,8},{11,9},{12,14},{13,15... | collective-permute-start | bytes 1966088 | tf_op jit(solution)/shard_map/ppermute | solution.py:571
  39.3 33.8 %collective-permute-start.5 = (bf16[2,4,2,160,128]{4,3,2,1,0:T(8,128)(2,1)}, bf16[2,4,2,160,128]{4,3,2,1,0:T(8,128)(2,1)S(1)}, u32[]{:S(2)}, u32[]{:S(2)}) collective-permute-start(bf16[2,4,2,160,128]{4,3,2,1,0:T(8,128)(2,1)} %copy-done.14), channel_id=1, source_target_pairs={{4,8},{5,9},{6,10},{7,11},{8,12},{9,13},{10,14},{11,15},{20,24},{2... | collective-permute-start | bytes 1966088 | tf_op jit(solution)/shard_map/ppermute | solution.py:571
  40.0 33.0 %collective-permute-start.7 = (bf16[2,4,2,160,128]{4,3,2,1,0:T(8,128)(2,1)}, bf16[2,4,2,160,128]{4,3,2,1,0:T(8,128)(2,1)S(1)}, u32[]{:S(2)}, u32[]{:S(2)}) collective-permute-start(bf16[2,4,2,160,128]{4,3,2,1,0:T(8,128)(2,1)} %copy-done.15), channel_id=1, source_target_pairs={{0,12},{1,13},{2,14},{3,15},{16,28},{17,29},{18,30},{19,31},{32,44... | collective-permute-start | bytes 1966088 | tf_op jit(solution)/shard_map/ppermute | solution.py:571
  47.6 25.5 %copy-start.8 = (bf16[16,6,16,128]{3,2,1,0:T(8,128)(2,1)}, bf16[16,6,16,128]{3,2,1,0:T(8,128)(2,1)S(1)}, u32[]{:S(2)}) copy-start(bf16[16,6,16,128]{3,2,1,0:T(8,128)(2,1)S(1)} %all-to-all-done.x_ref) | copy-start | bytes 1179652
  47.6 25.5 %all-to-all-start.1 = ((bf16[8,160,256]{2,1,0:T(8,128)(2,1)}), bf16[8,160,256]{2,1,0:T(8,128)(2,1)S(1)}, u32[]{:S(2)}, u32[]{:S(2)}) async-start(bf16[8,160,256]{2,1,0:T(8,128)(2,1)} %get-tuple-element.60), calls=%async_computation.1 | async-start | bytes 1310720 | tf_op jit(solution)/shard_map/all_to_all | solution.py:627
  73.0 4.7 %copy-start.18 = (bf16[2,4,2,160,128]{4,3,2,1,0:T(8,128)(2,1)}, bf16[2,4,2,160,128]{4,3,2,1,0:T(8,128)(2,1)S(1)}, u32[]{:S(2)}) copy-start(bf16[2,4,2,160,128]{4,3,2,1,0:T(8,128)(2,1)S(1)} %collective-permute-done.7.refs_2_) | copy-start | bytes 1966084
  73.1 11.3 %copy-start.16 = (bf16[2,4,2,160,128]{4,3,2,1,0:T(8,128)(2,1)}, bf16[2,4,2,160,128]{4,3,2,1,0:T(8,128)(2,1)S(1)}, u32[]{:S(2)}) copy-start(bf16[2,4,2,160,128]{4,3,2,1,0:T(8,128)(2,1)S(1)} %collective-permute-done.6.refs_1_) | copy-start | bytes 1966084
  73.1 4.7 %copy-start.17 = (bf16[2,4,2,160,128]{4,3,2,1,0:T(8,128)(2,1)}, bf16[2,4,2,160,128]{4,3,2,1,0:T(8,128)(2,1)S(1)}, u32[]{:S(2)}) copy-start(bf16[2,4,2,160,128]{4,3,2,1,0:T(8,128)(2,1)S(1)} %collective-permute-done.5.refs_0_) | copy-start | bytes 1966084
  75.3 0.7 copy-start.6
  77.7 26.0 %all-to-all-start.2 = ((bf16[8,2,176,256]{3,2,1,0:T(8,128)(2,1)}), bf16[8,2,176,256]{3,2,1,0:T(8,128)(2,1)S(1)}, u32[]{:S(2)}, u32[]{:S(2)}) async-start(bf16[8,2,176,256]{3,2,1,0:T(8,128)(2,1)} %select.16), calls=%async_computation.2 | async-start | bytes 2883584 | tf_op jit(solution)/shard_map/all_to_all | solution.py:635
  84.4 16.0 %collective-permute-start.8 = (bf16[2,4,2,160,128]{4,3,2,1,0:T(8,128)(2,1)S(1)}, bf16[2,4,2,160,128]{4,3,2,1,0:T(8,128)(2,1)S(1)}, u32[]{:S(2)}, u32[]{:S(2)}) collective-permute-start(bf16[2,4,2,160,128]{4,3,2,1,0:T(8,128)(2,1)S(1)} %collective-permute-done.6.refs_1_), channel_id=1, source_target_pairs={{4,8},{5,9},{6,10},{7,11},{8,12},{9,13},{10,14},{11,15},{20,24},{2... | collective-permute-start | bytes 1966088 | tf_op jit(solution)/shard_map/ppermute | solution.py:571
  100.4 3.4 %copy-start.19 = (bf16[2,4,2,160,128]{4,3,2,1,0:T(8,128)(2,1)}, bf16[2,4,2,160,128]{4,3,2,1,0:T(8,128)(2,1)S(1)}, u32[]{:S(2)}) copy-start(bf16[2,4,2,160,128]{4,3,2,1,0:T(8,128)(2,1)S(1)} %collective-permute-done.8.refs_0_) | copy-start | bytes 1966084
  103.8 12.7 %copy-start.11 = (bf16[4,16,128]{2,1,0:T(8,128)(2,1)S(1)}, bf16[4,16,128]{2,1,0:T(8,128)(2,1)}, u32[]{:S(2)}) copy-start(bf16[4,16,128]{2,1,0:T(8,128)(2,1)} %get-tuple-element.96) | copy-start | bytes 49156
  113.4 6.0 %copy-start.5 = (s32[6]{0:T(128)S(1)}, s32[6]{0:T(128)}, u32[]{:S(2)}) copy-start(s32[6]{0:T(128)} %copy-done.4) | copy-start | bytes 76
  113.4 6.0 %collective-permute-start.9 = (bf16[160,4096]{1,0:T(8,128)(2,1)}, bf16[160,4096]{1,0:T(8,128)(2,1)S(1)}, u32[]{:S(2)}, u32[]{:S(2)}) collective-permute-start(bf16[160,4096]{1,0:T(8,128)(2,1)} %get-tuple-element.93), channel_id=1, source_target_pairs={{0,1},{1,0},{2,3},{3,2},{4,5},{5,4},{6,7},{7,6},{8,9},{9,8},{10,11... | collective-permute-start | bytes 3932168 | tf_op jit(solution)/shard_map/ppermute | solution.py:571

commit v5 on v4

--- a/solution.py
+++ b/solution.py
@@ -612,6 +612,7 @@
     w1 = permute(own, around)
     q_sib = permute(q_send, swap)
     part = partials(info_decode, lengths, dec_rows, arrival, cache_kv, tail, pre_kv)
+    part = lax.all_to_all(part, "tp", 0, 0)
     part, a1, b0, w1, own, q_sib, info = lax.optimization_barrier(
         (part, a1, b0, w1, own, q_sib, info)
     )
@@ -622,7 +623,6 @@
     a2 = permute(a1, forward[4:])
     b1 = permute(a1, across[4:])
     w2 = permute(b0, around)
-    part = lax.all_to_all(part, "tp", 0, 0)
     part, pieces, info = lax.optimization_barrier((part, pieces, info))
     pieces = lax.all_to_all(pieces, "pool", 0, 0)
     carry = take(info, [own, a1, b0, w1], [-1, back1, upper, wrapped], None, False)

time: 123 us -> 122 us (level)
  waiting for transfers between devices: 8.07 us -> 11 us
  local copies, waits for them, and re-layouts: 8.69 us -> 6.62 us
  starting transfers between devices: 40.6 us -> 38.7 us
    all_to_all x1, waiting for transfers between devices: 0.01 us -> 7.46 us  [body(): part = lax.all_to_all(part, 'tp', 0, 0)]
    ppermute x10, waiting for transfers between devices: 4.72 us -> 0.03 us  [permute(): return lax.ppermute(a, 'tp', pairs)]
    ppermute x10, starting transfers between devices: 21.6 us -> 20.3 us  [permute(): return lax.ppermute(a, 'tp', pairs)]
    unnamed x45 -> x39, local copies, waits for them, and re-layouts: 6.16 us -> 5.04 us
  transfers between devices with their start and end apart: 13 -> 13, of which waited for: 4 -> 2; matrix products, arithmetic and copies ran while one was open for 4% -> 4% of each run, Pallas kernels for 36% -> 37%
where the time goes in v5:
time: 122 us; the launch traced here: 121 us
  Pallas kernels  62.4 us (51%)
  starting transfers between devices  38.7 us (32%)
  waiting for transfers between devices  11 us (9%)
  local copies, waits for them, and re-layouts  6.62 us (5%)
  other arithmetic  1.4 us (1%)
    pallas_call x3, Pallas kernels, prefill(): pl.pallas_call(functools.partial(prefill_kernel, kinds=kinds, first=first...  42.8 us
    ppermute x10, starting transfers between devices, permute(): return lax.ppermute(a, 'tp', pairs)  20.3 us
    pallas_call x1, Pallas kernels, partials(): pl.pallas_call(partial_kernel, out_shape=jax.ShapeDtypeStruct((TP, reques...  8.71 us
    all_to_all x1, waiting for transfers between devices, body(): part = lax.all_to_all(part, 'tp', 0, 0)  7.46 us
    all_to_all x1, starting transfers between devices, body(): pieces = lax.all_to_all(pieces, 'pool', 0, 0)  7.38 us
    all_to_all x1, starting transfers between devices, body(): landed = lax.all_to_all(select(table, pieces, arrived), 'pool', 0, 0)  6.65 us
    unnamed x39, local copies, waits for them, and re-layouts  5.04 us
    all_to_all x1, starting transfers between devices, body(): part = lax.all_to_all(part, 'tp', 0, 0)  4.4 us
  transfers between devices with their start and end apart: 13, of which 2 were waited for; matrix products, arithmetic and copies ran while one was open for 4% of the time, Pallas kernels for 37%

profile of v5, /device:TPU:1, one launch (start us, length us, event | category | flops | bytes accessed | tf_op | source)
XLA Modules:
  0.0 121.2 jit_solution(8760890092128088765)
XLA Ops:
  0.6 0.0 copy-start
  0.7 0.1 stack.59.info
  0.8 1.1 copy-done.2
  1.9 1.6 %prep_kv.1 = (bf16[4,2,160,128]{3,2,1,0:T(8,128)(2,1)S(1)}, bf16[4,2,160,128]{3,2,1,0:T(8,128)(2,1)S(1)}, bf16[8,160,256]{2,1,0:T(8,128)(2,1)}) custom-call(s32[6]{0:T(128)S(1)} %stack.59.info, bf16[2,160,1024]{2,1,0:T(8,128)(2,1)S(1)} %copy-done.2), custom_call_target="tpu_custom_call" | custom-call | tf_op jit(solution)/shard_map/prep_kv/pallas_call | solution.py:58
  3.5 1.4 %collective-permute-start = (bf16[4,2,160,128]{3,2,1,0:T(8,128)(2,1)S(1)}, bf16[4,2,160,128]{3,2,1,0:T(8,128)(2,1)S(1)}, u32[]{:S(2)}, u32[]{:S(2)}) collective-permute-start(bf16[4,2,160,128]{3,2,1,0:T(8,128)(2,1)S(1)} %get-tuple-element.52), channel_id=1, source_target_pairs={{0,1},{1,0},{2,3},{3,2},{4,5},{5,4},{6,7},{7,6},{8,9},{9,8},{10,11... | collective-permute-start | bytes 983048 | tf_op jit(solution)/shard_map/ppermute | solution.py:571
  4.9 0.9 copy.29
  5.8 0.1 dynamic-slice_reduce_fusion
  6.0 0.3 reshape.113
  6.2 0.1 copy.20
  6.3 0.0 copy-start.1
  6.4 1.7 %copy-done.1 = bf16[160,8192]{1,0:T(8,128)(2,1)S(1)} copy-done((bf16[160,8192]{1,0:T(8,128)(2,1)S(1)}, bf16[160,8192]{1,0:T(8,128)(2,1)}, u32[]{:S(2)}) %copy-start.1) | copy-done | bytes 2621464
  8.1 0.9 other_half.1
  9.0 0.2 convert_reduce_fusion
  9.2 0.1 pad_maximum_fusion.refs_0_
  9.3 0.1 collective-permute-start.4
  9.4 0.1 and_reduce_fusion
  9.6 0.2 fusion
  9.7 5.3 %collective-permute-start.3 = (bf16[2,4,2,160,128]{4,3,2,1,0:T(8,128)(2,1)S(1)}, bf16[2,4,2,160,128]{4,3,2,1,0:T(8,128)(2,1)}, u32[]{:S(2)}, u32[]{:S(2)}) collective-permute-start(bf16[2,4,2,160,128]{4,3,2,1,0:T(8,128)(2,1)S(1)} %pad_maximum_fusion.refs_0_), channel_id=1, source_target_pairs={{0,12},{1,13},{2,14},{3,15},{16,28},{17,29},{18,30},{19,31},{32,44... | collective-permute-start | bytes 1966088 | tf_op jit(solution)/shard_map/ppermute | solution.py:571
  15.0 1.3 %collective-permute-start.2 = (bf16[2,4,2,160,128]{4,3,2,1,0:T(8,128)(2,1)S(1)}, bf16[2,4,2,160,128]{4,3,2,1,0:T(8,128)(2,1)}, u32[]{:S(2)}, u32[]{:S(2)}) collective-permute-start(bf16[2,4,2,160,128]{4,3,2,1,0:T(8,128)(2,1)S(1)} %pad_maximum_fusion.refs_0_), channel_id=1, source_target_pairs={{0,2},{1,3},{2,0},{3,1},{4,6},{5,7},{6,4},{7,5},{8,10},{9,11},{10,... | collective-permute-start | bytes 1966088 | tf_op jit(solution)/shard_map/ppermute | solution.py:571
  16.3 2.2 %collective-permute-start.1 = (bf16[2,4,2,160,128]{4,3,2,1,0:T(8,128)(2,1)S(1)}, bf16[2,4,2,160,128]{4,3,2,1,0:T(8,128)(2,1)}, u32[]{:S(2)}, u32[]{:S(2)}) collective-permute-start(bf16[2,4,2,160,128]{4,3,2,1,0:T(8,128)(2,1)S(1)} %pad_maximum_fusion.refs_0_), channel_id=1, source_target_pairs={{0,4},{1,5},{2,6},{3,7},{4,8},{5,9},{6,10},{7,11},{8,12},{9,13},{1... | collective-permute-start | bytes 1966088 | tf_op jit(solution)/shard_map/ppermute | solution.py:571
  18.5 8.7 %partials.1 = bf16[16,6,16,128]{3,2,1,0:T(8,128)(2,1)} custom-call(s32[6]{0:T(128)S(1)} %stack.59.info, s32[4]{0:T(128)S(1)} %copy-done.7, bf16[4,8,32,128]{3,2,1,0:T(8,128)(2,1)S(1)} %bitcast.28, bf16[1,8,32,128]{3,2,1,0:T(8,128)(2,1)S(1)} %bitcast.30, bf16[2,4,512,1024]{3,2,1,0:T(8,128)(2,1)} %cache.1, bf16[2,4,16,1024]{3,2,1,0:T(8,128)(2,1)S(1)} %pad.9.tail_ref, ...), custom_call_target="tpu_custom_call" | custom-call | flops 2684354560 | bytes 8388608 | tf_op jit(solution)/shard_map/partials/pallas_call | solution.py:434
  27.2 4.4 %all-to-all-start = ((bf16[16,6,16,128]{3,2,1,0:T(8,128)(2,1)}), bf16[16,6,16,128]{3,2,1,0:T(8,128)(2,1)S(1)}, u32[]{:S(2)}, u32[]{:S(2)}) async-start(bf16[16,6,16,128]{3,2,1,0:T(8,128)(2,1)} %partials.1), calls=%async_computation | async-start | bytes 786432 | tf_op jit(solution)/shard_map/all_to_all | solution.py:615
  31.6 0.1 add_multiply_fusion
  31.7 0.1 copy.23
  31.8 0.1 reshape.125
  31.9 0.1 copy.22
  31.9 0.1 reshape.117
  32.0 0.1 pad_add_fusion.table
  32.1 0.7 broadcast_add_fusion.pos_ref
  32.8 7.5 %all-to-all-done.x_ref = bf16[16,6,16,128]{3,2,1,0:T(8,128)(2,1)S(1)} async-done(((bf16[16,6,16,128]{3,2,1,0:T(8,128)(2,1)}), bf16[16,6,16,128]{3,2,1,0:T(8,128)(2,1)S(1)}, u32[]{:S(2)}, u32[]{:S(2)}) %all-to-all-start) | async-done | bytes 393248 | tf_op jit(solution)/shard_map/all_to_all | solution.py:615
  40.3 0.7 collective-permute-start.6
  41.0 0.7 collective-permute-start.5
  41.7 7.4 %all-to-all-start.1 = ((bf16[8,160,256]{2,1,0:T(8,128)(2,1)}), bf16[8,160,256]{2,1,0:T(8,128)(2,1)S(1)}, u32[]{:S(2)}, u32[]{:S(2)}) async-start(bf16[8,160,256]{2,1,0:T(8,128)(2,1)} %get-tuple-element.60), calls=%async_computation.1 | async-start | bytes 1310720 | tf_op jit(solution)/shard_map/all_to_all | solution.py:627
  49.1 4.9 %collective-permute-start.7 = (bf16[2,4,2,160,128]{4,3,2,1,0:T(8,128)(2,1)}, bf16[2,4,2,160,128]{4,3,2,1,0:T(8,128)(2,1)S(1)}, u32[]{:S(2)}, u32[]{:S(2)}) collective-permute-start(bf16[2,4,2,160,128]{4,3,2,1,0:T(8,128)(2,1)} %collective-permute-done.2.refs_2_), channel_id=1, source_target_pairs={{0,12},{1,13},{2,14},{3,15},{16,28},{17,29},{18,30},{19,31},{32,44... | collective-permute-start | bytes 1966088 | tf_op jit(solution)/shard_map/ppermute | solution.py:571
  54.0 18.1 %prefill.3 = (bf16[4,5,128,256]{3,2,1,0:T(8,128)(2,1)}, f32[4,5,8,256]{3,2,1,0:T(8,128)}, bf16[4,5,128,256]{3,2,1,0:T(8,128)(2,1)}, f32[4,5,8,256]{3,2,1,0:T(8,128)}) custom-call(s32[6]{0:T(128)} %copy-done.4, s32[2,5,256]{2,1,0:T(8,128)} %broadcast_add_fusion.pos_ref, bf16[160,8192]{1,0:T(8,128)(2,1)} %qa_ref.5, ...), custom_call_target="tpu_custom_call" | custom-call | flops 13421772800 | bytes 15728640 | tf_op jit(solution)/shard_map/prefill/pallas_call | solution.py:298
  72.1 2.2 %merge.1 = (bf16[4,16,128]{2,1,0:T(8,128)(2,1)}, bf16[16,128]{1,0:T(8,128)(2,1)}) custom-call(bf16[16,6,16,128]{3,2,1,0:T(8,128)(2,1)} %copy-done.8), custom_call_target="tpu_custom_call" | custom-call | tf_op jit(solution)/shard_map/merge/pallas_call | solution.py:483
  74.3 0.7 copy-done.6
  75.0 1.7 %select.16 = bf16[8,2,176,256]{3,2,1,0:T(8,128)(2,1)} custom-call(s32[33]{0:T(128)S(1)} %pad_add_fusion.table, bf16[8,160,256]{2,1,0:T(8,128)(2,1)S(1)} %all-to-all-done.1.x_ref, bf16[16,128]{1,0:T(8,128)(2,1)S(1)} %copy-done.6), custom_call_target="tpu_custom_call" | custom-call | tf_op jit(solution)/shard_map/select/pallas_call | solution.py:513
  76.8 6.6 %all-to-all-start.2 = ((bf16[8,2,176,256]{3,2,1,0:T(8,128)(2,1)}), bf16[8,2,176,256]{3,2,1,0:T(8,128)(2,1)S(1)}, u32[]{:S(2)}, u32[]{:S(2)}) async-start(bf16[8,2,176,256]{3,2,1,0:T(8,128)(2,1)} %select.16), calls=%async_computation.2 | async-start | bytes 2883584 | tf_op jit(solution)/shard_map/all_to_all | solution.py:635
  83.4 0.9 collective-permute-start.8
  84.3 15.1 %prefill.4 = (bf16[4,5,128,256]{3,2,1,0:T(8,128)(2,1)}, f32[4,5,8,256]{3,2,1,0:T(8,128)}, bf16[4,5,128,256]{3,2,1,0:T(8,128)(2,1)}, f32[4,5,8,256]{3,2,1,0:T(8,128)}) custom-call(s32[6]{0:T(128)} %copy-done.4, s32[2,5,256]{2,1,0:T(8,128)} %broadcast_add_fusion.pos_ref, bf16[160,8192]{1,0:T(8,128)(2,1)} %qa_ref.5, ...), custom_call_target="tpu_custom_call" | custom-call | flops 10066329600 | bytes 15728640 | tf_op jit(solution)/shard_map/prefill/pallas_call | solution.py:298
  99.5 3.6 %all-to-all-done.2.x_ref = bf16[8,2,176,256]{3,2,1,0:T(8,128)(2,1)S(1)} async-done(((bf16[8,2,176,256]{3,2,1,0:T(8,128)(2,1)}), bf16[8,2,176,256]{3,2,1,0:T(8,128)(2,1)S(1)}, u32[]{:S(2)}, u32[]{:S(2)}) %all-to-all-start.2) | async-done | bytes 1441824 | tf_op jit(solution)/shard_map/all_to_all | solution.py:635
  103.0 9.6 %prefill.5 = (bf16[160,8192]{1,0:T(8,128)(2,1)}, bf16[160,4096]{1,0:T(8,128)(2,1)}) custom-call(s32[6]{0:T(128)} %copy-done.4, s32[2,5,256]{2,1,0:T(8,128)} %broadcast_add_fusion.pos_ref, bf16[160,8192]{1,0:T(8,128)(2,1)} %qa_ref.5, bf16[160,4096]{1,0:T(8,128)(2,1)} %collective-permute-done.4.qb_ref, bf16[2,4,2,160,128]{4,3,2,1,0:T(8,128)(2,1)} %copy-done.16, ...), custom_call_target="tpu_custom_call" | custom-call | flops 3355443200 | bytes 15728640 | tf_op jit(solution)/shard_map/prefill/pallas_call | solution.py:298
  112.6 2.8 %collective-permute-start.9 = (bf16[160,4096]{1,0:T(8,128)(2,1)}, bf16[160,4096]{1,0:T(8,128)(2,1)S(1)}, u32[]{:S(2)}, u32[]{:S(2)}) collective-permute-start(bf16[160,4096]{1,0:T(8,128)(2,1)} %get-tuple-element.93), channel_id=1, source_target_pairs={{0,1},{1,0},{2,3},{3,2},{4,5},{5,4},{6,7},{7,6},{8,9},{9,8},{10,11... | collective-permute-start | bytes 3932168 | tf_op jit(solution)/shard_map/ppermute | solution.py:571
  115.5 0.6 copy.25
  116.1 1.7 %settle.1 = (bf16[2,2,160,1024]{3,2,1,0:T(8,128)(2,1)}, bf16[2,16,128]{2,1,0:T(8,128)(2,1)S(1)}) custom-call(s32[33]{0:T(128)S(1)} %pad_add_fusion.table, bf16[8,2,176,256]{3,2,1,0:T(8,128)(2,1)S(1)} %all-to-all-done.2.x_ref), custom_call_target="tpu_custom_call" | custom-call | tf_op jit(solution)/shard_map/settle/pallas_call | solution.py:542
  117.9 0.6 copy.30
  118.4 2.7 %place.1 = bf16[160,8192]{1,0:T(8,128)(2,1)} custom-call(s32[6]{0:T(128)S(1)} %copy-done.5, bf16[160,8192]{1,0:T(8,128)(2,1)} %get-tuple-element.92.kept_ref, bf16[160,4096]{1,0:T(8,128)(2,1)S(1)} %collective-permute-done.9.x_ref), custom_call_target="tpu_custom_call", output_to_operand_aliasing={{}: (1, {})} | custom-call | tf_op jit(solution)/shard_map/place/pallas_call | solution.py:105
  (49 shorter events, 0.2 us)
Async XLA Ops:
  0.6 5.1 %copy-start = (bf16[8,8192]{1,0:T(8,128)(2,1)S(1)}, bf16[8,8192]{1,0:T(8,128)(2,1)}, u32[]{:S(2)}) copy-start(bf16[8,8192]{1,0:T(8,128)(2,1)} %param.11) | copy-start | bytes 393220
  0.8 1.1 copy-start.2
  1.9 16.6 %copy-start.4 = (s32[6]{0:T(128)}, s32[6]{0:T(128)S(1)}, u32[]{:S(2)}) copy-start(s32[6]{0:T(128)S(1)} %stack.59.info) | copy-start | bytes 76
  1.9 4.1 %copy-start.10 = (bf16[4,4,8192]{2,1,0:T(4,128)(2,1)S(1)}, bf16[4,4,8192]{2,1,0:T(4,128)(2,1)}, u32[]{:S(2)}) copy-start(bf16[4,4,8192]{2,1,0:T(4,128)(2,1)} %param.15) | copy-start | bytes 786436
  3.5 5.7 %collective-permute-start = (bf16[4,2,160,128]{3,2,1,0:T(8,128)(2,1)S(1)}, bf16[4,2,160,128]{3,2,1,0:T(8,128)(2,1)S(1)}, u32[]{:S(2)}, u32[]{:S(2)}) collective-permute-start(bf16[4,2,160,128]{3,2,1,0:T(8,128)(2,1)S(1)} %get-tuple-element.52), channel_id=1, source_target_pairs={{0,1},{1,0},{2,3},{3,2},{4,5},{5,4},{6,7},{7,6},{8,9},{9,8},{10,11... | collective-permute-start | bytes 983048 | tf_op jit(solution)/shard_map/ppermute | solution.py:571
  6.3 1.7 %copy-start.1 = (bf16[160,8192]{1,0:T(8,128)(2,1)S(1)}, bf16[160,8192]{1,0:T(8,128)(2,1)}, u32[]{:S(2)}) copy-start(bf16[160,8192]{1,0:T(8,128)(2,1)} %qa_ref.5) | copy-start | bytes 7864324
  8.1 0.9 copy-start.17
  9.0 9.5 %copy-start.3 = (bf16[2,160,1024]{2,1,0:T(8,128)(2,1)S(1)}, bf16[2,160,1024]{2,1,0:T(8,128)(2,1)}, u32[]{:S(2)}) copy-start(bf16[2,160,1024]{2,1,0:T(8,128)(2,1)} %pre_ref.1) | copy-start | bytes 1966084
  9.0 9.5 %copy-start.7 = (s32[4]{0:T(128)S(1)}, s32[4]{0:T(128)}, u32[]{:S(2)}) copy-start(s32[4]{0:T(128)} %lens.1) | copy-start | bytes 52
  9.3 17.9 %copy-start.9 = (bf16[2,4,2,160,128]{4,3,2,1,0:T(8,128)(2,1)}, bf16[2,4,2,160,128]{4,3,2,1,0:T(8,128)(2,1)S(1)}, u32[]{:S(2)}) copy-start(bf16[2,4,2,160,128]{4,3,2,1,0:T(8,128)(2,1)S(1)} %pad_maximum_fusion.refs_0_) | copy-start | bytes 1966084
  9.3 31.0 %collective-permute-start.4 = (bf16[160,4096]{1,0:T(8,128)(2,1)S(1)}, bf16[160,4096]{1,0:T(8,128)(2,1)}, u32[]{:S(2)}, u32[]{:S(2)}) collective-permute-start(bf16[160,4096]{1,0:T(8,128)(2,1)S(1)} %other_half.1), channel_id=1, source_target_pairs={{0,1},{1,0},{2,3},{3,2},{4,5},{5,4},{6,7},{7,6},{8,9},{9,8},{10,11... | collective-permute-start | bytes 3932168 | tf_op jit(solution)/shard_map/ppermute | solution.py:571
  9.7 30.5 %collective-permute-start.3 = (bf16[2,4,2,160,128]{4,3,2,1,0:T(8,128)(2,1)S(1)}, bf16[2,4,2,160,128]{4,3,2,1,0:T(8,128)(2,1)}, u32[]{:S(2)}, u32[]{:S(2)}) collective-permute-start(bf16[2,4,2,160,128]{4,3,2,1,0:T(8,128)(2,1)S(1)} %pad_maximum_fusion.refs_0_), channel_id=1, source_target_pairs={{0,12},{1,13},{2,14},{3,15},{16,28},{17,29},{18,30},{19,31},{32,44... | collective-permute-start | bytes 1966088 | tf_op jit(solution)/shard_map/ppermute | solution.py:571
  15.0 25.2 %collective-permute-start.2 = (bf16[2,4,2,160,128]{4,3,2,1,0:T(8,128)(2,1)S(1)}, bf16[2,4,2,160,128]{4,3,2,1,0:T(8,128)(2,1)}, u32[]{:S(2)}, u32[]{:S(2)}) collective-permute-start(bf16[2,4,2,160,128]{4,3,2,1,0:T(8,128)(2,1)S(1)} %pad_maximum_fusion.refs_0_), channel_id=1, source_target_pairs={{0,2},{1,3},{2,0},{3,1},{4,6},{5,7},{6,4},{7,5},{8,10},{9,11},{10,... | collective-permute-start | bytes 1966088 | tf_op jit(solution)/shard_map/ppermute | solution.py:571
  16.3 23.9 %collective-permute-start.1 = (bf16[2,4,2,160,128]{4,3,2,1,0:T(8,128)(2,1)S(1)}, bf16[2,4,2,160,128]{4,3,2,1,0:T(8,128)(2,1)}, u32[]{:S(2)}, u32[]{:S(2)}) collective-permute-start(bf16[2,4,2,160,128]{4,3,2,1,0:T(8,128)(2,1)S(1)} %pad_maximum_fusion.refs_0_), channel_id=1, source_target_pairs={{0,4},{1,5},{2,6},{3,7},{4,8},{5,9},{6,10},{7,11},{8,12},{9,13},{1... | collective-permute-start | bytes 1966088 | tf_op jit(solution)/shard_map/ppermute | solution.py:571
  18.5 13.6 %copy-start.12 = (s32[5,256]{1,0:T(8,128)S(1)}, s32[5,256]{1,0:T(8,128)}, u32[]{:S(2)}) copy-start(s32[5,256]{1,0:T(8,128)} %constant.79) | copy-start | bytes 15364
  27.2 13.0 %all-to-all-start = ((bf16[16,6,16,128]{3,2,1,0:T(8,128)(2,1)}), bf16[16,6,16,128]{3,2,1,0:T(8,128)(2,1)S(1)}, u32[]{:S(2)}, u32[]{:S(2)}) async-start(bf16[16,6,16,128]{3,2,1,0:T(8,128)(2,1)} %partials.1), calls=%async_computation | async-start | bytes 786432 | tf_op jit(solution)/shard_map/all_to_all | solution.py:615
  40.2 31.8 %copy-start.8 = (bf16[16,6,16,128]{3,2,1,0:T(8,128)(2,1)}, bf16[16,6,16,128]{3,2,1,0:T(8,128)(2,1)S(1)}, u32[]{:S(2)}) copy-start(bf16[16,6,16,128]{3,2,1,0:T(8,128)(2,1)S(1)} %all-to-all-done.x_ref) | copy-start | bytes 1179652
  40.3 31.8 %collective-permute-start.6 = (bf16[2,4,2,160,128]{4,3,2,1,0:T(8,128)(2,1)}, bf16[2,4,2,160,128]{4,3,2,1,0:T(8,128)(2,1)S(1)}, u32[]{:S(2)}, u32[]{:S(2)}) collective-permute-start(bf16[2,4,2,160,128]{4,3,2,1,0:T(8,128)(2,1)} %collective-permute-done.1.refs_1_), channel_id=1, source_target_pairs={{4,6},{5,7},{6,4},{7,5},{8,10},{9,11},{10,8},{11,9},{12,14},{13,15... | collective-permute-start | bytes 1966088 | tf_op jit(solution)/shard_map/ppermute | solution.py:571
  41.0 31.1 %collective-permute-start.5 = (bf16[2,4,2,160,128]{4,3,2,1,0:T(8,128)(2,1)}, bf16[2,4,2,160,128]{4,3,2,1,0:T(8,128)(2,1)S(1)}, u32[]{:S(2)}, u32[]{:S(2)}) collective-permute-start(bf16[2,4,2,160,128]{4,3,2,1,0:T(8,128)(2,1)} %collective-permute-done.1.refs_1_), channel_id=1, source_target_pairs={{4,8},{5,9},{6,10},{7,11},{8,12},{9,13},{10,14},{11,15},{20,24},{2... | collective-permute-start | bytes 1966088 | tf_op jit(solution)/shard_map/ppermute | solution.py:571
  41.7 30.3 %all-to-all-start.1 = ((bf16[8,160,256]{2,1,0:T(8,128)(2,1)}), bf16[8,160,256]{2,1,0:T(8,128)(2,1)S(1)}, u32[]{:S(2)}, u32[]{:S(2)}) async-start(bf16[8,160,256]{2,1,0:T(8,128)(2,1)} %get-tuple-element.60), calls=%async_computation.1 | async-start | bytes 1310720 | tf_op jit(solution)/shard_map/all_to_all | solution.py:627
  49.1 23.0 %collective-permute-start.7 = (bf16[2,4,2,160,128]{4,3,2,1,0:T(8,128)(2,1)}, bf16[2,4,2,160,128]{4,3,2,1,0:T(8,128)(2,1)S(1)}, u32[]{:S(2)}, u32[]{:S(2)}) collective-permute-start(bf16[2,4,2,160,128]{4,3,2,1,0:T(8,128)(2,1)} %collective-permute-done.2.refs_2_), channel_id=1, source_target_pairs={{0,12},{1,13},{2,14},{3,15},{16,28},{17,29},{18,30},{19,31},{32,44... | collective-permute-start | bytes 1966088 | tf_op jit(solution)/shard_map/ppermute | solution.py:571
  72.1 4.7 %copy-start.15 = (bf16[2,4,2,160,128]{4,3,2,1,0:T(8,128)(2,1)}, bf16[2,4,2,160,128]{4,3,2,1,0:T(8,128)(2,1)S(1)}, u32[]{:S(2)}) copy-start(bf16[2,4,2,160,128]{4,3,2,1,0:T(8,128)(2,1)S(1)} %collective-permute-done.7.refs_2_) | copy-start | bytes 1966084
  72.1 11.3 %copy-start.13 = (bf16[2,4,2,160,128]{4,3,2,1,0:T(8,128)(2,1)}, bf16[2,4,2,160,128]{4,3,2,1,0:T(8,128)(2,1)S(1)}, u32[]{:S(2)}) copy-start(bf16[2,4,2,160,128]{4,3,2,1,0:T(8,128)(2,1)S(1)} %collective-permute-done.6.refs_1_) | copy-start | bytes 1966084
  72.1 4.7 %copy-start.14 = (bf16[2,4,2,160,128]{4,3,2,1,0:T(8,128)(2,1)}, bf16[2,4,2,160,128]{4,3,2,1,0:T(8,128)(2,1)S(1)}, u32[]{:S(2)}) copy-start(bf16[2,4,2,160,128]{4,3,2,1,0:T(8,128)(2,1)S(1)} %collective-permute-done.5.refs_0_) | copy-start | bytes 1966084
  74.3 0.7 copy-start.6
  76.8 26.3 %all-to-all-start.2 = ((bf16[8,2,176,256]{3,2,1,0:T(8,128)(2,1)}), bf16[8,2,176,256]{3,2,1,0:T(8,128)(2,1)S(1)}, u32[]{:S(2)}, u32[]{:S(2)}) async-start(bf16[8,2,176,256]{3,2,1,0:T(8,128)(2,1)} %select.16), calls=%async_computation.2 | async-start | bytes 2883584 | tf_op jit(solution)/shard_map/all_to_all | solution.py:635
  83.4 16.0 %collective-permute-start.8 = (bf16[2,4,2,160,128]{4,3,2,1,0:T(8,128)(2,1)S(1)}, bf16[2,4,2,160,128]{4,3,2,1,0:T(8,128)(2,1)S(1)}, u32[]{:S(2)}, u32[]{:S(2)}) collective-permute-start(bf16[2,4,2,160,128]{4,3,2,1,0:T(8,128)(2,1)S(1)} %collective-permute-done.6.refs_1_), channel_id=1, source_target_pairs={{4,8},{5,9},{6,10},{7,11},{8,12},{9,13},{10,14},{11,15},{20,24},{2... | collective-permute-start | bytes 1966088 | tf_op jit(solution)/shard_map/ppermute | solution.py:571
  99.5 3.6 %copy-start.16 = (bf16[2,4,2,160,128]{4,3,2,1,0:T(8,128)(2,1)}, bf16[2,4,2,160,128]{4,3,2,1,0:T(8,128)(2,1)S(1)}, u32[]{:S(2)}) copy-start(bf16[2,4,2,160,128]{4,3,2,1,0:T(8,128)(2,1)S(1)} %collective-permute-done.8.refs_0_) | copy-start | bytes 1966084
  103.0 12.5 %copy-start.11 = (bf16[4,16,128]{2,1,0:T(8,128)(2,1)S(1)}, bf16[4,16,128]{2,1,0:T(8,128)(2,1)}, u32[]{:S(2)}) copy-start(bf16[4,16,128]{2,1,0:T(8,128)(2,1)} %get-tuple-element.96) | copy-start | bytes 49156
  112.6 5.8 %copy-start.5 = (s32[6]{0:T(128)S(1)}, s32[6]{0:T(128)}, u32[]{:S(2)}) copy-start(s32[6]{0:T(128)} %copy-done.4) | copy-start | bytes 76
  112.6 5.8 %collective-permute-start.9 = (bf16[160,4096]{1,0:T(8,128)(2,1)}, bf16[160,4096]{1,0:T(8,128)(2,1)S(1)}, u32[]{:S(2)}, u32[]{:S(2)}) collective-permute-start(bf16[160,4096]{1,0:T(8,128)(2,1)} %get-tuple-element.93), channel_id=1, source_target_pairs={{0,1},{1,0},{2,3},{3,2},{4,5},{5,4},{6,7},{7,6},{8,9},{9,8},{10,11... | collective-permute-start | bytes 3932168 | tf_op jit(solution)/shard_map/ppermute | solution.py:571

commit v6 on v5

--- a/solution.py
+++ b/solution.py
@@ -22,7 +22,7 @@
 FLOOR = -1e29
 SCALE2 = math.log2(math.e) / math.sqrt(HD)
 LOG2E = math.log2(math.e)
-TILE = 512
+TILE = 256
 UNIT = 64
 COLS = 256
 VMEM_BYTES = 48 * 1024 * 1024

time: 122 us -> 122 us (level)
  transfers between devices with their start and end apart: 13 -> 13, of which waited for: 2 -> 2; matrix products, arithmetic and copies ran while one was open for 4% -> 4% of each run, Pallas kernels for 37% -> 36%
where the time goes in v6:
time: 122 us; the launch traced here: 121 us
  Pallas kernels  62 us (51%)
  starting transfers between devices  38.7 us (32%)
  waiting for transfers between devices  11.4 us (9%)
  local copies, waits for them, and re-layouts  6.62 us (5%)
  other arithmetic  1.4 us (1%)
    pallas_call x3, Pallas kernels, prefill(): pl.pallas_call(functools.partial(prefill_kernel, kinds=kinds, first=first...  42.4 us
    ppermute x10, starting transfers between devices, permute(): return lax.ppermute(a, 'tp', pairs)  20.3 us
    pallas_call x1, Pallas kernels, partials(): pl.pallas_call(partial_kernel, out_shape=jax.ShapeDtypeStruct((TP, reques...  8.71 us
    all_to_all x1, waiting for transfers between devices, body(): part = lax.all_to_all(part, 'tp', 0, 0)  7.46 us
    all_to_all x1, starting transfers between devices, body(): pieces = lax.all_to_all(pieces, 'pool', 0, 0)  7.38 us
    all_to_all x1, starting transfers between devices, body(): landed = lax.all_to_all(select(table, pieces, arrived), 'pool', 0, 0)  6.64 us
    unnamed x39, local copies, waits for them, and re-layouts  5.04 us
    all_to_all x1, starting transfers between devices, body(): part = lax.all_to_all(part, 'tp', 0, 0)  4.4 us
  transfers between devices with their start and end apart: 13, of which 2 were waited for; matrix products, arithmetic and copies ran while one was open for 4% of the time, Pallas kernels for 36%

profile of v6, /device:TPU:1, one launch (start us, length us, event | category | flops | bytes accessed | tf_op | source)
XLA Modules:
  0.0 121.1 jit_solution(6392507319941785479)
XLA Ops:
  0.6 0.0 copy-start
  0.7 0.1 stack.59.info
  0.8 1.1 copy-done.2
  1.9 1.6 %prep_kv.1 = (bf16[4,2,160,128]{3,2,1,0:T(8,128)(2,1)S(1)}, bf16[4,2,160,128]{3,2,1,0:T(8,128)(2,1)S(1)}, bf16[8,160,256]{2,1,0:T(8,128)(2,1)}) custom-call(s32[6]{0:T(128)S(1)} %stack.59.info, bf16[2,160,1024]{2,1,0:T(8,128)(2,1)S(1)} %copy-done.2), custom_call_target="tpu_custom_call" | custom-call | tf_op jit(solution)/shard_map/prep_kv/pallas_call | solution.py:58
  3.5 1.4 %collective-permute-start = (bf16[4,2,160,128]{3,2,1,0:T(8,128)(2,1)S(1)}, bf16[4,2,160,128]{3,2,1,0:T(8,128)(2,1)S(1)}, u32[]{:S(2)}, u32[]{:S(2)}) collective-permute-start(bf16[4,2,160,128]{3,2,1,0:T(8,128)(2,1)S(1)} %get-tuple-element.52), channel_id=1, source_target_pairs={{0,1},{1,0},{2,3},{3,2},{4,5},{5,4},{6,7},{7,6},{8,9},{9,8},{10,11... | collective-permute-start | bytes 983048 | tf_op jit(solution)/shard_map/ppermute | solution.py:571
  4.9 0.9 copy.29
  5.8 0.1 dynamic-slice_reduce_fusion
  6.0 0.3 reshape.113
  6.2 0.1 copy.20
  6.4 1.7 %copy-done.1 = bf16[160,8192]{1,0:T(8,128)(2,1)S(1)} copy-done((bf16[160,8192]{1,0:T(8,128)(2,1)S(1)}, bf16[160,8192]{1,0:T(8,128)(2,1)}, u32[]{:S(2)}) %copy-start.1) | copy-done | bytes 2621464
  8.1 0.9 other_half.1
  9.0 0.0 copy-start.3
  9.0 0.2 convert_reduce_fusion
  9.2 0.1 pad_maximum_fusion.refs_0_
  9.3 0.1 collective-permute-start.4
  9.4 0.1 and_reduce_fusion
  9.6 0.2 fusion
  9.7 5.3 %collective-permute-start.3 = (bf16[2,4,2,160,128]{4,3,2,1,0:T(8,128)(2,1)S(1)}, bf16[2,4,2,160,128]{4,3,2,1,0:T(8,128)(2,1)}, u32[]{:S(2)}, u32[]{:S(2)}) collective-permute-start(bf16[2,4,2,160,128]{4,3,2,1,0:T(8,128)(2,1)S(1)} %pad_maximum_fusion.refs_0_), channel_id=1, source_target_pairs={{0,12},{1,13},{2,14},{3,15},{16,28},{17,29},{18,30},{19,31},{32,44... | collective-permute-start | bytes 1966088 | tf_op jit(solution)/shard_map/ppermute | solution.py:571
  15.0 1.3 %collective-permute-start.2 = (bf16[2,4,2,160,128]{4,3,2,1,0:T(8,128)(2,1)S(1)}, bf16[2,4,2,160,128]{4,3,2,1,0:T(8,128)(2,1)}, u32[]{:S(2)}, u32[]{:S(2)}) collective-permute-start(bf16[2,4,2,160,128]{4,3,2,1,0:T(8,128)(2,1)S(1)} %pad_maximum_fusion.refs_0_), channel_id=1, source_target_pairs={{0,2},{1,3},{2,0},{3,1},{4,6},{5,7},{6,4},{7,5},{8,10},{9,11},{10,... | collective-permute-start | bytes 1966088 | tf_op jit(solution)/shard_map/ppermute | solution.py:571
  16.3 2.2 %collective-permute-start.1 = (bf16[2,4,2,160,128]{4,3,2,1,0:T(8,128)(2,1)S(1)}, bf16[2,4,2,160,128]{4,3,2,1,0:T(8,128)(2,1)}, u32[]{:S(2)}, u32[]{:S(2)}) collective-permute-start(bf16[2,4,2,160,128]{4,3,2,1,0:T(8,128)(2,1)S(1)} %pad_maximum_fusion.refs_0_), channel_id=1, source_target_pairs={{0,4},{1,5},{2,6},{3,7},{4,8},{5,9},{6,10},{7,11},{8,12},{9,13},{1... | collective-permute-start | bytes 1966088 | tf_op jit(solution)/shard_map/ppermute | solution.py:571
  18.5 8.7 %partials.1 = bf16[16,6,16,128]{3,2,1,0:T(8,128)(2,1)} custom-call(s32[6]{0:T(128)S(1)} %stack.59.info, s32[4]{0:T(128)S(1)} %copy-done.7, bf16[4,8,32,128]{3,2,1,0:T(8,128)(2,1)S(1)} %bitcast.28, bf16[1,8,32,128]{3,2,1,0:T(8,128)(2,1)S(1)} %bitcast.30, bf16[2,4,512,1024]{3,2,1,0:T(8,128)(2,1)} %cache.1, bf16[2,4,16,1024]{3,2,1,0:T(8,128)(2,1)S(1)} %pad.9.tail_ref, ...), custom_call_target="tpu_custom_call" | custom-call | flops 2684354560 | bytes 8388608 | tf_op jit(solution)/shard_map/partials/pallas_call | solution.py:434
  27.2 4.4 %all-to-all-start = ((bf16[16,6,16,128]{3,2,1,0:T(8,128)(2,1)}), bf16[16,6,16,128]{3,2,1,0:T(8,128)(2,1)S(1)}, u32[]{:S(2)}, u32[]{:S(2)}) async-start(bf16[16,6,16,128]{3,2,1,0:T(8,128)(2,1)} %partials.1), calls=%async_computation | async-start | bytes 786432 | tf_op jit(solution)/shard_map/all_to_all | solution.py:615
  31.6 0.1 add_multiply_fusion
  31.7 0.1 copy.23
  31.8 0.1 reshape.125
  31.9 0.1 copy.22
  31.9 0.1 reshape.117
  32.0 0.1 pad_add_fusion.table
  32.1 0.7 broadcast_add_fusion.pos_ref
  32.8 7.5 %all-to-all-done.x_ref = bf16[16,6,16,128]{3,2,1,0:T(8,128)(2,1)S(1)} async-done(((bf16[16,6,16,128]{3,2,1,0:T(8,128)(2,1)}), bf16[16,6,16,128]{3,2,1,0:T(8,128)(2,1)S(1)}, u32[]{:S(2)}, u32[]{:S(2)}) %all-to-all-start) | async-done | bytes 393248 | tf_op jit(solution)/shard_map/all_to_all | solution.py:615
  40.3 0.7 collective-permute-start.6
  41.0 0.7 collective-permute-start.5
  41.7 7.4 %all-to-all-start.1 = ((bf16[8,160,256]{2,1,0:T(8,128)(2,1)}), bf16[8,160,256]{2,1,0:T(8,128)(2,1)S(1)}, u32[]{:S(2)}, u32[]{:S(2)}) async-start(bf16[8,160,256]{2,1,0:T(8,128)(2,1)} %get-tuple-element.60), calls=%async_computation.1 | async-start | bytes 1310720 | tf_op jit(solution)/shard_map/all_to_all | solution.py:627
  49.1 4.9 %collective-permute-start.7 = (bf16[2,4,2,160,128]{4,3,2,1,0:T(8,128)(2,1)}, bf16[2,4,2,160,128]{4,3,2,1,0:T(8,128)(2,1)S(1)}, u32[]{:S(2)}, u32[]{:S(2)}) collective-permute-start(bf16[2,4,2,160,128]{4,3,2,1,0:T(8,128)(2,1)} %collective-permute-done.2.refs_2_), channel_id=1, source_target_pairs={{0,12},{1,13},{2,14},{3,15},{16,28},{17,29},{18,30},{19,31},{32,44... | collective-permute-start | bytes 1966088 | tf_op jit(solution)/shard_map/ppermute | solution.py:571
  54.0 17.5 %prefill.3 = (bf16[4,5,128,256]{3,2,1,0:T(8,128)(2,1)}, f32[4,5,8,256]{3,2,1,0:T(8,128)}, bf16[4,5,128,256]{3,2,1,0:T(8,128)(2,1)}, f32[4,5,8,256]{3,2,1,0:T(8,128)}) custom-call(s32[6]{0:T(128)} %copy-done.4, s32[2,5,256]{2,1,0:T(8,128)} %broadcast_add_fusion.pos_ref, bf16[160,8192]{1,0:T(8,128)(2,1)} %qa_ref.5, ...), custom_call_target="tpu_custom_call" | custom-call | flops 13421772800 | bytes 15728640 | tf_op jit(solution)/shard_map/prefill/pallas_call | solution.py:298
  71.6 2.2 %merge.1 = (bf16[4,16,128]{2,1,0:T(8,128)(2,1)}, bf16[16,128]{1,0:T(8,128)(2,1)}) custom-call(bf16[16,6,16,128]{3,2,1,0:T(8,128)(2,1)} %copy-done.8), custom_call_target="tpu_custom_call" | custom-call | tf_op jit(solution)/shard_map/merge/pallas_call | solution.py:483
  73.8 0.7 copy-done.6
  74.5 1.7 %select.16 = bf16[8,2,176,256]{3,2,1,0:T(8,128)(2,1)} custom-call(s32[33]{0:T(128)S(1)} %pad_add_fusion.table, bf16[8,160,256]{2,1,0:T(8,128)(2,1)S(1)} %all-to-all-done.1.x_ref, bf16[16,128]{1,0:T(8,128)(2,1)S(1)} %copy-done.6), custom_call_target="tpu_custom_call" | custom-call | tf_op jit(solution)/shard_map/select/pallas_call | solution.py:513
  76.2 6.6 %all-to-all-start.2 = ((bf16[8,2,176,256]{3,2,1,0:T(8,128)(2,1)}), bf16[8,2,176,256]{3,2,1,0:T(8,128)(2,1)S(1)}, u32[]{:S(2)}, u32[]{:S(2)}) async-start(bf16[8,2,176,256]{3,2,1,0:T(8,128)(2,1)} %select.16), calls=%async_computation.2 | async-start | bytes 2883584 | tf_op jit(solution)/shard_map/all_to_all | solution.py:635
  82.9 0.9 collective-permute-start.8
  83.7 14.8 %prefill.4 = (bf16[4,5,128,256]{3,2,1,0:T(8,128)(2,1)}, f32[4,5,8,256]{3,2,1,0:T(8,128)}, bf16[4,5,128,256]{3,2,1,0:T(8,128)(2,1)}, f32[4,5,8,256]{3,2,1,0:T(8,128)}) custom-call(s32[6]{0:T(128)} %copy-done.4, s32[2,5,256]{2,1,0:T(8,128)} %broadcast_add_fusion.pos_ref, bf16[160,8192]{1,0:T(8,128)(2,1)} %qa_ref.5, ...), custom_call_target="tpu_custom_call" | custom-call | flops 10066329600 | bytes 15728640 | tf_op jit(solution)/shard_map/prefill/pallas_call | solution.py:298
  98.5 3.9 %all-to-all-done.2.x_ref = bf16[8,2,176,256]{3,2,1,0:T(8,128)(2,1)S(1)} async-done(((bf16[8,2,176,256]{3,2,1,0:T(8,128)(2,1)}), bf16[8,2,176,256]{3,2,1,0:T(8,128)(2,1)S(1)}, u32[]{:S(2)}, u32[]{:S(2)}) %all-to-all-start.2) | async-done | bytes 1441824 | tf_op jit(solution)/shard_map/all_to_all | solution.py:635
  102.5 10.1 %prefill.5 = (bf16[160,8192]{1,0:T(8,128)(2,1)}, bf16[160,4096]{1,0:T(8,128)(2,1)}) custom-call(s32[6]{0:T(128)} %copy-done.4, s32[2,5,256]{2,1,0:T(8,128)} %broadcast_add_fusion.pos_ref, bf16[160,8192]{1,0:T(8,128)(2,1)} %qa_ref.5, bf16[160,4096]{1,0:T(8,128)(2,1)} %collective-permute-done.4.qb_ref, bf16[2,4,2,160,128]{4,3,2,1,0:T(8,128)(2,1)} %copy-done.16, ...), custom_call_target="tpu_custom_call" | custom-call | flops 3355443200 | bytes 15728640 | tf_op jit(solution)/shard_map/prefill/pallas_call | solution.py:298
  112.6 2.8 %collective-permute-start.9 = (bf16[160,4096]{1,0:T(8,128)(2,1)}, bf16[160,4096]{1,0:T(8,128)(2,1)S(1)}, u32[]{:S(2)}, u32[]{:S(2)}) collective-permute-start(bf16[160,4096]{1,0:T(8,128)(2,1)} %get-tuple-element.93), channel_id=1, source_target_pairs={{0,1},{1,0},{2,3},{3,2},{4,5},{5,4},{6,7},{7,6},{8,9},{9,8},{10,11... | collective-permute-start | bytes 3932168 | tf_op jit(solution)/shard_map/ppermute | solution.py:571
  115.4 0.6 copy.25
  116.0 1.7 %settle.1 = (bf16[2,2,160,1024]{3,2,1,0:T(8,128)(2,1)}, bf16[2,16,128]{2,1,0:T(8,128)(2,1)S(1)}) custom-call(s32[33]{0:T(128)S(1)} %pad_add_fusion.table, bf16[8,2,176,256]{3,2,1,0:T(8,128)(2,1)S(1)} %all-to-all-done.2.x_ref), custom_call_target="tpu_custom_call" | custom-call | tf_op jit(solution)/shard_map/settle/pallas_call | solution.py:542
  117.8 0.6 copy.30
  118.4 2.7 %place.1 = bf16[160,8192]{1,0:T(8,128)(2,1)} custom-call(s32[6]{0:T(128)S(1)} %copy-done.5, bf16[160,8192]{1,0:T(8,128)(2,1)} %get-tuple-element.92.kept_ref, bf16[160,4096]{1,0:T(8,128)(2,1)S(1)} %collective-permute-done.9.x_ref), custom_call_target="tpu_custom_call", output_to_operand_aliasing={{}: (1, {})} | custom-call | tf_op jit(solution)/shard_map/place/pallas_call | solution.py:105
  (49 shorter events, 0.2 us)
Async XLA Ops:
  0.6 5.1 %copy-start = (bf16[8,8192]{1,0:T(8,128)(2,1)S(1)}, bf16[8,8192]{1,0:T(8,128)(2,1)}, u32[]{:S(2)}) copy-start(bf16[8,8192]{1,0:T(8,128)(2,1)} %param.11) | copy-start | bytes 393220
  0.8 1.1 copy-start.2
  1.9 16.6 %copy-start.4 = (s32[6]{0:T(128)}, s32[6]{0:T(128)S(1)}, u32[]{:S(2)}) copy-start(s32[6]{0:T(128)S(1)} %stack.59.info) | copy-start | bytes 76
  1.9 4.1 %copy-start.10 = (bf16[4,4,8192]{2,1,0:T(4,128)(2,1)S(1)}, bf16[4,4,8192]{2,1,0:T(4,128)(2,1)}, u32[]{:S(2)}) copy-start(bf16[4,4,8192]{2,1,0:T(4,128)(2,1)} %param.15) | copy-start | bytes 786436
  3.5 5.7 %collective-permute-start = (bf16[4,2,160,128]{3,2,1,0:T(8,128)(2,1)S(1)}, bf16[4,2,160,128]{3,2,1,0:T(8,128)(2,1)S(1)}, u32[]{:S(2)}, u32[]{:S(2)}) collective-permute-start(bf16[4,2,160,128]{3,2,1,0:T(8,128)(2,1)S(1)} %get-tuple-element.52), channel_id=1, source_target_pairs={{0,1},{1,0},{2,3},{3,2},{4,5},{5,4},{6,7},{7,6},{8,9},{9,8},{10,11... | collective-permute-start | bytes 983048 | tf_op jit(solution)/shard_map/ppermute | solution.py:571
  6.3 1.7 %copy-start.1 = (bf16[160,8192]{1,0:T(8,128)(2,1)S(1)}, bf16[160,8192]{1,0:T(8,128)(2,1)}, u32[]{:S(2)}) copy-start(bf16[160,8192]{1,0:T(8,128)(2,1)} %qa_ref.5) | copy-start | bytes 7864324
  8.1 0.9 copy-start.17
  9.0 9.5 %copy-start.3 = (bf16[2,160,1024]{2,1,0:T(8,128)(2,1)S(1)}, bf16[2,160,1024]{2,1,0:T(8,128)(2,1)}, u32[]{:S(2)}) copy-start(bf16[2,160,1024]{2,1,0:T(8,128)(2,1)} %pre_ref.1) | copy-start | bytes 1966084
  9.0 9.5 %copy-start.7 = (s32[4]{0:T(128)S(1)}, s32[4]{0:T(128)}, u32[]{:S(2)}) copy-start(s32[4]{0:T(128)} %lens.1) | copy-start | bytes 52
  9.3 17.9 %copy-start.9 = (bf16[2,4,2,160,128]{4,3,2,1,0:T(8,128)(2,1)}, bf16[2,4,2,160,128]{4,3,2,1,0:T(8,128)(2,1)S(1)}, u32[]{:S(2)}) copy-start(bf16[2,4,2,160,128]{4,3,2,1,0:T(8,128)(2,1)S(1)} %pad_maximum_fusion.refs_0_) | copy-start | bytes 1966084
  9.3 31.0 %collective-permute-start.4 = (bf16[160,4096]{1,0:T(8,128)(2,1)S(1)}, bf16[160,4096]{1,0:T(8,128)(2,1)}, u32[]{:S(2)}, u32[]{:S(2)}) collective-permute-start(bf16[160,4096]{1,0:T(8,128)(2,1)S(1)} %other_half.1), channel_id=1, source_target_pairs={{0,1},{1,0},{2,3},{3,2},{4,5},{5,4},{6,7},{7,6},{8,9},{9,8},{10,11... | collective-permute-start | bytes 3932168 | tf_op jit(solution)/shard_map/ppermute | solution.py:571
  9.7 30.5 %collective-permute-start.3 = (bf16[2,4,2,160,128]{4,3,2,1,0:T(8,128)(2,1)S(1)}, bf16[2,4,2,160,128]{4,3,2,1,0:T(8,128)(2,1)}, u32[]{:S(2)}, u32[]{:S(2)}) collective-permute-start(bf16[2,4,2,160,128]{4,3,2,1,0:T(8,128)(2,1)S(1)} %pad_maximum_fusion.refs_0_), channel_id=1, source_target_pairs={{0,12},{1,13},{2,14},{3,15},{16,28},{17,29},{18,30},{19,31},{32,44... | collective-permute-start | bytes 1966088 | tf_op jit(solution)/shard_map/ppermute | solution.py:571
  15.0 25.2 %collective-permute-start.2 = (bf16[2,4,2,160,128]{4,3,2,1,0:T(8,128)(2,1)S(1)}, bf16[2,4,2,160,128]{4,3,2,1,0:T(8,128)(2,1)}, u32[]{:S(2)}, u32[]{:S(2)}) collective-permute-start(bf16[2,4,2,160,128]{4,3,2,1,0:T(8,128)(2,1)S(1)} %pad_maximum_fusion.refs_0_), channel_id=1, source_target_pairs={{0,2},{1,3},{2,0},{3,1},{4,6},{5,7},{6,4},{7,5},{8,10},{9,11},{10,... | collective-permute-start | bytes 1966088 | tf_op jit(solution)/shard_map/ppermute | solution.py:571
  16.3 23.9 %collective-permute-start.1 = (bf16[2,4,2,160,128]{4,3,2,1,0:T(8,128)(2,1)S(1)}, bf16[2,4,2,160,128]{4,3,2,1,0:T(8,128)(2,1)}, u32[]{:S(2)}, u32[]{:S(2)}) collective-permute-start(bf16[2,4,2,160,128]{4,3,2,1,0:T(8,128)(2,1)S(1)} %pad_maximum_fusion.refs_0_), channel_id=1, source_target_pairs={{0,4},{1,5},{2,6},{3,7},{4,8},{5,9},{6,10},{7,11},{8,12},{9,13},{1... | collective-permute-start | bytes 1966088 | tf_op jit(solution)/shard_map/ppermute | solution.py:571
  18.5 13.6 %copy-start.12 = (s32[5,256]{1,0:T(8,128)S(1)}, s32[5,256]{1,0:T(8,128)}, u32[]{:S(2)}) copy-start(s32[5,256]{1,0:T(8,128)} %constant.79) | copy-start | bytes 15364
  27.2 13.0 %all-to-all-start = ((bf16[16,6,16,128]{3,2,1,0:T(8,128)(2,1)}), bf16[16,6,16,128]{3,2,1,0:T(8,128)(2,1)S(1)}, u32[]{:S(2)}, u32[]{:S(2)}) async-start(bf16[16,6,16,128]{3,2,1,0:T(8,128)(2,1)} %partials.1), calls=%async_computation | async-start | bytes 786432 | tf_op jit(solution)/shard_map/all_to_all | solution.py:615
  40.2 31.2 %copy-start.8 = (bf16[16,6,16,128]{3,2,1,0:T(8,128)(2,1)}, bf16[16,6,16,128]{3,2,1,0:T(8,128)(2,1)S(1)}, u32[]{:S(2)}) copy-start(bf16[16,6,16,128]{3,2,1,0:T(8,128)(2,1)S(1)} %all-to-all-done.x_ref) | copy-start | bytes 1179652
  40.3 31.2 %collective-permute-start.6 = (bf16[2,4,2,160,128]{4,3,2,1,0:T(8,128)(2,1)}, bf16[2,4,2,160,128]{4,3,2,1,0:T(8,128)(2,1)S(1)}, u32[]{:S(2)}, u32[]{:S(2)}) collective-permute-start(bf16[2,4,2,160,128]{4,3,2,1,0:T(8,128)(2,1)} %collective-permute-done.1.refs_1_), channel_id=1, source_target_pairs={{4,6},{5,7},{6,4},{7,5},{8,10},{9,11},{10,8},{11,9},{12,14},{13,15... | collective-permute-start | bytes 1966088 | tf_op jit(solution)/shard_map/ppermute | solution.py:571
  41.0 30.6 %collective-permute-start.5 = (bf16[2,4,2,160,128]{4,3,2,1,0:T(8,128)(2,1)}, bf16[2,4,2,160,128]{4,3,2,1,0:T(8,128)(2,1)S(1)}, u32[]{:S(2)}, u32[]{:S(2)}) collective-permute-start(bf16[2,4,2,160,128]{4,3,2,1,0:T(8,128)(2,1)} %collective-permute-done.1.refs_1_), channel_id=1, source_target_pairs={{4,8},{5,9},{6,10},{7,11},{8,12},{9,13},{10,14},{11,15},{20,24},{2... | collective-permute-start | bytes 1966088 | tf_op jit(solution)/shard_map/ppermute | solution.py:571
  41.7 29.8 %all-to-all-start.1 = ((bf16[8,160,256]{2,1,0:T(8,128)(2,1)}), bf16[8,160,256]{2,1,0:T(8,128)(2,1)S(1)}, u32[]{:S(2)}, u32[]{:S(2)}) async-start(bf16[8,160,256]{2,1,0:T(8,128)(2,1)} %get-tuple-element.60), calls=%async_computation.1 | async-start | bytes 1310720 | tf_op jit(solution)/shard_map/all_to_all | solution.py:627
  49.1 22.4 %collective-permute-start.7 = (bf16[2,4,2,160,128]{4,3,2,1,0:T(8,128)(2,1)}, bf16[2,4,2,160,128]{4,3,2,1,0:T(8,128)(2,1)S(1)}, u32[]{:S(2)}, u32[]{:S(2)}) collective-permute-start(bf16[2,4,2,160,128]{4,3,2,1,0:T(8,128)(2,1)} %collective-permute-done.2.refs_2_), channel_id=1, source_target_pairs={{0,12},{1,13},{2,14},{3,15},{16,28},{17,29},{18,30},{19,31},{32,44... | collective-permute-start | bytes 1966088 | tf_op jit(solution)/shard_map/ppermute | solution.py:571
  71.5 4.7 %copy-start.15 = (bf16[2,4,2,160,128]{4,3,2,1,0:T(8,128)(2,1)}, bf16[2,4,2,160,128]{4,3,2,1,0:T(8,128)(2,1)S(1)}, u32[]{:S(2)}) copy-start(bf16[2,4,2,160,128]{4,3,2,1,0:T(8,128)(2,1)S(1)} %collective-permute-done.7.refs_2_) | copy-start | bytes 1966084
  71.5 11.3 %copy-start.13 = (bf16[2,4,2,160,128]{4,3,2,1,0:T(8,128)(2,1)}, bf16[2,4,2,160,128]{4,3,2,1,0:T(8,128)(2,1)S(1)}, u32[]{:S(2)}) copy-start(bf16[2,4,2,160,128]{4,3,2,1,0:T(8,128)(2,1)S(1)} %collective-permute-done.6.refs_1_) | copy-start | bytes 1966084
  71.5 4.7 %copy-start.14 = (bf16[2,4,2,160,128]{4,3,2,1,0:T(8,128)(2,1)}, bf16[2,4,2,160,128]{4,3,2,1,0:T(8,128)(2,1)S(1)}, u32[]{:S(2)}) copy-start(bf16[2,4,2,160,128]{4,3,2,1,0:T(8,128)(2,1)S(1)} %collective-permute-done.5.refs_0_) | copy-start | bytes 1966084
  73.8 0.7 copy-start.6
  76.2 26.2 %all-to-all-start.2 = ((bf16[8,2,176,256]{3,2,1,0:T(8,128)(2,1)}), bf16[8,2,176,256]{3,2,1,0:T(8,128)(2,1)S(1)}, u32[]{:S(2)}, u32[]{:S(2)}) async-start(bf16[8,2,176,256]{3,2,1,0:T(8,128)(2,1)} %select.16), calls=%async_computation.2 | async-start | bytes 2883584 | tf_op jit(solution)/shard_map/all_to_all | solution.py:635
  82.9 15.7 %collective-permute-start.8 = (bf16[2,4,2,160,128]{4,3,2,1,0:T(8,128)(2,1)S(1)}, bf16[2,4,2,160,128]{4,3,2,1,0:T(8,128)(2,1)S(1)}, u32[]{:S(2)}, u32[]{:S(2)}) collective-permute-start(bf16[2,4,2,160,128]{4,3,2,1,0:T(8,128)(2,1)S(1)} %collective-permute-done.6.refs_1_), channel_id=1, source_target_pairs={{4,8},{5,9},{6,10},{7,11},{8,12},{9,13},{10,14},{11,15},{20,24},{2... | collective-permute-start | bytes 1966088 | tf_op jit(solution)/shard_map/ppermute | solution.py:571
  98.5 3.9 %copy-start.16 = (bf16[2,4,2,160,128]{4,3,2,1,0:T(8,128)(2,1)}, bf16[2,4,2,160,128]{4,3,2,1,0:T(8,128)(2,1)S(1)}, u32[]{:S(2)}) copy-start(bf16[2,4,2,160,128]{4,3,2,1,0:T(8,128)(2,1)S(1)} %collective-permute-done.8.refs_0_) | copy-start | bytes 1966084
  102.5 13.0 %copy-start.11 = (bf16[4,16,128]{2,1,0:T(8,128)(2,1)S(1)}, bf16[4,16,128]{2,1,0:T(8,128)(2,1)}, u32[]{:S(2)}) copy-start(bf16[4,16,128]{2,1,0:T(8,128)(2,1)} %get-tuple-element.96) | copy-start | bytes 49156
  112.6 5.8 %copy-start.5 = (s32[6]{0:T(128)S(1)}, s32[6]{0:T(128)}, u32[]{:S(2)}) copy-start(s32[6]{0:T(128)} %copy-done.4) | copy-start | bytes 76
  112.6 5.8 %collective-permute-start.9 = (bf16[160,4096]{1,0:T(8,128)(2,1)}, bf16[160,4096]{1,0:T(8,128)(2,1)S(1)}, u32[]{:S(2)}, u32[]{:S(2)}) collective-permute-start(bf16[160,4096]{1,0:T(8,128)(2,1)} %get-tuple-element.93), channel_id=1, source_target_pairs={{0,1},{1,0},{2,3},{3,2},{4,5},{5,4},{6,7},{7,6},{8,9},{9,8},{10,11... | collective-permute-start | bytes 3932168 | tf_op jit(solution)/shard_map/ppermute | solution.py:571
